TPU v7x, 256 devices: a whole 4x4x8 slice. The times are simulated.
256 devices in a mesh: occ: 8 (over y, x_lo), vir: 32 (over z, x_hi, core).
Axes of the slice: x: 4 (x_hi: 2, x_lo: 2; x = x_hi * 2 + x_lo), y: 4, z: 8, core: 2. Of those that a mesh axis runs over, the one named last changes fastest.
Arguments:
- b_factors: float32 [64, 1024, 4096], P('occ', 'vir'), may hold values from -0.6 to 0.6
- occ_energy: float32 [64], replicated, may hold values from -2 to -0.3
- vir_energy: float32 [1024], replicated, may hold values from 0.2 to 3
Outputs:
- gamma: float32 [64, 1024, 4096], P('occ', 'vir')
All inputs are finite; a program needn't handle non-finite values.
Results may differ from a plain program's by a relative error of at most 0.0003.
Values sent between devices are 32-bit elements; how exact they have to be, the bound alone decides.
No kernel may reach another device: no remote copies, remote signals or barrier semaphores. Data moves between devices by JAX's collectives and lax.ppermute only.
A program may use at most 128 MiB of HBM per device.

v0:
```python
import functools
import jax
import jax.numpy as jnp
from jax import lax
from jax.experimental import pallas as pl
from jax.experimental.pallas import tpu as pltpu
from jax.sharding import PartitionSpec as P

AXES = ("occ", "vir")
PANEL = 512
NT = (((1,), (1,)), ((), ()))
NN = (((1,), (0,)), ((), ()))


def mxu(left, right, dims=NN):
    return lax.dot_general(left, right, dims, preferred_element_type=jnp.float32)


def halves(value):
    high = value.astype(jnp.bfloat16)
    low = (value - high.astype(jnp.float32)).astype(jnp.bfloat16)
    return high, low


def panels(width):
    return [slice(at, at + PANEL) for at in range(0, width, PANEL)]


def fetch(source_ref, target_ref, sem):
    copy = pltpu.make_async_copy(source_ref, target_ref, sem)
    copy.start()
    return copy


def row_cuts(mine_ref, targets, first, sem):
    height = targets[0].shape[0]
    copies = []
    for at, target in enumerate(targets):
        rows = pl.ds((first + at) * height, height)
        copies.append(fetch(mine_ref.at[rows], target, sem.at[at]))
    return copies


def cut_kernel(count, mine_ref, *refs):
    for copy in row_cuts(mine_ref, refs[:count], 0, refs[count]):
        copy.wait()


def own_kernel(skip, mine_ref, gap_row_ref, gap_col_ref, *refs):
    high_ref, low_ref, a_high_ref, a_low_ref, *parts, stage_ref, panel_sem, part_sem = refs
    rows, width = mine_ref.shape
    arrivals = [
        fetch(mine_ref.at[:, cols], stage_ref.at[:, cols], panel_sem.at[at])
        for at, cols in enumerate(panels(width))
    ]
    integral = jnp.zeros((rows, rows), jnp.float32)
    cross = jnp.zeros((rows, rows), jnp.float32)
    for copy, cols in zip(arrivals, panels(width)):
        copy.wait()
        high, low = halves(stage_ref[:, cols])
        high_ref[:, cols] = high
        low_ref[:, cols] = low
        integral += mxu(high, high, NT)
        cross += mxu(high, low, NT)
    cuts = row_cuts(stage_ref, parts, skip, part_sem)
    integral = integral + (cross + cross.T)
    a_high, a_low = halves(integral / (gap_row_ref[...] + gap_col_ref[...]))
    a_high_ref[...] = a_high
    a_low_ref[...] = a_low
    for copy in cuts:
        copy.wait()


def step_kernel(plan, *refs):
    count, own, inner_rows, final = plan
    refs = list(refs)
    take = lambda number: [refs.pop(0) for _ in range(number)]
    others = take(count)
    high_ref, low_ref, gap_row_ref, gap_col_ref = take(4)
    a_own = [ref[...] for ref in take(2)] if own else None
    start_ref = None if own else take(1)[0]
    inner_ref = take(1)[0] if inner_rows else None
    gamma_ref, both_ref = take(2)
    if inner_rows:
        inner_stage_ref, inner_sem = take(2)
        at, height = inner_rows
        fetch(inner_ref.at[pl.ds(at, height)], inner_stage_ref, inner_sem).wait()
        others.append(inner_stage_ref)
    rows, width = high_ref.shape
    extent = both_ref.shape[0] // 2
    main = jnp.zeros((rows, 2 * extent), jnp.float32)
    rest = jnp.zeros((rows, extent), jnp.float32)
    for cols in panels(width):
        high, low = halves(jnp.concatenate([ref[:, cols] for ref in others], axis=0))
        both = jnp.concatenate([high, low], axis=0)
        both_ref[:, cols] = both
        main += mxu(high_ref[:, cols], both, NT)
        rest += mxu(low_ref[:, cols], high, NT)
    integral = main[:, :extent] + (main[:, extent:] + rest)
    a_high, a_low = halves(integral / (gap_row_ref[...] + gap_col_ref[...]))
    a_twice = jnp.concatenate([a_high, a_high], axis=1)
    departures = []
    for at, cols in enumerate(panels(width)):
        both = both_ref[:, cols]
        gamma = mxu(a_twice, both) + mxu(a_low, both[:extent])
        if own:
            high, low = high_ref[:, cols], low_ref[:, cols]
            gamma += mxu(a_own[0], high) + (mxu(a_own[0], low) + mxu(a_own[1], high))
        else:
            gamma += start_ref[:, cols]
        if final:
            stage_ref, sem = refs
            stage_ref[:, cols] = gamma
            departures.append(fetch(stage_ref.at[:, cols], gamma_ref.at[:, cols], sem.at[at]))
        else:
            gamma_ref[:, cols] = gamma
    for copy in departures:
        copy.wait()


VMEM = pl.BlockSpec(memory_space=pltpu.VMEM)
HBM = pl.BlockSpec(memory_space=pltpu.HBM)


def cost(rows, extent, width):
    return pl.CostEstimate(flops=12 * rows * extent * width, bytes_accessed=4 * extent * width, transcendentals=0)


def in_vmem(array):
    return pltpu.with_memory_space_constraint(array, pltpu.VMEM)


def in_hbm(array):
    return pltpu.with_memory_space_constraint(array, pltpu.HBM)


def params(mebibytes):
    return pltpu.CompilerParams(vmem_limit_bytes=mebibytes << 20)


def cut_call(mine, count, height):
    width = mine.shape[1]
    return pl.pallas_call(
        functools.partial(cut_kernel, count),
        out_shape=(pltpu.VMEM((height, width), jnp.float32),) * count,
        in_specs=[HBM],
        out_specs=(VMEM,) * count,
        scratch_shapes=[pltpu.SemaphoreType.DMA((count,))],
        compiler_params=params(2),
        cost_estimate=pl.CostEstimate(flops=0, bytes_accessed=8 * count * height * width, transcendentals=0),
        name="first_cuts",
    )(in_hbm(mine))


def own_call(mine, gap_row, gap_col, skip, height):
    rows, width = mine.shape
    count = rows // height - skip
    factor = pltpu.VMEM((rows, width), jnp.bfloat16)
    amplitude = pltpu.VMEM((rows, rows), jnp.bfloat16)
    part = pltpu.HBM((height, width), jnp.float32)
    return pl.pallas_call(
        functools.partial(own_kernel, skip),
        out_shape=(factor, factor, amplitude, amplitude) + (part,) * count,
        in_specs=[HBM, VMEM, VMEM],
        out_specs=(VMEM,) * 4 + (HBM,) * count,
        scratch_shapes=[
            pltpu.VMEM((rows, width), jnp.float32),
            pltpu.SemaphoreType.DMA((width // PANEL,)),
            pltpu.SemaphoreType.DMA((count,)),
        ],
        compiler_params=params(10),
        cost_estimate=cost(rows, rows, width),
        name="own_block",
    )(in_hbm(mine), gap_row, gap_col)


def step_call(others, high, low, gap_row, gap_col, begin, inner, inner_rows, final, name):
    rows, width = high.shape
    own = len(begin) == 2
    extent = sum(other.shape[0] for other in others)
    scratch = []
    if inner_rows:
        extent += inner_rows[1]
        scratch += [pltpu.VMEM((inner_rows[1], width), jnp.float32), pltpu.SemaphoreType.DMA]
    if final:
        scratch += [pltpu.VMEM((rows, width), jnp.float32), pltpu.SemaphoreType.DMA((width // PANEL,))]
    extra = [in_hbm(inner)] if inner_rows else []
    return pl.pallas_call(
        functools.partial(step_kernel, (len(others), own, inner_rows, final)),
        out_shape=(pltpu.HBM if final else pltpu.VMEM)((rows, width), jnp.float32),
        in_specs=[VMEM] * (len(others) + 4 + len(begin)) + [HBM] * len(extra),
        out_specs=HBM if final else VMEM,
        scratch_shapes=[pltpu.VMEM((2 * extent, width), jnp.bfloat16)] + scratch,
        input_output_aliases={} if final or own else {len(others) + 4: 0},
        compiler_params=params(10),
        cost_estimate=cost(rows, extent, width),
        name=name,
    )(*map(in_vmem, others), in_vmem(high), in_vmem(low), gap_row, gap_col, *map(in_vmem, begin), *extra)


def local(b_factors, occ_energy, vir_energy):
    occ_block, vir_block, width = b_factors.shape
    occ_count = lax.axis_size("occ")
    vir_count = lax.axis_size("vir")
    occ_here = lax.axis_index("occ")
    vir_here = lax.axis_index("vir")

    def moved(block, target):
        route = []
        for occ in range(occ_count):
            for vir in range(vir_count):
                occ_to, vir_to = target(occ, vir)
                route.append(
                    (occ * vir_count + vir, occ_to % occ_count * vir_count + vir_to % vir_count)
                )
        return lax.ppermute(block, AXES, route)

    def across(occ, vir):
        return occ ^ 1, vir

    def along(occ, vir):
        return (occ - 2 if occ % 2 else occ + 2), vir

    def outward(occ, vir):
        return occ ^ 1, (vir + 1 if vir % 2 else vir - 1)

    def inward(occ, vir):
        return occ, vir ^ 1

    def gap_of(occ_place, vir_place):
        occ_part = lax.dynamic_slice_in_dim(
            occ_energy, occ_place % occ_count * occ_block, occ_block
        )
        vir_part = lax.dynamic_slice_in_dim(
            vir_energy, vir_place % vir_count * vir_block, vir_block
        )
        return occ_part[:, None] - vir_part[None, :]

    occ_side = 1 - 2 * (occ_here % 2)
    vir_side = 1 - 2 * (vir_here % 2)
    gap = gap_of(occ_here, vir_here)
    gap_inner = gap_of(occ_here, vir_here + vir_side)
    gap_near = gap_of(occ_here + occ_side, vir_here)
    gap_far = gap_of(occ_here + occ_count - occ_side, vir_here)
    gap_outer = gap_of(occ_here, vir_here + vir_count - vir_side)
    gap_row = gap.reshape(-1, 1)
    gap_step = jnp.concatenate([gap_near, gap_far, gap_outer], axis=1)
    gap_inner = gap_inner.reshape(1, -1)

    def held(value, *earlier):
        return lax.optimization_barrier((value, earlier))[0]

    mine = b_factors.reshape(occ_block * vir_block, width)
    parts = list(cut_call(mine, 2, vir_block))
    near = [moved(part, across) for part in parts]
    inner = moved(held(b_factors, *parts), inward).reshape(mine.shape)
    high, low, a_high, a_low, *rest = own_call(held(mine, *parts), gap_row, gap.reshape(1, -1), 2, vir_block)
    parts += rest

    done = [a_high, a_high]
    far, outer = [], []
    begin = [a_high, a_low]
    inner_at = 0

    def step(k, *earlier):
        nonlocal begin, inner_at
        others = [near[k], far[k], outer[k]]
        if earlier:
            others = [held(other, *earlier) for other in others]
        gap_col = gap_step[k : k + 1]
        rows = None
        final = k == occ_block - 1
        if not final:
            height = vir_block if k < occ_block - 2 else 2 * vir_block
            rows = (inner_at, height)
            gap_col = jnp.concatenate([gap_col, gap_inner[:, inner_at : inner_at + height]], axis=1)
            inner_at += height
        gamma = step_call(others, high, low, gap_row, gap_col, begin, inner, rows, final, "step_%d" % k)
        begin = [gamma]
        done.append(gamma)
        return gamma

    for k in range(occ_block):
        part = held(near[k], done[k], inner) if k == 1 else held(near[k], done[k])
        far.append(moved(part, along))
        outer.append(moved(part, outward))
        if k + 2 < occ_block:
            near.append(moved(held(parts[k + 2], part), across))
        if k > 0:
            step(k - 1, part)
    gamma = step(occ_block - 1)
    return gamma.reshape(occ_block, vir_block, width)


def solution(mesh):
    in_specs = (P("occ", "vir", None), P(), P())
    out_specs = P("occ", "vir", None)
    return jax.shard_map(local, mesh=mesh, in_specs=in_specs, out_specs=out_specs, check_vma=False)
```

profile of v0, /device:TPU:1, one launch (start us, length us, event | category | flops | bytes accessed | tf_op | source)
XLA Modules:
  0.0 138.6 jit_solution(10911745054425076899)
XLA Ops:
  0.0 2.3 %first_cuts.1 = (f32[32,4096]{1,0:T(8,128)}, f32[32,4096]{1,0:T(8,128)}) custom-call(f32[256,4096]{1,0:T(8,128)} %bitcast.mine_ref), custom_call_target="tpu_custom_call" | custom-call | bytes 2097152 | tf_op jit(solution)/shard_map/first_cuts/pallas_call | solution.py:143
  2.3 3.3 %collective-permute-start.1 = (f32[8,32,4096]{2,1,0:T(8,128)}, f32[8,32,4096]{2,1,0:T(8,128)}, u32[]{:S(2)}, u32[]{:S(2)}) collective-permute-start(f32[8,32,4096]{2,1,0:T(8,128)} %param.3), channel_id=1, source_target_pairs={{0,1},{1,0},{2,3},{3,2},{4,5},{5,4},{6,7},{7,6},{8,9},{9,8},{10,11... | collective-permute-start | bytes 12582920 | tf_op jit(solution)/shard_map/ppermute | solution.py:216
  5.6 1.5 %collective-permute-start.3 = (f32[32,4096]{1,0:T(8,128)}, f32[32,4096]{1,0:T(8,128)S(1)}, u32[]{:S(2)}, u32[]{:S(2)}) collective-permute-start(f32[32,4096]{1,0:T(8,128)} %get-tuple-element.54), channel_id=1, source_target_pairs={{0,32},{1,33},{2,34},{3,35},{4,36},{5,37},{6,38},{7,39},{8,40},{9,... | collective-permute-start | bytes 1572872 | tf_op jit(solution)/shard_map/ppermute | solution.py:216
  8.4 4.9 %own_block.1 = (bf16[256,4096]{1,0:T(8,128)(2,1)S(1)}, bf16[256,4096]{1,0:T(8,128)(2,1)S(1)}, bf16[256,256]{1,0:T(8,128)(2,1)S(1)}, bf16[256,256]{1,0:T(8,128)(2...) custom-call(f32[256,4096]{1,0:T(8,128)} %bitcast.mine_ref, ...), custom_call_target="tpu_custom_call" | custom-call | flops 3221225472 | bytes 4194304 | tf_op jit(solution)/shard_map/own_block/pallas_call | solution.py:161
  13.4 1.3 copy-done
  14.7 15.8 %collective-permute-done.3.refs_0_ = f32[32,4096]{1,0:T(8,128)S(1)} collective-permute-done((f32[32,4096]{1,0:T(8,128)}, f32[32,4096]{1,0:T(8,128)S(1)}, u32[]{:S(2)}, u32[]{:S(2)}) %collective-permute-start.3) | collective-permute-done | bytes 524320 | tf_op jit(solution)/shard_map/ppermute | solution.py:216
  30.6 1.5 %collective-permute-start.6 = (f32[32,4096]{1,0:T(8,128)S(1)}, f32[32,4096]{1,0:T(8,128)}, u32[]{:S(2)}, u32[]{:S(2)}) collective-permute-start(f32[32,4096]{1,0:T(8,128)S(1)} %collective-permute-done.3.refs_0_), channel_id=1, source_target_pairs={{0,63},{1,34},{2,33},{3,36},{4,35},{5,38},{6,37},{7,40},{8,39},{9,... | collective-permute-start | bytes 1572872 | tf_op jit(solution)/shard_map/ppermute | solution.py:216
  32.1 1.3 collective-permute-start.5
  33.4 1.4 collective-permute-start.4
  37.3 12.1 %collective-permute-done.6.refs_2_ = f32[32,4096]{1,0:T(8,128)} collective-permute-done((f32[32,4096]{1,0:T(8,128)S(1)}, f32[32,4096]{1,0:T(8,128)}, u32[]{:S(2)}, u32[]{:S(2)}) %collective-permute-start.6) | collective-permute-done | bytes 524320 | tf_op jit(solution)/shard_map/ppermute | solution.py:216
  49.4 1.6 %copy-done.1 = bf16[256,4096]{1,0:T(8,128)(2,1)S(1)} copy-done((bf16[256,4096]{1,0:T(8,128)(2,1)S(1)}, bf16[256,4096]{1,0:T(8,128)(2,1)}, u32[]{:S(2)}) %copy-start.1) | copy-done | bytes 2097176
  51.0 6.5 %step_0.1.refs_7_ = f32[256,4096]{1,0:T(8,128)S(1)} custom-call(f32[32,4096]{1,0:T(8,128)S(1)} %collective-permute-done.3.refs_0_, f32[32,4096]{1,0:T(8,128)} %collective-permute-done.5.refs_1_, f32[32,4096]{1,0:T(8,128)} %collective-permute-done.6.refs_2_, bf16[256,4096]{1,0:T(8,128)(2,1)S(1)} %get-tuple-element.70.refs_3_, ...), custom_call_target="tpu_custom_call" | custom-call | flops 1610612736 | bytes 2097152 | tf_op jit(solution)/shard_map/step_0/pallas_call | solution.py:188
  57.5 3.9 %collective-permute-start.12 = (f32[32,4096]{1,0:T(8,128)}, f32[32,4096]{1,0:T(8,128)S(1)}, u32[]{:S(2)}, u32[]{:S(2)}) collective-permute-start(f32[32,4096]{1,0:T(8,128)} %collective-permute-done.4.refs_0_), channel_id=1, source_target_pairs={{0,63},{1,34},{2,33},{3,36},{4,35},{5,38},{6,37},{7,40},{8,39},{9,... | collective-permute-start | bytes 1572872 | tf_op jit(solution)/shard_map/ppermute | solution.py:216
  61.4 1.3 collective-permute-start.11
  62.7 2.6 %collective-permute-start.10 = (f32[32,4096]{1,0:T(8,128)S(1)}, f32[32,4096]{1,0:T(8,128)S(1)}, u32[]{:S(2)}, u32[]{:S(2)}) collective-permute-start(f32[32,4096]{1,0:T(8,128)S(1)} %copy-done.11), channel_id=1, source_target_pairs={{0,32},{1,33},{2,34},{3,35},{4,36},{5,37},{6,38},{7,39},{8,40},{9,... | collective-permute-start | bytes 1572872 | tf_op jit(solution)/shard_map/ppermute | solution.py:216
  65.4 3.7 %step_1.1.refs_7_ = f32[256,4096]{1,0:T(8,128)S(1)} custom-call(f32[32,4096]{1,0:T(8,128)S(1)} %collective-permute-done.refs_0_, f32[32,4096]{1,0:T(8,128)S(1)} %collective-permute-done.7.refs_1_, f32[32,4096]{1,0:T(8,128)S(1)} %collective-permute-done.8.refs_2_, bf16[256,4096]{1,0:T(8,128)(2,1)S(1)} %get-tuple-element.70.refs_3_, ...), custom_call_target="tpu_custom_call", output_to_operand_aliasing={{}: (7, {})} | custom-call | flops 1610612736 | bytes 2097152 | tf_op jit(solution)/shard_map/step_1/pallas_call | solution.py:188
  70.4 6.3 %collective-permute-done.12.refs_2_ = f32[32,4096]{1,0:T(8,128)S(1)} collective-permute-done((f32[32,4096]{1,0:T(8,128)}, f32[32,4096]{1,0:T(8,128)S(1)}, u32[]{:S(2)}, u32[]{:S(2)}) %collective-permute-start.12) | collective-permute-done | bytes 524320 | tf_op jit(solution)/shard_map/ppermute | solution.py:216
  76.7 4.5 %collective-permute-start.9 = (f32[32,4096]{1,0:T(8,128)S(1)}, f32[32,4096]{1,0:T(8,128)S(1)}, u32[]{:S(2)}, u32[]{:S(2)}) collective-permute-start(f32[32,4096]{1,0:T(8,128)S(1)} %copy-done.10), channel_id=1, source_target_pairs={{0,32},{1,33},{2,34},{3,35},{4,36},{5,37},{6,38},{7,39},{8,40},{9,... | collective-permute-start | bytes 1572872 | tf_op jit(solution)/shard_map/ppermute | solution.py:216
  81.2 4.7 %step_2.1.refs_7_ = f32[256,4096]{1,0:T(8,128)S(1)} custom-call(f32[32,4096]{1,0:T(8,128)} %collective-permute-done.4.refs_0_, f32[32,4096]{1,0:T(8,128)S(1)} %collective-permute-done.11.refs_1_, f32[32,4096]{1,0:T(8,128)S(1)} %collective-permute-done.12.refs_2_, bf16[256,4096]{1,0:T(8,128)(2,1)S(1)} %get-tuple-element.70.refs_3_, ...), custom_call_target="tpu_custom_call", output_to_operand_aliasing={{}: (7, {})} | custom-call | flops 1610612736 | bytes 2097152 | tf_op jit(solution)/shard_map/step_2/pallas_call | solution.py:188
  88.0 1.4 collective-permute-start.16
  89.3 3.7 %step_3.1.refs_7_ = f32[256,4096]{1,0:T(8,128)S(1)} custom-call(f32[32,4096]{1,0:T(8,128)S(1)} %collective-permute-done.2.refs_0_, f32[32,4096]{1,0:T(8,128)S(1)} %collective-permute-done.13.refs_1_, f32[32,4096]{1,0:T(8,128)S(1)} %collective-permute-done.14.refs_2_, ...), custom_call_target="tpu_custom_call", output_to_operand_aliasing={{}: (7, {})} | custom-call | flops 1610612736 | bytes 2097152 | tf_op jit(solution)/shard_map/step_3/pallas_call | solution.py:188
  93.0 3.0 %collective-permute-start.20 = (f32[32,4096]{1,0:T(8,128)S(1)}, f32[32,4096]{1,0:T(8,128)S(1)}, u32[]{:S(2)}, u32[]{:S(2)}) collective-permute-start(f32[32,4096]{1,0:T(8,128)S(1)} %collective-permute-done.9.refs_0_), channel_id=1, source_target_pairs={{0,63},{1,34},{2,33},{3,36},{4,35},{5,38},{6,37},{7,40},{8,39},{9,... | collective-permute-start | bytes 1572872 | tf_op jit(solution)/shard_map/ppermute | solution.py:216
  96.0 5.1 %collective-permute-start.19 = (f32[32,4096]{1,0:T(8,128)S(1)}, f32[32,4096]{1,0:T(8,128)S(1)}, u32[]{:S(2)}, u32[]{:S(2)}) collective-permute-start(f32[32,4096]{1,0:T(8,128)S(1)} %collective-permute-done.9.refs_0_), channel_id=1, source_target_pairs={{0,64},{1,65},{2,66},{3,67},{4,68},{5,69},{6,70},{7,71},{8,72},{9,... | collective-permute-start | bytes 1572872 | tf_op jit(solution)/shard_map/ppermute | solution.py:216
  101.1 5.0 %collective-permute-done.18.refs_2_ = f32[32,4096]{1,0:T(8,128)S(1)} collective-permute-done((f32[32,4096]{1,0:T(8,128)S(1)}, f32[32,4096]{1,0:T(8,128)S(1)}, u32[]{:S(2)}, u32[]{:S(2)}) %collective-permute-start.18) | collective-permute-done | bytes 524320 | tf_op jit(solution)/shard_map/ppermute | solution.py:216
  106.1 3.7 %step_4.1.refs_7_ = f32[256,4096]{1,0:T(8,128)S(1)} custom-call(f32[32,4096]{1,0:T(8,128)S(1)} %collective-permute-done.10.refs_0_, f32[32,4096]{1,0:T(8,128)S(1)} %collective-permute-done.17.refs_1_, f32[32,4096]{1,0:T(8,128)S(1)} %collective-permute-done.18.refs_2_, ...), custom_call_target="tpu_custom_call", output_to_operand_aliasing={{}: (7, {})} | custom-call | flops 1610612736 | bytes 2097152 | tf_op jit(solution)/shard_map/step_4/pallas_call | solution.py:188
  109.8 2.4 %collective-permute-start.24 = (f32[32,4096]{1,0:T(8,128)S(1)}, f32[32,4096]{1,0:T(8,128)S(1)}, u32[]{:S(2)}, u32[]{:S(2)}) collective-permute-start(f32[32,4096]{1,0:T(8,128)S(1)} %collective-permute-done.16.refs_0_), channel_id=1, source_target_pairs={{0,63},{1,34},{2,33},{3,36},{4,35},{5,38},{6,37},{7,40},{8,39},{9,... | collective-permute-start | bytes 1572872 | tf_op jit(solution)/shard_map/ppermute | solution.py:216
  112.5 4.8 %collective-permute-done.20.refs_2_ = f32[32,4096]{1,0:T(8,128)S(1)} collective-permute-done((f32[32,4096]{1,0:T(8,128)S(1)}, f32[32,4096]{1,0:T(8,128)S(1)}, u32[]{:S(2)}, u32[]{:S(2)}) %collective-permute-start.20) | collective-permute-done | bytes 524320 | tf_op jit(solution)/shard_map/ppermute | solution.py:216
  117.3 3.7 %step_5.1.refs_7_ = f32[256,4096]{1,0:T(8,128)S(1)} custom-call(f32[32,4096]{1,0:T(8,128)S(1)} %collective-permute-done.9.refs_0_, f32[32,4096]{1,0:T(8,128)S(1)} %collective-permute-done.19.refs_1_, f32[32,4096]{1,0:T(8,128)S(1)} %collective-permute-done.20.refs_2_, ...), custom_call_target="tpu_custom_call", output_to_operand_aliasing={{}: (7, {})} | custom-call | flops 1610612736 | bytes 2097152 | tf_op jit(solution)/shard_map/step_5/pallas_call | solution.py:188
  121.1 4.8 %collective-permute-start.22 = (f32[32,4096]{1,0:T(8,128)S(1)}, f32[32,4096]{1,0:T(8,128)S(1)}, u32[]{:S(2)}, u32[]{:S(2)}) collective-permute-start(f32[32,4096]{1,0:T(8,128)S(1)} %collective-permute-done.15.refs_0_), channel_id=1, source_target_pairs={{0,63},{1,34},{2,33},{3,36},{4,35},{5,38},{6,37},{7,40},{8,39},{9,... | collective-permute-start | bytes 1572872 | tf_op jit(solution)/shard_map/ppermute | solution.py:216
  126.0 2.5 %collective-permute-done.24.refs_2_ = f32[32,4096]{1,0:T(8,128)S(1)} collective-permute-done((f32[32,4096]{1,0:T(8,128)S(1)}, f32[32,4096]{1,0:T(8,128)S(1)}, u32[]{:S(2)}, u32[]{:S(2)}) %collective-permute-start.24) | collective-permute-done | bytes 524320 | tf_op jit(solution)/shard_map/ppermute | solution.py:216
  128.5 5.2 %step_6.1.refs_7_ = f32[256,4096]{1,0:T(8,128)S(1)} custom-call(f32[32,4096]{1,0:T(8,128)S(1)} %collective-permute-done.16.refs_0_, f32[32,4096]{1,0:T(8,128)S(1)} %collective-permute-done.23.refs_1_, f32[32,4096]{1,0:T(8,128)S(1)} %collective-permute-done.24.refs_2_, ...), custom_call_target="tpu_custom_call", output_to_operand_aliasing={{}: (7, {})} | custom-call | flops 2013265920 | bytes 2621440 | tf_op jit(solution)/shard_map/step_6/pallas_call | solution.py:188
  134.7 3.7 %step_7.1 = f32[256,4096]{1,0:T(8,128)} custom-call(f32[32,4096]{1,0:T(8,128)S(1)} %collective-permute-done.15.refs_0_, f32[32,4096]{1,0:T(8,128)S(1)} %collective-permute-done.21.refs_1_, f32[32,4096]{1,0:T(8,128)S(1)} %collective-permute-done.22.refs_2_, bf16[256,4096]{1,0:T(8,128)(2,1)S(1)} %get-tuple-element.70.refs_3_, bf16[256,4096]{1,0:T(8,128)(2,1)S(1)} %copy-done.1, ...), custom_call_target="tpu_custom_call" | custom-call | flops 1207959552 | bytes 1572864 | tf_op jit(solution)/shard_map/step_7/pallas_call | solution.py:188
  (69 shorter events, 8.8 us)
Async XLA Ops:
  2.3 33.1 %collective-permute-start.1 = (f32[8,32,4096]{2,1,0:T(8,128)}, f32[8,32,4096]{2,1,0:T(8,128)}, u32[]{:S(2)}, u32[]{:S(2)}) collective-permute-start(f32[8,32,4096]{2,1,0:T(8,128)} %param.3), channel_id=1, source_target_pairs={{0,1},{1,0},{2,3},{3,2},{4,5},{5,4},{6,7},{7,6},{8,9},{9,8},{10,11... | collective-permute-start | bytes 12582920 | tf_op jit(solution)/shard_map/ppermute | solution.py:216
  5.6 29.8 %collective-permute-start = (f32[32,4096]{1,0:T(8,128)}, f32[32,4096]{1,0:T(8,128)S(1)}, u32[]{:S(2)}, u32[]{:S(2)}) collective-permute-start(f32[32,4096]{1,0:T(8,128)} %get-tuple-element.55), channel_id=1, source_target_pairs={{0,32},{1,33},{2,34},{3,35},{4,36},{5,37},{6,38},{7,39},{8,40},{9,... | collective-permute-start | bytes 1572872 | tf_op jit(solution)/shard_map/ppermute | solution.py:216
  5.6 24.9 %collective-permute-start.3 = (f32[32,4096]{1,0:T(8,128)}, f32[32,4096]{1,0:T(8,128)S(1)}, u32[]{:S(2)}, u32[]{:S(2)}) collective-permute-start(f32[32,4096]{1,0:T(8,128)} %get-tuple-element.54), channel_id=1, source_target_pairs={{0,32},{1,33},{2,34},{3,35},{4,36},{5,37},{6,38},{7,39},{8,40},{9,... | collective-permute-start | bytes 1572872 | tf_op jit(solution)/shard_map/ppermute | solution.py:216
  30.6 18.9 %collective-permute-start.6 = (f32[32,4096]{1,0:T(8,128)S(1)}, f32[32,4096]{1,0:T(8,128)}, u32[]{:S(2)}, u32[]{:S(2)}) collective-permute-start(f32[32,4096]{1,0:T(8,128)S(1)} %collective-permute-done.3.refs_0_), channel_id=1, source_target_pairs={{0,63},{1,34},{2,33},{3,36},{4,35},{5,38},{6,37},{7,40},{8,39},{9,... | collective-permute-start | bytes 1572872 | tf_op jit(solution)/shard_map/ppermute | solution.py:216
  32.1 17.4 %collective-permute-start.5 = (f32[32,4096]{1,0:T(8,128)S(1)}, f32[32,4096]{1,0:T(8,128)}, u32[]{:S(2)}, u32[]{:S(2)}) collective-permute-start(f32[32,4096]{1,0:T(8,128)S(1)} %collective-permute-done.3.refs_0_), channel_id=1, source_target_pairs={{0,64},{1,65},{2,66},{3,67},{4,68},{5,69},{6,70},{7,71},{8,72},{9,... | collective-permute-start | bytes 1572872 | tf_op jit(solution)/shard_map/ppermute | solution.py:216
  33.4 24.1 %collective-permute-start.4 = (f32[32,4096]{1,0:T(8,128)}, f32[32,4096]{1,0:T(8,128)}, u32[]{:S(2)}, u32[]{:S(2)}) collective-permute-start(f32[32,4096]{1,0:T(8,128)} %get-tuple-element.66), channel_id=1, source_target_pairs={{0,32},{1,33},{2,34},{3,35},{4,36},{5,37},{6,38},{7,39},{8,40},{9,... | collective-permute-start | bytes 1572872 | tf_op jit(solution)/shard_map/ppermute | solution.py:216
  35.5 27.2 %collective-permute-start.8 = (f32[32,4096]{1,0:T(8,128)S(1)}, f32[32,4096]{1,0:T(8,128)S(1)}, u32[]{:S(2)}, u32[]{:S(2)}) collective-permute-start(f32[32,4096]{1,0:T(8,128)S(1)} %collective-permute-done.refs_0_), channel_id=1, source_target_pairs={{0,63},{1,34},{2,33},{3,36},{4,35},{5,38},{6,37},{7,40},{8,39},{9,... | collective-permute-start | bytes 1572872 | tf_op jit(solution)/shard_map/ppermute | solution.py:216
  35.9 29.5 %collective-permute-start.7 = (f32[32,4096]{1,0:T(8,128)S(1)}, f32[32,4096]{1,0:T(8,128)S(1)}, u32[]{:S(2)}, u32[]{:S(2)}) collective-permute-start(f32[32,4096]{1,0:T(8,128)S(1)} %collective-permute-done.refs_0_), channel_id=1, source_target_pairs={{0,64},{1,65},{2,66},{3,67},{4,68},{5,69},{6,70},{7,71},{8,72},{9,... | collective-permute-start | bytes 1572872 | tf_op jit(solution)/shard_map/ppermute | solution.py:216
  49.4 19.6 %collective-permute-start.2 = (f32[32,4096]{1,0:T(8,128)}, f32[32,4096]{1,0:T(8,128)S(1)}, u32[]{:S(2)}, u32[]{:S(2)}) collective-permute-start(f32[32,4096]{1,0:T(8,128)} %get-tuple-element.63), channel_id=1, source_target_pairs={{0,32},{1,33},{2,34},{3,35},{4,36},{5,37},{6,38},{7,39},{8,40},{9,... | collective-permute-start | bytes 1572872 | tf_op jit(solution)/shard_map/ppermute | solution.py:216
  51.0 11.7 %copy-start.11 = (f32[32,4096]{1,0:T(8,128)S(1)}, f32[32,4096]{1,0:T(8,128)}, u32[]{:S(2)}) copy-start(f32[32,4096]{1,0:T(8,128)} %get-tuple-element.80) | copy-start | bytes 1572868
  51.0 14.2 %copy-start.7 = (f32[1,96]{1,0:T(1,128)S(1)}, f32[1,96]{1,0:T(1,128)}, u32[]{:S(2)}) copy-start(f32[1,96]{1,0:T(1,128)} %get-tuple-element.109) | copy-start | bytes 1156
  57.5 19.2 %collective-permute-start.12 = (f32[32,4096]{1,0:T(8,128)}, f32[32,4096]{1,0:T(8,128)S(1)}, u32[]{:S(2)}, u32[]{:S(2)}) collective-permute-start(f32[32,4096]{1,0:T(8,128)} %collective-permute-done.4.refs_0_), channel_id=1, source_target_pairs={{0,63},{1,34},{2,33},{3,36},{4,35},{5,38},{6,37},{7,40},{8,39},{9,... | collective-permute-start | bytes 1572872 | tf_op jit(solution)/shard_map/ppermute | solution.py:216
  61.4 15.3 %collective-permute-start.11 = (f32[32,4096]{1,0:T(8,128)}, f32[32,4096]{1,0:T(8,128)S(1)}, u32[]{:S(2)}, u32[]{:S(2)}) collective-permute-start(f32[32,4096]{1,0:T(8,128)} %collective-permute-done.4.refs_0_), channel_id=1, source_target_pairs={{0,64},{1,65},{2,66},{3,67},{4,68},{5,69},{6,70},{7,71},{8,72},{9,... | collective-permute-start | bytes 1572872 | tf_op jit(solution)/shard_map/ppermute | solution.py:216
  62.7 23.3 %collective-permute-start.10 = (f32[32,4096]{1,0:T(8,128)S(1)}, f32[32,4096]{1,0:T(8,128)S(1)}, u32[]{:S(2)}, u32[]{:S(2)}) collective-permute-start(f32[32,4096]{1,0:T(8,128)S(1)} %copy-done.11), channel_id=1, source_target_pairs={{0,32},{1,33},{2,34},{3,35},{4,36},{5,37},{6,38},{7,39},{8,40},{9,... | collective-permute-start | bytes 1572872 | tf_op jit(solution)/shard_map/ppermute | solution.py:216
  65.3 11.3 %copy-start.10 = (f32[32,4096]{1,0:T(8,128)S(1)}, f32[32,4096]{1,0:T(8,128)}, u32[]{:S(2)}) copy-start(f32[32,4096]{1,0:T(8,128)} %get-tuple-element.78) | copy-start | bytes 1572868
  69.1 18.9 %collective-permute-start.14 = (f32[32,4096]{1,0:T(8,128)S(1)}, f32[32,4096]{1,0:T(8,128)S(1)}, u32[]{:S(2)}, u32[]{:S(2)}) collective-permute-start(f32[32,4096]{1,0:T(8,128)S(1)} %collective-permute-done.2.refs_0_), channel_id=1, source_target_pairs={{0,63},{1,34},{2,33},{3,36},{4,35},{5,38},{6,37},{7,40},{8,39},{9,... | collective-permute-start | bytes 1572872 | tf_op jit(solution)/shard_map/ppermute | solution.py:216
  69.2 20.1 %collective-permute-start.13 = (f32[32,4096]{1,0:T(8,128)S(1)}, f32[32,4096]{1,0:T(8,128)S(1)}, u32[]{:S(2)}, u32[]{:S(2)}) collective-permute-start(f32[32,4096]{1,0:T(8,128)S(1)} %collective-permute-done.2.refs_0_), channel_id=1, source_target_pairs={{0,64},{1,65},{2,66},{3,67},{4,68},{5,69},{6,70},{7,71},{8,72},{9,... | collective-permute-start | bytes 1572872 | tf_op jit(solution)/shard_map/ppermute | solution.py:216
  76.7 11.2 %copy-start.5 = (f32[1,96]{1,0:T(1,128)S(1)}, f32[1,96]{1,0:T(1,128)}, u32[]{:S(2)}) copy-start(f32[1,96]{1,0:T(1,128)} %get-tuple-element.107) | copy-start | bytes 1156
  76.7 11.3 %copy-start.9 = (f32[32,4096]{1,0:T(8,128)S(1)}, f32[32,4096]{1,0:T(8,128)}, u32[]{:S(2)}) copy-start(f32[32,4096]{1,0:T(8,128)} %get-tuple-element.91) | copy-start | bytes 1572868
  76.7 16.3 %collective-permute-start.9 = (f32[32,4096]{1,0:T(8,128)S(1)}, f32[32,4096]{1,0:T(8,128)S(1)}, u32[]{:S(2)}, u32[]{:S(2)}) collective-permute-start(f32[32,4096]{1,0:T(8,128)S(1)} %copy-done.10), channel_id=1, source_target_pairs={{0,32},{1,33},{2,34},{3,35},{4,36},{5,37},{6,38},{7,39},{8,40},{9,... | collective-permute-start | bytes 1572872 | tf_op jit(solution)/shard_map/ppermute | solution.py:216
  86.0 20.1 %collective-permute-start.18 = (f32[32,4096]{1,0:T(8,128)S(1)}, f32[32,4096]{1,0:T(8,128)S(1)}, u32[]{:S(2)}, u32[]{:S(2)}) collective-permute-start(f32[32,4096]{1,0:T(8,128)S(1)} %collective-permute-done.10.refs_0_), channel_id=1, source_target_pairs={{0,63},{1,34},{2,33},{3,36},{4,35},{5,38},{6,37},{7,40},{8,39},{9,... | collective-permute-start | bytes 1572872 | tf_op jit(solution)/shard_map/ppermute | solution.py:216
  86.6 19.5 %collective-permute-start.17 = (f32[32,4096]{1,0:T(8,128)S(1)}, f32[32,4096]{1,0:T(8,128)S(1)}, u32[]{:S(2)}, u32[]{:S(2)}) collective-permute-start(f32[32,4096]{1,0:T(8,128)S(1)} %collective-permute-done.10.refs_0_), channel_id=1, source_target_pairs={{0,64},{1,65},{2,66},{3,67},{4,68},{5,69},{6,70},{7,71},{8,72},{9,... | collective-permute-start | bytes 1572872 | tf_op jit(solution)/shard_map/ppermute | solution.py:216
  88.0 18.1 %copy-start.8 = (f32[32,4096]{1,0:T(8,128)S(1)}, f32[32,4096]{1,0:T(8,128)}, u32[]{:S(2)}) copy-start(f32[32,4096]{1,0:T(8,128)} %get-tuple-element.89) | copy-start | bytes 1572868
  88.0 18.1 %copy-start.4 = (f32[1,96]{1,0:T(1,128)S(1)}, f32[1,96]{1,0:T(1,128)}, u32[]{:S(2)}) copy-start(f32[1,96]{1,0:T(1,128)} %get-tuple-element.106) | copy-start | bytes 1156
  88.0 21.9 %collective-permute-start.16 = (f32[32,4096]{1,0:T(8,128)S(1)}, f32[32,4096]{1,0:T(8,128)S(1)}, u32[]{:S(2)}, u32[]{:S(2)}) collective-permute-start(f32[32,4096]{1,0:T(8,128)S(1)} %copy-done.9), channel_id=1, source_target_pairs={{0,32},{1,33},{2,34},{3,35},{4,36},{5,37},{6,38},{7,39},{8,40},{9,... | collective-permute-start | bytes 1572872 | tf_op jit(solution)/shard_map/ppermute | solution.py:216
  93.0 24.3 %collective-permute-start.20 = (f32[32,4096]{1,0:T(8,128)S(1)}, f32[32,4096]{1,0:T(8,128)S(1)}, u32[]{:S(2)}, u32[]{:S(2)}) collective-permute-start(f32[32,4096]{1,0:T(8,128)S(1)} %collective-permute-done.9.refs_0_), channel_id=1, source_target_pairs={{0,63},{1,34},{2,33},{3,36},{4,35},{5,38},{6,37},{7,40},{8,39},{9,... | collective-permute-start | bytes 1572872 | tf_op jit(solution)/shard_map/ppermute | solution.py:216
  96.0 21.3 %collective-permute-start.19 = (f32[32,4096]{1,0:T(8,128)S(1)}, f32[32,4096]{1,0:T(8,128)S(1)}, u32[]{:S(2)}, u32[]{:S(2)}) collective-permute-start(f32[32,4096]{1,0:T(8,128)S(1)} %collective-permute-done.9.refs_0_), channel_id=1, source_target_pairs={{0,64},{1,65},{2,66},{3,67},{4,68},{5,69},{6,70},{7,71},{8,72},{9,... | collective-permute-start | bytes 1572872 | tf_op jit(solution)/shard_map/ppermute | solution.py:216
  106.1 14.9 %collective-permute-start.15 = (f32[32,4096]{1,0:T(8,128)S(1)}, f32[32,4096]{1,0:T(8,128)S(1)}, u32[]{:S(2)}, u32[]{:S(2)}) collective-permute-start(f32[32,4096]{1,0:T(8,128)S(1)} %copy-done.8), channel_id=1, source_target_pairs={{0,32},{1,33},{2,34},{3,35},{4,36},{5,37},{6,38},{7,39},{8,40},{9,... | collective-permute-start | bytes 1572872 | tf_op jit(solution)/shard_map/ppermute | solution.py:216
  109.8 18.7 %collective-permute-start.24 = (f32[32,4096]{1,0:T(8,128)S(1)}, f32[32,4096]{1,0:T(8,128)S(1)}, u32[]{:S(2)}, u32[]{:S(2)}) collective-permute-start(f32[32,4096]{1,0:T(8,128)S(1)} %collective-permute-done.16.refs_0_), channel_id=1, source_target_pairs={{0,63},{1,34},{2,33},{3,36},{4,35},{5,38},{6,37},{7,40},{8,39},{9,... | collective-permute-start | bytes 1572872 | tf_op jit(solution)/shard_map/ppermute | solution.py:216
  112.2 16.3 %collective-permute-start.23 = (f32[32,4096]{1,0:T(8,128)S(1)}, f32[32,4096]{1,0:T(8,128)S(1)}, u32[]{:S(2)}, u32[]{:S(2)}) collective-permute-start(f32[32,4096]{1,0:T(8,128)S(1)} %collective-permute-done.16.refs_0_), channel_id=1, source_target_pairs={{0,64},{1,65},{2,66},{3,67},{4,68},{5,69},{6,70},{7,71},{8,72},{9,... | collective-permute-start | bytes 1572872 | tf_op jit(solution)/shard_map/ppermute | solution.py:216
  121.0 13.7 %collective-permute-start.21 = (f32[32,4096]{1,0:T(8,128)S(1)}, f32[32,4096]{1,0:T(8,128)S(1)}, u32[]{:S(2)}, u32[]{:S(2)}) collective-permute-start(f32[32,4096]{1,0:T(8,128)S(1)} %collective-permute-done.15.refs_0_), channel_id=1, source_target_pairs={{0,64},{1,65},{2,66},{3,67},{4,68},{5,69},{6,70},{7,71},{8,72},{9,... | collective-permute-start | bytes 1572872 | tf_op jit(solution)/shard_map/ppermute | solution.py:216
  121.1 13.7 %collective-permute-start.22 = (f32[32,4096]{1,0:T(8,128)S(1)}, f32[32,4096]{1,0:T(8,128)S(1)}, u32[]{:S(2)}, u32[]{:S(2)}) collective-permute-start(f32[32,4096]{1,0:T(8,128)S(1)} %collective-permute-done.15.refs_0_), channel_id=1, source_target_pairs={{0,63},{1,34},{2,33},{3,36},{4,35},{5,38},{6,37},{7,40},{8,39},{9,... | collective-permute-start | bytes 1572872 | tf_op jit(solution)/shard_map/ppermute | solution.py:216
  (5 other events, 22.1 us)
where the time goes:
time: 139 us
  waiting for transfers between devices  47.5 us (34%)
  starting transfers between devices  42.4 us (31%)
  Pallas kernels  42 us (30%)
  local copies, waits for them, and re-layouts  4.94 us (4%)
    ppermute x25, waiting for transfers between devices, moved(): return lax.ppermute(block, AXES, route)  47.5 us
    ppermute x25, starting transfers between devices, moved(): return lax.ppermute(block, AXES, route)  42.4 us
    pallas_call x8, Pallas kernels, step_call(): pl.pallas_call(functools.partial(step_kernel, (len(others), own, inner_ro...  34.8 us
    pallas_call x1, Pallas kernels, own_call(): pl.pallas_call(functools.partial(own_kernel, skip), out_shape=(factor, fa...  4.95 us
    unnamed x24, local copies, waits for them, and re-layouts  2.94 us
  transfers between devices with their start and end apart: 25, of which 7 were waited for; matrix products, arithmetic and copies ran while one was open for 2% of the time, Pallas kernels for 26%

commit v1 on v0

--- a/solution.py
+++ b/solution.py
@@ -251,11 +251,12 @@
         return lax.optimization_barrier((value, earlier))[0]
 
     mine = b_factors.reshape(occ_block * vir_block, width)
-    parts = list(cut_call(mine, 2, vir_block))
+    parts = list(cut_call(mine, 1, vir_block))
     near = [moved(part, across) for part in parts]
-    inner = moved(held(b_factors, *parts), inward).reshape(mine.shape)
-    high, low, a_high, a_low, *rest = own_call(held(mine, *parts), gap_row, gap.reshape(1, -1), 2, vir_block)
+    high, low, a_high, a_low, *rest = own_call(held(mine, *parts), gap_row, gap.reshape(1, -1), 1, vir_block)
     parts += rest
+    near.append(moved(parts[1], across))
+    inner = moved(held(b_factors, parts[0]), inward).reshape(mine.shape)
 
     done = [a_high, a_high]
     far, outer = [], []

time: 139 us -> 122 us (0.88)
  waiting for transfers between devices: 47.5 us -> 24.5 us
  starting transfers between devices: 42.4 us -> 49.4 us
    ppermute x25, waiting for transfers between devices: 47.5 us -> 24.5 us  [moved(): return lax.ppermute(block, AXES, route)]
    ppermute x25, starting transfers between devices: 42.4 us -> 49.4 us  [moved(): return lax.ppermute(block, AXES, route)]
    unnamed x24 -> x28, local copies, waits for them, and re-layouts: 2.94 us -> 2.95 us
  transfers between devices with their start and end apart: 25 -> 25, of which waited for: 7 -> 10; matrix products, arithmetic and copies ran while one was open for 2% -> 3% of each run, Pallas kernels for 26% -> 30%
where the time goes in v1:
time: 122 us
  starting transfers between devices  49.4 us (40%)
  Pallas kernels  40.8 us (33%)
  waiting for transfers between devices  24.5 us (20%)
  local copies, waits for them, and re-layouts  4.94 us (4%)
  other arithmetic  1.88 us (2%)
    ppermute x25, starting transfers between devices, moved(): return lax.ppermute(block, AXES, route)  49.4 us
    pallas_call x8, Pallas kernels, step_call(): pl.pallas_call(functools.partial(step_kernel, (len(others), own, inner_ro...  34.7 us
    ppermute x25, waiting for transfers between devices, moved(): return lax.ppermute(block, AXES, route)  24.5 us
    pallas_call x1, Pallas kernels, own_call(): pl.pallas_call(functools.partial(own_kernel, skip), out_shape=(factor, fa...  4.98 us
    unnamed x28, local copies, waits for them, and re-layouts  2.95 us
  transfers between devices with their start and end apart: 25, of which 10 were waited for; matrix products, arithmetic and copies ran while one was open for 3% of the time, Pallas kernels for 30%

profile of v1, /device:TPU:1, one launch (start us, length us, event | category | flops | bytes accessed | tf_op | source)
XLA Modules:
  0.0 121.8 jit_solution(7795433136636730652)
XLA Ops:
  1.1 3.3 %collective-permute-start.1 = (f32[8,32,4096]{2,1,0:T(8,128)}, f32[8,32,4096]{2,1,0:T(8,128)}, u32[]{:S(2)}, u32[]{:S(2)}) collective-permute-start(f32[8,32,4096]{2,1,0:T(8,128)} %param.3), channel_id=1, source_target_pairs={{0,1},{1,0},{2,3},{3,2},{4,5},{5,4},{6,7},{7,6},{8,9},{9,8},{10,11... | collective-permute-start | bytes 12582920 | tf_op jit(solution)/shard_map/ppermute | solution.py:216
  6.2 5.0 %own_block.1 = (bf16[256,4096]{1,0:T(8,128)(2,1)S(1)}, bf16[256,4096]{1,0:T(8,128)(2,1)S(1)}, bf16[256,256]{1,0:T(8,128)(2,1)S(1)}, bf16[256,256]{1,0:T(8,128)(2...) custom-call(f32[256,4096]{1,0:T(8,128)} %bitcast.mine_ref, ...), custom_call_target="tpu_custom_call" | custom-call | flops 3221225472 | bytes 4194304 | tf_op jit(solution)/shard_map/own_block/pallas_call | solution.py:161
  11.3 1.3 %copy-done = bf16[256,4096]{1,0:T(8,128)(2,1)} copy-done((bf16[256,4096]{1,0:T(8,128)(2,1)}, bf16[256,4096]{1,0:T(8,128)(2,1)S(1)}, u32[]{:S(2)}) %copy-start) | copy-done | bytes 2097176
  12.6 1.5 %collective-permute-start = (f32[32,4096]{1,0:T(8,128)}, f32[32,4096]{1,0:T(8,128)}, u32[]{:S(2)}, u32[]{:S(2)}) collective-permute-start(f32[32,4096]{1,0:T(8,128)} %get-tuple-element.57), channel_id=1, source_target_pairs={{0,32},{1,33},{2,34},{3,35},{4,36},{5,37},{6,38},{7,39},{8,40},{9,... | collective-permute-start | bytes 1572872 | tf_op jit(solution)/shard_map/ppermute | solution.py:216
  14.1 3.7 %collective-permute-done.3.refs_0_ = f32[32,4096]{1,0:T(8,128)S(1)} collective-permute-done((f32[32,4096]{1,0:T(8,128)S(1)}, f32[32,4096]{1,0:T(8,128)S(1)}, u32[]{:S(2)}, u32[]{:S(2)}) %collective-permute-start.3) | collective-permute-done | bytes 524320 | tf_op jit(solution)/shard_map/ppermute | solution.py:216
  17.9 2.0 %collective-permute-start.6 = (f32[32,4096]{1,0:T(8,128)S(1)}, f32[32,4096]{1,0:T(8,128)}, u32[]{:S(2)}, u32[]{:S(2)}) collective-permute-start(f32[32,4096]{1,0:T(8,128)S(1)} %collective-permute-done.3.refs_0_), channel_id=1, source_target_pairs={{0,63},{1,34},{2,33},{3,36},{4,35},{5,38},{6,37},{7,40},{8,39},{9,... | collective-permute-start | bytes 1572872 | tf_op jit(solution)/shard_map/ppermute | solution.py:216
  19.9 1.3 %collective-permute-start.5 = (f32[32,4096]{1,0:T(8,128)S(1)}, f32[32,4096]{1,0:T(8,128)}, u32[]{:S(2)}, u32[]{:S(2)}) collective-permute-start(f32[32,4096]{1,0:T(8,128)S(1)} %collective-permute-done.3.refs_0_), channel_id=1, source_target_pairs={{0,64},{1,65},{2,66},{3,67},{4,68},{5,69},{6,70},{7,71},{8,72},{9,... | collective-permute-start | bytes 1572872 | tf_op jit(solution)/shard_map/ppermute | solution.py:216
  21.2 1.4 %collective-permute-start.4 = (f32[32,4096]{1,0:T(8,128)}, f32[32,4096]{1,0:T(8,128)S(1)}, u32[]{:S(2)}, u32[]{:S(2)}) collective-permute-start(f32[32,4096]{1,0:T(8,128)} %get-tuple-element.64), channel_id=1, source_target_pairs={{0,32},{1,33},{2,34},{3,35},{4,36},{5,37},{6,38},{7,39},{8,40},{9,... | collective-permute-start | bytes 1572872 | tf_op jit(solution)/shard_map/ppermute | solution.py:216
  23.2 6.0 %collective-permute-done.refs_0_ = f32[32,4096]{1,0:T(8,128)} collective-permute-done((f32[32,4096]{1,0:T(8,128)}, f32[32,4096]{1,0:T(8,128)}, u32[]{:S(2)}, u32[]{:S(2)}) %collective-permute-start) | collective-permute-done | bytes 524320 | tf_op jit(solution)/shard_map/ppermute | solution.py:216
  29.2 2.0 %collective-permute-start.8 = (f32[32,4096]{1,0:T(8,128)}, f32[32,4096]{1,0:T(8,128)S(1)}, u32[]{:S(2)}, u32[]{:S(2)}) collective-permute-start(f32[32,4096]{1,0:T(8,128)} %collective-permute-done.refs_0_), channel_id=1, source_target_pairs={{0,63},{1,34},{2,33},{3,36},{4,35},{5,38},{6,37},{7,40},{8,39},{9,... | collective-permute-start | bytes 1572872 | tf_op jit(solution)/shard_map/ppermute | solution.py:216
  31.2 1.3 %collective-permute-start.7 = (f32[32,4096]{1,0:T(8,128)}, f32[32,4096]{1,0:T(8,128)S(1)}, u32[]{:S(2)}, u32[]{:S(2)}) collective-permute-start(f32[32,4096]{1,0:T(8,128)} %collective-permute-done.refs_0_), channel_id=1, source_target_pairs={{0,64},{1,65},{2,66},{3,67},{4,68},{5,69},{6,70},{7,71},{8,72},{9,... | collective-permute-start | bytes 1572872 | tf_op jit(solution)/shard_map/ppermute | solution.py:216
  34.7 1.6 %copy-done.1 = bf16[256,4096]{1,0:T(8,128)(2,1)S(1)} copy-done((bf16[256,4096]{1,0:T(8,128)(2,1)S(1)}, bf16[256,4096]{1,0:T(8,128)(2,1)}, u32[]{:S(2)}) %copy-start.1) | copy-done | bytes 2097176
  36.3 6.4 %step_0.1.refs_7_ = f32[256,4096]{1,0:T(8,128)S(1)} custom-call(f32[32,4096]{1,0:T(8,128)S(1)} %collective-permute-done.3.refs_0_, f32[32,4096]{1,0:T(8,128)} %collective-permute-done.5.refs_1_, f32[32,4096]{1,0:T(8,128)} %collective-permute-done.6.refs_2_, bf16[256,4096]{1,0:T(8,128)(2,1)S(1)} %get-tuple-element.68.refs_3_, ...), custom_call_target="tpu_custom_call" | custom-call | flops 1610612736 | bytes 2097152 | tf_op jit(solution)/shard_map/step_0/pallas_call | solution.py:188
  45.2 2.2 %collective-permute-start.10 = (f32[32,4096]{1,0:T(8,128)S(1)}, f32[32,4096]{1,0:T(8,128)S(1)}, u32[]{:S(2)}, u32[]{:S(2)}) collective-permute-start(f32[32,4096]{1,0:T(8,128)S(1)} %copy-done.13), channel_id=1, source_target_pairs={{0,32},{1,33},{2,34},{3,35},{4,36},{5,37},{6,38},{7,39},{8,40},{9,... | collective-permute-start | bytes 1572872 | tf_op jit(solution)/shard_map/ppermute | solution.py:216
  47.5 4.8 %step_1.1.refs_7_ = f32[256,4096]{1,0:T(8,128)S(1)} custom-call(f32[32,4096]{1,0:T(8,128)} %collective-permute-done.refs_0_, f32[32,4096]{1,0:T(8,128)S(1)} %collective-permute-done.7.refs_1_, f32[32,4096]{1,0:T(8,128)S(1)} %collective-permute-done.8.refs_2_, bf16[256,4096]{1,0:T(8,128)(2,1)S(1)} %get-tuple-element.68.refs_3_, ...), custom_call_target="tpu_custom_call", output_to_operand_aliasing={{}: (7, {})} | custom-call | flops 1610612736 | bytes 2097152 | tf_op jit(solution)/shard_map/step_1/pallas_call | solution.py:188
  56.9 3.7 %step_2.1.refs_7_ = f32[256,4096]{1,0:T(8,128)S(1)} custom-call(f32[32,4096]{1,0:T(8,128)S(1)} %collective-permute-done.4.refs_0_, f32[32,4096]{1,0:T(8,128)S(1)} %collective-permute-done.11.refs_1_, f32[32,4096]{1,0:T(8,128)S(1)} %collective-permute-done.12.refs_2_, ...), custom_call_target="tpu_custom_call", output_to_operand_aliasing={{}: (7, {})} | custom-call | flops 1610612736 | bytes 2097152 | tf_op jit(solution)/shard_map/step_2/pallas_call | solution.py:188
  60.5 2.1 %collective-permute-done.10.refs_0_ = f32[32,4096]{1,0:T(8,128)S(1)} collective-permute-done((f32[32,4096]{1,0:T(8,128)S(1)}, f32[32,4096]{1,0:T(8,128)S(1)}, u32[]{:S(2)}, u32[]{:S(2)}) %collective-permute-start.10) | collective-permute-done | bytes 524320 | tf_op jit(solution)/shard_map/ppermute | solution.py:216
  62.6 2.5 %collective-permute-start.18 = (f32[32,4096]{1,0:T(8,128)S(1)}, f32[32,4096]{1,0:T(8,128)S(1)}, u32[]{:S(2)}, u32[]{:S(2)}) collective-permute-start(f32[32,4096]{1,0:T(8,128)S(1)} %collective-permute-done.10.refs_0_), channel_id=1, source_target_pairs={{0,63},{1,34},{2,33},{3,36},{4,35},{5,38},{6,37},{7,40},{8,39},{9,... | collective-permute-start | bytes 1572872 | tf_op jit(solution)/shard_map/ppermute | solution.py:216
  65.1 5.5 %collective-permute-start.17 = (f32[32,4096]{1,0:T(8,128)S(1)}, f32[32,4096]{1,0:T(8,128)S(1)}, u32[]{:S(2)}, u32[]{:S(2)}) collective-permute-start(f32[32,4096]{1,0:T(8,128)S(1)} %collective-permute-done.10.refs_0_), channel_id=1, source_target_pairs={{0,64},{1,65},{2,66},{3,67},{4,68},{5,69},{6,70},{7,71},{8,72},{9,... | collective-permute-start | bytes 1572872 | tf_op jit(solution)/shard_map/ppermute | solution.py:216
  70.7 1.8 %collective-permute-start.16 = (f32[32,4096]{1,0:T(8,128)S(1)}, f32[32,4096]{1,0:T(8,128)S(1)}, u32[]{:S(2)}, u32[]{:S(2)}) collective-permute-start(f32[32,4096]{1,0:T(8,128)S(1)} %copy-done.11), channel_id=1, source_target_pairs={{0,32},{1,33},{2,34},{3,35},{4,36},{5,37},{6,38},{7,39},{8,40},{9,... | collective-permute-start | bytes 1572872 | tf_op jit(solution)/shard_map/ppermute | solution.py:216
  72.5 3.7 %step_3.1.refs_7_ = f32[256,4096]{1,0:T(8,128)S(1)} custom-call(f32[32,4096]{1,0:T(8,128)S(1)} %collective-permute-done.2.refs_0_, f32[32,4096]{1,0:T(8,128)S(1)} %collective-permute-done.13.refs_1_, f32[32,4096]{1,0:T(8,128)S(1)} %collective-permute-done.14.refs_2_, ...), custom_call_target="tpu_custom_call", output_to_operand_aliasing={{}: (7, {})} | custom-call | flops 1610612736 | bytes 2097152 | tf_op jit(solution)/shard_map/step_3/pallas_call | solution.py:188
  76.4 5.3 %collective-permute-start.19 = (f32[32,4096]{1,0:T(8,128)S(1)}, f32[32,4096]{1,0:T(8,128)S(1)}, u32[]{:S(2)}, u32[]{:S(2)}) collective-permute-start(f32[32,4096]{1,0:T(8,128)S(1)} %collective-permute-done.9.refs_0_), channel_id=1, source_target_pairs={{0,64},{1,65},{2,66},{3,67},{4,68},{5,69},{6,70},{7,71},{8,72},{9,... | collective-permute-start | bytes 1572872 | tf_op jit(solution)/shard_map/ppermute | solution.py:216
  81.7 2.0 %collective-permute-done.18.refs_2_ = f32[32,4096]{1,0:T(8,128)S(1)} collective-permute-done((f32[32,4096]{1,0:T(8,128)S(1)}, f32[32,4096]{1,0:T(8,128)S(1)}, u32[]{:S(2)}, u32[]{:S(2)}) %collective-permute-start.18) | collective-permute-done | bytes 524320 | tf_op jit(solution)/shard_map/ppermute | solution.py:216
  84.9 3.7 %step_4.1.refs_7_ = f32[256,4096]{1,0:T(8,128)S(1)} custom-call(f32[32,4096]{1,0:T(8,128)S(1)} %collective-permute-done.10.refs_0_, f32[32,4096]{1,0:T(8,128)S(1)} %collective-permute-done.17.refs_1_, f32[32,4096]{1,0:T(8,128)S(1)} %collective-permute-done.18.refs_2_, ...), custom_call_target="tpu_custom_call", output_to_operand_aliasing={{}: (7, {})} | custom-call | flops 1610612736 | bytes 2097152 | tf_op jit(solution)/shard_map/step_4/pallas_call | solution.py:188
  88.6 3.5 %collective-permute-start.24 = (f32[32,4096]{1,0:T(8,128)S(1)}, f32[32,4096]{1,0:T(8,128)S(1)}, u32[]{:S(2)}, u32[]{:S(2)}) collective-permute-start(f32[32,4096]{1,0:T(8,128)S(1)} %collective-permute-done.16.refs_0_), channel_id=1, source_target_pairs={{0,63},{1,34},{2,33},{3,36},{4,35},{5,38},{6,37},{7,40},{8,39},{9,... | collective-permute-start | bytes 1572872 | tf_op jit(solution)/shard_map/ppermute | solution.py:216
  93.1 1.8 %collective-permute-done.20.refs_2_ = f32[32,4096]{1,0:T(8,128)S(1)} collective-permute-done((f32[32,4096]{1,0:T(8,128)S(1)}, f32[32,4096]{1,0:T(8,128)S(1)}, u32[]{:S(2)}, u32[]{:S(2)}) %collective-permute-start.20) | collective-permute-done | bytes 524320 | tf_op jit(solution)/shard_map/ppermute | solution.py:216
  94.9 3.7 %step_5.1.refs_7_ = f32[256,4096]{1,0:T(8,128)S(1)} custom-call(f32[32,4096]{1,0:T(8,128)S(1)} %collective-permute-done.9.refs_0_, f32[32,4096]{1,0:T(8,128)S(1)} %collective-permute-done.19.refs_1_, f32[32,4096]{1,0:T(8,128)S(1)} %collective-permute-done.20.refs_2_, ...), custom_call_target="tpu_custom_call", output_to_operand_aliasing={{}: (7, {})} | custom-call | flops 1610612736 | bytes 2097152 | tf_op jit(solution)/shard_map/step_5/pallas_call | solution.py:188
  99.7 5.6 %collective-permute-start.22 = (f32[32,4096]{1,0:T(8,128)S(1)}, f32[32,4096]{1,0:T(8,128)S(1)}, u32[]{:S(2)}, u32[]{:S(2)}) collective-permute-start(f32[32,4096]{1,0:T(8,128)S(1)} %collective-permute-done.15.refs_0_), channel_id=1, source_target_pairs={{0,63},{1,34},{2,33},{3,36},{4,35},{5,38},{6,37},{7,40},{8,39},{9,... | collective-permute-start | bytes 1572872 | tf_op jit(solution)/shard_map/ppermute | solution.py:216
  105.4 2.1 %collective-permute-done.23.refs_1_ = f32[32,4096]{1,0:T(8,128)S(1)} collective-permute-done((f32[32,4096]{1,0:T(8,128)S(1)}, f32[32,4096]{1,0:T(8,128)S(1)}, u32[]{:S(2)}, u32[]{:S(2)}) %collective-permute-start.23) | collective-permute-done | bytes 524320 | tf_op jit(solution)/shard_map/ppermute | solution.py:216
  107.5 5.2 %step_6.1.refs_7_ = f32[256,4096]{1,0:T(8,128)S(1)} custom-call(f32[32,4096]{1,0:T(8,128)S(1)} %collective-permute-done.16.refs_0_, f32[32,4096]{1,0:T(8,128)S(1)} %collective-permute-done.23.refs_1_, f32[32,4096]{1,0:T(8,128)S(1)} %collective-permute-done.24.refs_2_, ...), custom_call_target="tpu_custom_call", output_to_operand_aliasing={{}: (7, {})} | custom-call | flops 2013265920 | bytes 2621440 | tf_op jit(solution)/shard_map/step_6/pallas_call | solution.py:188
  112.7 5.2 %collective-permute-done.21.refs_1_ = f32[32,4096]{1,0:T(8,128)S(1)} collective-permute-done((f32[32,4096]{1,0:T(8,128)S(1)}, f32[32,4096]{1,0:T(8,128)S(1)}, u32[]{:S(2)}, u32[]{:S(2)}) %collective-permute-start.21) | collective-permute-done | bytes 524320 | tf_op jit(solution)/shard_map/ppermute | solution.py:216
  117.9 3.7 %step_7.1 = f32[256,4096]{1,0:T(8,128)} custom-call(f32[32,4096]{1,0:T(8,128)S(1)} %collective-permute-done.15.refs_0_, f32[32,4096]{1,0:T(8,128)S(1)} %collective-permute-done.21.refs_1_, f32[32,4096]{1,0:T(8,128)S(1)} %collective-permute-done.22.refs_2_, bf16[256,4096]{1,0:T(8,128)(2,1)S(1)} %get-tuple-element.68.refs_3_, bf16[256,4096]{1,0:T(8,128)(2,1)S(1)} %copy-done.1, ...), custom_call_target="tpu_custom_call" | custom-call | flops 1207959552 | bytes 1572864 | tf_op jit(solution)/shard_map/step_7/pallas_call | solution.py:188
  (73 shorter events, 16.7 us)
Async XLA Ops:
  1.1 28.2 %collective-permute-start.1 = (f32[8,32,4096]{2,1,0:T(8,128)}, f32[8,32,4096]{2,1,0:T(8,128)}, u32[]{:S(2)}, u32[]{:S(2)}) collective-permute-start(f32[8,32,4096]{2,1,0:T(8,128)} %param.3), channel_id=1, source_target_pairs={{0,1},{1,0},{2,3},{3,2},{4,5},{5,4},{6,7},{7,6},{8,9},{9,8},{10,11... | collective-permute-start | bytes 12582920 | tf_op jit(solution)/shard_map/ppermute | solution.py:216
  4.4 13.5 %collective-permute-start.3 = (f32[32,4096]{1,0:T(8,128)S(1)}, f32[32,4096]{1,0:T(8,128)S(1)}, u32[]{:S(2)}, u32[]{:S(2)}) collective-permute-start(f32[32,4096]{1,0:T(8,128)S(1)} %first_cuts.1), channel_id=1, source_target_pairs={{0,32},{1,33},{2,34},{3,35},{4,36},{5,37},{6,38},{7,39},{8,40},{9,... | collective-permute-start | bytes 1572872 | tf_op jit(solution)/shard_map/ppermute | solution.py:216
  12.6 16.7 %collective-permute-start = (f32[32,4096]{1,0:T(8,128)}, f32[32,4096]{1,0:T(8,128)}, u32[]{:S(2)}, u32[]{:S(2)}) collective-permute-start(f32[32,4096]{1,0:T(8,128)} %get-tuple-element.57), channel_id=1, source_target_pairs={{0,32},{1,33},{2,34},{3,35},{4,36},{5,37},{6,38},{7,39},{8,40},{9,... | collective-permute-start | bytes 1572872 | tf_op jit(solution)/shard_map/ppermute | solution.py:216
  17.9 15.8 %collective-permute-start.6 = (f32[32,4096]{1,0:T(8,128)S(1)}, f32[32,4096]{1,0:T(8,128)}, u32[]{:S(2)}, u32[]{:S(2)}) collective-permute-start(f32[32,4096]{1,0:T(8,128)S(1)} %collective-permute-done.3.refs_0_), channel_id=1, source_target_pairs={{0,63},{1,34},{2,33},{3,36},{4,35},{5,38},{6,37},{7,40},{8,39},{9,... | collective-permute-start | bytes 1572872 | tf_op jit(solution)/shard_map/ppermute | solution.py:216
  19.9 13.9 %collective-permute-start.5 = (f32[32,4096]{1,0:T(8,128)S(1)}, f32[32,4096]{1,0:T(8,128)}, u32[]{:S(2)}, u32[]{:S(2)}) collective-permute-start(f32[32,4096]{1,0:T(8,128)S(1)} %collective-permute-done.3.refs_0_), channel_id=1, source_target_pairs={{0,64},{1,65},{2,66},{3,67},{4,68},{5,69},{6,70},{7,71},{8,72},{9,... | collective-permute-start | bytes 1572872 | tf_op jit(solution)/shard_map/ppermute | solution.py:216
  21.2 21.6 %collective-permute-start.4 = (f32[32,4096]{1,0:T(8,128)}, f32[32,4096]{1,0:T(8,128)S(1)}, u32[]{:S(2)}, u32[]{:S(2)}) collective-permute-start(f32[32,4096]{1,0:T(8,128)} %get-tuple-element.64), channel_id=1, source_target_pairs={{0,32},{1,33},{2,34},{3,35},{4,36},{5,37},{6,38},{7,39},{8,40},{9,... | collective-permute-start | bytes 1572872 | tf_op jit(solution)/shard_map/ppermute | solution.py:216
  29.2 15.9 %collective-permute-start.8 = (f32[32,4096]{1,0:T(8,128)}, f32[32,4096]{1,0:T(8,128)S(1)}, u32[]{:S(2)}, u32[]{:S(2)}) collective-permute-start(f32[32,4096]{1,0:T(8,128)} %collective-permute-done.refs_0_), channel_id=1, source_target_pairs={{0,63},{1,34},{2,33},{3,36},{4,35},{5,38},{6,37},{7,40},{8,39},{9,... | collective-permute-start | bytes 1572872 | tf_op jit(solution)/shard_map/ppermute | solution.py:216
  31.2 16.3 %collective-permute-start.7 = (f32[32,4096]{1,0:T(8,128)}, f32[32,4096]{1,0:T(8,128)S(1)}, u32[]{:S(2)}, u32[]{:S(2)}) collective-permute-start(f32[32,4096]{1,0:T(8,128)} %collective-permute-done.refs_0_), channel_id=1, source_target_pairs={{0,64},{1,65},{2,66},{3,67},{4,68},{5,69},{6,70},{7,71},{8,72},{9,... | collective-permute-start | bytes 1572872 | tf_op jit(solution)/shard_map/ppermute | solution.py:216
  33.7 18.5 %collective-permute-start.2 = (f32[32,4096]{1,0:T(8,128)}, f32[32,4096]{1,0:T(8,128)S(1)}, u32[]{:S(2)}, u32[]{:S(2)}) collective-permute-start(f32[32,4096]{1,0:T(8,128)} %get-tuple-element.61), channel_id=1, source_target_pairs={{0,32},{1,33},{2,34},{3,35},{4,36},{5,37},{6,38},{7,39},{8,40},{9,... | collective-permute-start | bytes 1572872 | tf_op jit(solution)/shard_map/ppermute | solution.py:216
  36.3 8.9 %copy-start.13 = (f32[32,4096]{1,0:T(8,128)S(1)}, f32[32,4096]{1,0:T(8,128)}, u32[]{:S(2)}) copy-start(f32[32,4096]{1,0:T(8,128)} %get-tuple-element.78) | copy-start | bytes 1572868
  36.3 11.1 %copy-start.9 = (f32[1,96]{1,0:T(1,128)S(1)}, f32[1,96]{1,0:T(1,128)}, u32[]{:S(2)}) copy-start(f32[1,96]{1,0:T(1,128)} %get-tuple-element.107) | copy-start | bytes 1156
  42.7 12.9 %collective-permute-start.12 = (f32[32,4096]{1,0:T(8,128)S(1)}, f32[32,4096]{1,0:T(8,128)S(1)}, u32[]{:S(2)}, u32[]{:S(2)}) collective-permute-start(f32[32,4096]{1,0:T(8,128)S(1)} %collective-permute-done.4.refs_0_), channel_id=1, source_target_pairs={{0,63},{1,34},{2,33},{3,36},{4,35},{5,38},{6,37},{7,40},{8,39},{9,... | collective-permute-start | bytes 1572872 | tf_op jit(solution)/shard_map/ppermute | solution.py:216
  43.9 11.7 %collective-permute-start.11 = (f32[32,4096]{1,0:T(8,128)S(1)}, f32[32,4096]{1,0:T(8,128)S(1)}, u32[]{:S(2)}, u32[]{:S(2)}) collective-permute-start(f32[32,4096]{1,0:T(8,128)S(1)} %collective-permute-done.4.refs_0_), channel_id=1, source_target_pairs={{0,64},{1,65},{2,66},{3,67},{4,68},{5,69},{6,70},{7,71},{8,72},{9,... | collective-permute-start | bytes 1572872 | tf_op jit(solution)/shard_map/ppermute | solution.py:216
  45.2 17.5 %collective-permute-start.10 = (f32[32,4096]{1,0:T(8,128)S(1)}, f32[32,4096]{1,0:T(8,128)S(1)}, u32[]{:S(2)}, u32[]{:S(2)}) collective-permute-start(f32[32,4096]{1,0:T(8,128)S(1)} %copy-done.13), channel_id=1, source_target_pairs={{0,32},{1,33},{2,34},{3,35},{4,36},{5,37},{6,38},{7,39},{8,40},{9,... | collective-permute-start | bytes 1572872 | tf_op jit(solution)/shard_map/ppermute | solution.py:216
  47.5 8.1 %copy-start.12 = (f32[32,4096]{1,0:T(8,128)S(1)}, f32[32,4096]{1,0:T(8,128)}, u32[]{:S(2)}) copy-start(f32[32,4096]{1,0:T(8,128)} %get-tuple-element.76) | copy-start | bytes 1572868
  52.3 18.4 %collective-permute-start.14 = (f32[32,4096]{1,0:T(8,128)S(1)}, f32[32,4096]{1,0:T(8,128)S(1)}, u32[]{:S(2)}, u32[]{:S(2)}) collective-permute-start(f32[32,4096]{1,0:T(8,128)S(1)} %collective-permute-done.2.refs_0_), channel_id=1, source_target_pairs={{0,63},{1,34},{2,33},{3,36},{4,35},{5,38},{6,37},{7,40},{8,39},{9,... | collective-permute-start | bytes 1572872 | tf_op jit(solution)/shard_map/ppermute | solution.py:216
  53.6 19.0 %collective-permute-start.13 = (f32[32,4096]{1,0:T(8,128)S(1)}, f32[32,4096]{1,0:T(8,128)S(1)}, u32[]{:S(2)}, u32[]{:S(2)}) collective-permute-start(f32[32,4096]{1,0:T(8,128)S(1)} %collective-permute-done.2.refs_0_), channel_id=1, source_target_pairs={{0,64},{1,65},{2,66},{3,67},{4,68},{5,69},{6,70},{7,71},{8,72},{9,... | collective-permute-start | bytes 1572872 | tf_op jit(solution)/shard_map/ppermute | solution.py:216
  55.6 15.0 %copy-start.7 = (f32[1,96]{1,0:T(1,128)S(1)}, f32[1,96]{1,0:T(1,128)}, u32[]{:S(2)}) copy-start(f32[1,96]{1,0:T(1,128)} %get-tuple-element.105) | copy-start | bytes 1156
  55.6 15.1 %copy-start.11 = (f32[32,4096]{1,0:T(8,128)S(1)}, f32[32,4096]{1,0:T(8,128)}, u32[]{:S(2)}) copy-start(f32[32,4096]{1,0:T(8,128)} %get-tuple-element.89) | copy-start | bytes 1572868
  55.6 20.6 %collective-permute-start.9 = (f32[32,4096]{1,0:T(8,128)S(1)}, f32[32,4096]{1,0:T(8,128)S(1)}, u32[]{:S(2)}, u32[]{:S(2)}) collective-permute-start(f32[32,4096]{1,0:T(8,128)S(1)} %copy-done.12), channel_id=1, source_target_pairs={{0,32},{1,33},{2,34},{3,35},{4,36},{5,37},{6,38},{7,39},{8,40},{9,... | collective-permute-start | bytes 1572872 | tf_op jit(solution)/shard_map/ppermute | solution.py:216
  62.6 21.1 %collective-permute-start.18 = (f32[32,4096]{1,0:T(8,128)S(1)}, f32[32,4096]{1,0:T(8,128)S(1)}, u32[]{:S(2)}, u32[]{:S(2)}) collective-permute-start(f32[32,4096]{1,0:T(8,128)S(1)} %collective-permute-done.10.refs_0_), channel_id=1, source_target_pairs={{0,63},{1,34},{2,33},{3,36},{4,35},{5,38},{6,37},{7,40},{8,39},{9,... | collective-permute-start | bytes 1572872 | tf_op jit(solution)/shard_map/ppermute | solution.py:216
  65.1 19.8 %collective-permute-start.17 = (f32[32,4096]{1,0:T(8,128)S(1)}, f32[32,4096]{1,0:T(8,128)S(1)}, u32[]{:S(2)}, u32[]{:S(2)}) collective-permute-start(f32[32,4096]{1,0:T(8,128)S(1)} %collective-permute-done.10.refs_0_), channel_id=1, source_target_pairs={{0,64},{1,65},{2,66},{3,67},{4,68},{5,69},{6,70},{7,71},{8,72},{9,... | collective-permute-start | bytes 1572872 | tf_op jit(solution)/shard_map/ppermute | solution.py:216
  70.7 13.0 %copy-start.10 = (f32[32,4096]{1,0:T(8,128)S(1)}, f32[32,4096]{1,0:T(8,128)}, u32[]{:S(2)}) copy-start(f32[32,4096]{1,0:T(8,128)} %get-tuple-element.87) | copy-start | bytes 1572868
  70.7 14.2 %copy-start.6 = (f32[1,96]{1,0:T(1,128)S(1)}, f32[1,96]{1,0:T(1,128)}, u32[]{:S(2)}) copy-start(f32[1,96]{1,0:T(1,128)} %get-tuple-element.104) | copy-start | bytes 1156
  70.7 17.9 %collective-permute-start.16 = (f32[32,4096]{1,0:T(8,128)S(1)}, f32[32,4096]{1,0:T(8,128)S(1)}, u32[]{:S(2)}, u32[]{:S(2)}) collective-permute-start(f32[32,4096]{1,0:T(8,128)S(1)} %copy-done.11), channel_id=1, source_target_pairs={{0,32},{1,33},{2,34},{3,35},{4,36},{5,37},{6,38},{7,39},{8,40},{9,... | collective-permute-start | bytes 1572872 | tf_op jit(solution)/shard_map/ppermute | solution.py:216
  76.2 18.7 %collective-permute-start.20 = (f32[32,4096]{1,0:T(8,128)S(1)}, f32[32,4096]{1,0:T(8,128)S(1)}, u32[]{:S(2)}, u32[]{:S(2)}) collective-permute-start(f32[32,4096]{1,0:T(8,128)S(1)} %collective-permute-done.9.refs_0_), channel_id=1, source_target_pairs={{0,63},{1,34},{2,33},{3,36},{4,35},{5,38},{6,37},{7,40},{8,39},{9,... | collective-permute-start | bytes 1572872 | tf_op jit(solution)/shard_map/ppermute | solution.py:216
  76.4 18.5 %collective-permute-start.19 = (f32[32,4096]{1,0:T(8,128)S(1)}, f32[32,4096]{1,0:T(8,128)S(1)}, u32[]{:S(2)}, u32[]{:S(2)}) collective-permute-start(f32[32,4096]{1,0:T(8,128)S(1)} %collective-permute-done.9.refs_0_), channel_id=1, source_target_pairs={{0,64},{1,65},{2,66},{3,67},{4,68},{5,69},{6,70},{7,71},{8,72},{9,... | collective-permute-start | bytes 1572872 | tf_op jit(solution)/shard_map/ppermute | solution.py:216
  83.7 14.9 %collective-permute-start.15 = (f32[32,4096]{1,0:T(8,128)S(1)}, f32[32,4096]{1,0:T(8,128)S(1)}, u32[]{:S(2)}, u32[]{:S(2)}) collective-permute-start(f32[32,4096]{1,0:T(8,128)S(1)} %copy-done.10), channel_id=1, source_target_pairs={{0,32},{1,33},{2,34},{3,35},{4,36},{5,37},{6,38},{7,39},{8,40},{9,... | collective-permute-start | bytes 1572872 | tf_op jit(solution)/shard_map/ppermute | solution.py:216
  88.6 16.8 %collective-permute-start.24 = (f32[32,4096]{1,0:T(8,128)S(1)}, f32[32,4096]{1,0:T(8,128)S(1)}, u32[]{:S(2)}, u32[]{:S(2)}) collective-permute-start(f32[32,4096]{1,0:T(8,128)S(1)} %collective-permute-done.16.refs_0_), channel_id=1, source_target_pairs={{0,63},{1,34},{2,33},{3,36},{4,35},{5,38},{6,37},{7,40},{8,39},{9,... | collective-permute-start | bytes 1572872 | tf_op jit(solution)/shard_map/ppermute | solution.py:216
  92.1 15.5 %collective-permute-start.23 = (f32[32,4096]{1,0:T(8,128)S(1)}, f32[32,4096]{1,0:T(8,128)S(1)}, u32[]{:S(2)}, u32[]{:S(2)}) collective-permute-start(f32[32,4096]{1,0:T(8,128)S(1)} %collective-permute-done.16.refs_0_), channel_id=1, source_target_pairs={{0,64},{1,65},{2,66},{3,67},{4,68},{5,69},{6,70},{7,71},{8,72},{9,... | collective-permute-start | bytes 1572872 | tf_op jit(solution)/shard_map/ppermute | solution.py:216
  98.6 19.3 %collective-permute-start.21 = (f32[32,4096]{1,0:T(8,128)S(1)}, f32[32,4096]{1,0:T(8,128)S(1)}, u32[]{:S(2)}, u32[]{:S(2)}) collective-permute-start(f32[32,4096]{1,0:T(8,128)S(1)} %collective-permute-done.15.refs_0_), channel_id=1, source_target_pairs={{0,64},{1,65},{2,66},{3,67},{4,68},{5,69},{6,70},{7,71},{8,72},{9,... | collective-permute-start | bytes 1572872 | tf_op jit(solution)/shard_map/ppermute | solution.py:216
  99.7 18.2 %collective-permute-start.22 = (f32[32,4096]{1,0:T(8,128)S(1)}, f32[32,4096]{1,0:T(8,128)S(1)}, u32[]{:S(2)}, u32[]{:S(2)}) collective-permute-start(f32[32,4096]{1,0:T(8,128)S(1)} %collective-permute-done.15.refs_0_), channel_id=1, source_target_pairs={{0,63},{1,34},{2,33},{3,36},{4,35},{5,38},{6,37},{7,40},{8,39},{9,... | collective-permute-start | bytes 1572872 | tf_op jit(solution)/shard_map/ppermute | solution.py:216
  (7 other events, 39.3 us)

commit v2 on v0

v2 whole, which is shorter than its diff:
```python
import functools
import jax
import jax.numpy as jnp
from jax import lax
from jax.experimental import pallas as pl
from jax.experimental.pallas import tpu as pltpu
from jax.sharding import PartitionSpec as P

AXES = ("occ", "vir")
PANEL = 1024
NT = (((1,), (1,)), ((), ()))
NN = (((1,), (0,)), ((), ()))


def mxu(left, right, dims=NN):
    return lax.dot_general(left, right, dims, preferred_element_type=jnp.float32)


def halves(value):
    high = value.astype(jnp.bfloat16)
    low = (value - high.astype(jnp.float32)).astype(jnp.bfloat16)
    return high, low


def panels(width):
    return [slice(at, at + PANEL) for at in range(0, width, PANEL)]


def fetch(source_ref, target_ref, sem):
    copy = pltpu.make_async_copy(source_ref, target_ref, sem)
    copy.start()
    return copy


def row_cuts(mine_ref, targets, starts, sem):
    copies = []
    for at, (target, start) in enumerate(zip(targets, starts)):
        rows = pl.ds(start, target.shape[0])
        copies.append(fetch(mine_ref.at[rows], target, sem.at[at]))
    return copies


def cut_kernel(starts, mine_ref, *refs):
    for copy in row_cuts(mine_ref, refs[:-1], starts, refs[-1]):
        copy.wait()


def over_panels(width, body, start):
    def turn(at, state):
        return body(at, pl.ds(pl.multiple_of(at * PANEL, PANEL), PANEL), state)

    return lax.fori_loop(0, width // PANEL, turn, start)


def own_kernel(starts, mine_ref, gap_row_ref, gap_col_ref, *refs):
    high_ref, low_ref, a_high_ref, a_low_ref, *parts, stage_ref, panel_sem, part_sem = refs
    rows, width = mine_ref.shape
    for at, cols in enumerate(panels(width)):
        fetch(mine_ref.at[:, cols], stage_ref.at[:, cols], panel_sem.at[at])

    def body(at, cols, state):
        integral, cross = state
        pltpu.make_async_copy(mine_ref.at[:, cols], stage_ref.at[:, cols], panel_sem.at[at]).wait()
        high, low = halves(stage_ref[:, cols])
        high_ref[:, cols] = high
        low_ref[:, cols] = low
        return integral + mxu(high, high, NT), cross + mxu(high, low, NT)

    zero = jnp.zeros((rows, rows), jnp.float32)
    integral, cross = over_panels(width, body, (zero, zero))
    cuts = row_cuts(stage_ref, parts, starts, part_sem)
    integral = integral + (cross + cross.T)
    a_high, a_low = halves(integral / (gap_row_ref[...] + gap_col_ref[...]))
    a_high_ref[...] = a_high
    a_low_ref[...] = a_low
    for copy in cuts:
        copy.wait()


def step_kernel(plan, *refs):
    count, own, inner_rows, gaps, final = plan
    refs = list(refs)
    take = lambda number: [refs.pop(0) for _ in range(number)]
    others = take(count)
    high_ref, low_ref, gap_row_ref, table_ref = take(4)
    a_own = take(2) if own else None
    start_ref = None if own else take(1)[0]
    inner_ref = take(1)[0] if inner_rows else None
    gamma_ref, both_ref = take(2)
    if inner_rows:
        inner_stage_ref, inner_sem = take(2)
        at, height = inner_rows
        fetch(inner_ref.at[pl.ds(at, height)], inner_stage_ref, inner_sem).wait()
        others.append(inner_stage_ref)
    rows, width = high_ref.shape
    extent = both_ref.shape[0] // 2

    def gather(at, cols, state):
        main, rest = state
        high, low = halves(jnp.concatenate([ref[:, cols] for ref in others], axis=0))
        both = jnp.concatenate([high, low], axis=0)
        both_ref[:, cols] = both
        return main + mxu(high_ref[:, cols], both, NT), rest + mxu(low_ref[:, cols], high, NT)

    start = (jnp.zeros((rows, 2 * extent), jnp.float32), jnp.zeros((rows, extent), jnp.float32))
    main, rest = over_panels(width, gather, start)
    integral = main[:, :extent] + (main[:, extent:] + rest)
    gap_col = jnp.concatenate(
        [table_ref[row : row + 1, at : at + height] for row, at, height in gaps], axis=1
    )
    a_high, a_low = halves(integral / (gap_row_ref[...] + gap_col))
    a_twice = jnp.concatenate([a_high, a_high], axis=1)

    def spread(at, cols, state):
        both = both_ref[:, cols]
        gamma = mxu(a_twice, both) + mxu(a_low, both[:extent])
        if own:
            high, low = high_ref[:, cols], low_ref[:, cols]
            a_high_own, a_low_own = a_own[0][...], a_own[1][...]
            gamma += mxu(a_high_own, high) + (mxu(a_high_own, low) + mxu(a_low_own, high))
        else:
            gamma += start_ref[:, cols]
        if final:
            stage_ref, sem = refs
            stage_ref[:, cols] = gamma
            fetch(stage_ref.at[:, cols], gamma_ref.at[:, cols], sem.at[at])
        else:
            gamma_ref[:, cols] = gamma
        return state

    over_panels(width, spread, 0)
    if final:
        stage_ref, sem = refs
        for at, cols in enumerate(panels(width)):
            pltpu.make_async_copy(stage_ref.at[:, cols], gamma_ref.at[:, cols], sem.at[at]).wait()


VMEM = pl.BlockSpec(memory_space=pltpu.VMEM)
HBM = pl.BlockSpec(memory_space=pltpu.HBM)


def cost(rows, extent, width):
    return pl.CostEstimate(flops=12 * rows * extent * width, bytes_accessed=4 * extent * width, transcendentals=0)


def in_vmem(array):
    return pltpu.with_memory_space_constraint(array, pltpu.VMEM)


def in_hbm(array):
    return pltpu.with_memory_space_constraint(array, pltpu.HBM)


def params(mebibytes):
    return pltpu.CompilerParams(vmem_limit_bytes=mebibytes << 20)


def cut_call(mine, ranges):
    width = mine.shape[1]
    count = len(ranges)
    return pl.pallas_call(
        functools.partial(cut_kernel, [start for start, _ in ranges]),
        out_shape=tuple(pltpu.VMEM((height, width), jnp.float32) for _, height in ranges),
        in_specs=[HBM],
        out_specs=(VMEM,) * count,
        scratch_shapes=[pltpu.SemaphoreType.DMA((count,))],
        compiler_params=params(2),
        cost_estimate=pl.CostEstimate(flops=0, bytes_accessed=1 << 20, transcendentals=0),
        name="first_cuts",
    )(in_hbm(mine))


def own_call(mine, gap_row, gap_col, ranges):
    rows, width = mine.shape
    count = len(ranges)
    factor = pltpu.VMEM((rows, width), jnp.bfloat16)
    amplitude = pltpu.VMEM((rows, rows), jnp.bfloat16)
    return pl.pallas_call(
        functools.partial(own_kernel, [start for start, _ in ranges]),
        out_shape=(factor, factor, amplitude, amplitude)
        + tuple(pltpu.HBM((height, width), jnp.float32) for _, height in ranges),
        in_specs=[HBM, VMEM, VMEM],
        out_specs=(VMEM,) * 4 + (HBM,) * count,
        scratch_shapes=[
            pltpu.VMEM((rows, width), jnp.float32),
            pltpu.SemaphoreType.DMA((width // PANEL,)),
            pltpu.SemaphoreType.DMA((count,)),
        ],
        compiler_params=params(10),
        cost_estimate=cost(rows, rows, width),
        name="own_block",
    )(in_hbm(mine), gap_row, gap_col)


def step_call(others, high, low, gap_row, table, gaps, begin, inner, inner_rows, final, name):
    rows, width = high.shape
    own = len(begin) == 2
    extent = sum(other.shape[0] for other in others)
    scratch = []
    if inner_rows:
        extent += inner_rows[1]
        scratch += [pltpu.VMEM((inner_rows[1], width), jnp.float32), pltpu.SemaphoreType.DMA]
    if final:
        scratch += [pltpu.VMEM((rows, width), jnp.float32), pltpu.SemaphoreType.DMA((width // PANEL,))]
    extra = [in_hbm(inner)] if inner_rows else []
    return pl.pallas_call(
        functools.partial(step_kernel, (len(others), own, inner_rows, gaps, final)),
        out_shape=(pltpu.HBM if final else pltpu.VMEM)((rows, width), jnp.float32),
        in_specs=[VMEM] * (len(others) + 4 + len(begin)) + [HBM] * len(extra),
        out_specs=HBM if final else VMEM,
        scratch_shapes=[pltpu.VMEM((2 * extent, width), jnp.bfloat16)] + scratch,
        input_output_aliases={} if final or own else {len(others) + 4: 0},
        compiler_params=params(10),
        cost_estimate=pl.CostEstimate(flops=1 << 20, bytes_accessed=1 << 16, transcendentals=0),
        name=name,
    )(*map(in_vmem, others), in_vmem(high), in_vmem(low), gap_row, table, *map(in_vmem, begin), *extra)


def local(b_factors, occ_energy, vir_energy):
    occ_block, vir_block, width = b_factors.shape
    occ_count = lax.axis_size("occ")
    vir_count = lax.axis_size("vir")
    occ_here = lax.axis_index("occ")
    vir_here = lax.axis_index("vir")

    def moved(block, target):
        route = []
        for occ in range(occ_count):
            for vir in range(vir_count):
                occ_to, vir_to = target(occ, vir)
                route.append(
                    (occ * vir_count + vir, occ_to % occ_count * vir_count + vir_to % vir_count)
                )
        return lax.ppermute(block, AXES, route)

    def across(occ, vir):
        return occ ^ 1, vir

    def back(occ, vir):
        return (occ + 2 if occ % 2 else occ - 2), vir

    def along(occ, vir):
        return (occ - 2 if occ % 2 else occ + 2), vir

    def outward(occ, vir):
        return occ ^ 1, (vir + 1 if vir % 2 else vir - 1)

    def inward(occ, vir):
        return occ, vir ^ 1

    def gap_of(occ_place, vir_place):
        occ_part = lax.dynamic_slice_in_dim(
            occ_energy, occ_place % occ_count * occ_block, occ_block
        )
        vir_part = lax.dynamic_slice_in_dim(
            vir_energy, vir_place % vir_count * vir_block, vir_block
        )
        return occ_part[:, None] - vir_part[None, :]

    occ_side = 1 - 2 * (occ_here % 2)
    vir_side = 1 - 2 * (vir_here % 2)
    gap = gap_of(occ_here, vir_here)
    gap_inner = gap_of(occ_here, vir_here + vir_side)
    gap_near = gap_of(occ_here + occ_side, vir_here)
    gap_far = gap_of(occ_here + occ_count - occ_side, vir_here)
    gap_outer = gap_of(occ_here, vir_here + vir_count - vir_side)
    gap_row = gap.reshape(-1, 1)
    table = jnp.concatenate([gap_near, gap_far, gap_outer, gap_inner], axis=1)

    def held(value, *earlier):
        return lax.optimization_barrier((value, earlier))[0]

    mine = b_factors.reshape(occ_block * vir_block, width)
    size = mine.shape[0]
    early = vir_block // 2
    count = occ_block
    ranges = [(k * vir_block, vir_block) for k in range(count)]

    first, ahead = cut_call(mine, [ranges[0], (size - early, early)])
    parts = [first]
    near = [moved(first, across)]
    inner = moved(held(b_factors, first), inward).reshape(size, width)
    ahead_back, ahead_out = moved(ahead, back), moved(ahead, outward)
    high, low, a_high, a_low, *rest = own_call(held(mine, first), gap_row, gap.reshape(1, -1), ranges[1:])
    parts += rest
    near.append(moved(held(parts[1], ahead_back, ahead_out), across))

    done = [a_high, a_high]
    far, outer = [], []
    begin = [a_high, a_low]
    inner_at = 0

    def step(k, *earlier):
        nonlocal begin, inner_at
        final = k == count - 1
        others = [near[k], far[k], outer[k]]
        rows = None
        if final:
            others.append(late)
            at = vir_block - early
            gaps = [(k, 0, vir_block)]
            gaps += [(k, which * vir_block + shift, early) for shift in (0, at) for which in (1, 2)]
        else:
            others = [held(other, *earlier) for other in others]
            height = vir_block if k < count - 2 else size - inner_at
            rows = (inner_at, height)
            gaps = [(k, 0, 3 * vir_block)]
            gaps += [(row, 3 * vir_block, vir_block) for row in range(inner_at // vir_block, (inner_at + height) // vir_block)]
            inner_at += height
        gamma = step_call(others, high, low, gap_row, table, gaps, begin, inner, rows, final, "step_%d" % k)
        begin = [gamma]
        done.append(gamma)
        return gamma

    late = None
    for k in range(count):
        part = held(near[k], done[k])
        if k == 0:
            part = held(part, inner)
        if k == count - 1:
            part = part[: vir_block - early]
        far.append(moved(part, along))
        outer.append(moved(part, outward))
        if k + 2 < count:
            near.append(moved(held(parts[k + 2], part), across))
        elif k + 2 == count:
            relayed = held(jnp.concatenate([ahead_back, ahead_out], axis=0), part, far[k - 1], outer[k - 1])
            late = moved(relayed, across)
        if k > 0:
            step(k - 1, part)
    gamma = step(count - 1)
    return gamma.reshape(occ_block, vir_block, width)


def solution(mesh):
    in_specs = (P("occ", "vir", None), P(), P())
    out_specs = P("occ", "vir", None)
    return jax.shard_map(local, mesh=mesh, in_specs=in_specs, out_specs=out_specs, check_vma=False)
```

time: 139 us -> 120 us (0.86)
  waiting for transfers between devices: 47.5 us -> 11.2 us
  starting transfers between devices: 42.4 us -> 57.7 us
  Pallas kernels: 42 us -> 49 us
  local copies, waits for them, and re-layouts: 4.94 us -> 1.2 us
    ppermute x25 -> x28, waiting for transfers between devices: 47.5 us -> 11.2 us  [moved(): return lax.ppermute(block, AXES, route)]
    ppermute x25 -> x28, starting transfers between devices: 42.4 us -> 57.7 us  [moved(): return lax.ppermute(block, AXES, route)]
    pallas_call x8, Pallas kernels: 34.8 us -> 43.1 us  [step_call(): pl.pallas_call(functools.partial(step_kernel, (len(others), own, inner_ro...]
    unnamed x24 -> x10, local copies, waits for them, and re-layouts: 2.94 us -> 0.02 us
  transfers between devices with their start and end apart: 25 -> 28, of which waited for: 7 -> 6; matrix products, arithmetic and copies ran while one was open for 2% -> 1% of each run, Pallas kernels for 26% -> 36%
where the time goes in v2:
time: 120 us
  starting transfers between devices  57.7 us (48%)
  Pallas kernels  49 us (41%)
  waiting for transfers between devices  11.2 us (9%)
  local copies, waits for them, and re-layouts  1.2 us (1%)
    ppermute x28, starting transfers between devices, moved(): return lax.ppermute(block, AXES, route)  57.7 us
    pallas_call x8, Pallas kernels, step_call(): pl.pallas_call(functools.partial(step_kernel, (len(others), own, inner_ro...  43.1 us
    ppermute x28, waiting for transfers between devices, moved(): return lax.ppermute(block, AXES, route)  11.2 us
    pallas_call x1, Pallas kernels, own_call(): pl.pallas_call(functools.partial(own_kernel, [start for start, _ in range...  4.82 us
  transfers between devices with their start and end apart: 28, of which 6 were waited for; matrix products, arithmetic and copies ran while one was open for 1% of the time, Pallas kernels for 36%

profile of v2, /device:TPU:1, one launch (start us, length us, event | category | flops | bytes accessed | tf_op | source)
XLA Modules:
  0.0 119.7 jit_solution(9068481448474324779)
XLA Ops:
  1.1 3.3 %collective-permute-start.5 = (f32[8,32,4096]{2,1,0:T(8,128)}, f32[8,32,4096]{2,1,0:T(8,128)}, u32[]{:S(2)}, u32[]{:S(2)}) collective-permute-start(f32[8,32,4096]{2,1,0:T(8,128)} %param.3), channel_id=1, source_target_pairs={{0,1},{1,0},{2,3},{3,2},{4,5},{5,4},{6,7},{7,6},{8,9},{9,8},{10,11... | collective-permute-start | bytes 12582920 | tf_op jit(solution)/shard_map/ppermute | solution.py:234
  4.5 2.2 %collective-permute-start = (f32[16,4096]{1,0:T(8,128)S(1)}, f32[16,4096]{1,0:T(8,128)S(1)}, u32[]{:S(2)}, u32[]{:S(2)}) collective-permute-start(f32[16,4096]{1,0:T(8,128)S(1)} %get-tuple-element.64), channel_id=1, source_target_pairs={{0,192},{1,193},{2,194},{3,195},{4,196},{5,197},{6,198},{7,199},{8... | collective-permute-start | bytes 786440 | tf_op jit(solution)/shard_map/ppermute | solution.py:234
  8.9 4.8 %own_block.1 = (bf16[256,4096]{1,0:T(8,128)(2,1)S(1)}, bf16[256,4096]{1,0:T(8,128)(2,1)S(1)}, bf16[256,256]{1,0:T(8,128)(2,1)S(1)}, bf16[256,256]{1,0:T(8,128)(2...) custom-call(f32[256,4096]{1,0:T(8,128)} %bitcast.mine_ref, ...), custom_call_target="tpu_custom_call" | custom-call | flops 3221225472 | bytes 4194304 | tf_op jit(solution)/shard_map/own_block/pallas_call | solution.py:178
  13.7 2.8 %collective-permute-done.1 = f32[16,4096]{1,0:T(8,128)S(1)} collective-permute-done((f32[16,4096]{1,0:T(8,128)S(1)}, f32[16,4096]{1,0:T(8,128)S(1)}, u32[]{:S(2)}, u32[]{:S(2)}) %collective-permute-start.1) | collective-permute-done | bytes 262176 | tf_op jit(solution)/shard_map/ppermute | solution.py:234
  16.5 1.4 %collective-permute-done.4.refs_0_ = f32[32,4096]{1,0:T(8,128)S(1)} collective-permute-done((f32[32,4096]{1,0:T(8,128)S(1)}, f32[32,4096]{1,0:T(8,128)S(1)}, u32[]{:S(2)}, u32[]{:S(2)}) %collective-permute-start.4) | collective-permute-done | bytes 524320 | tf_op jit(solution)/shard_map/ppermute | solution.py:234
  18.0 1.5 %collective-permute-start.8 = (f32[32,4096]{1,0:T(8,128)S(1)}, f32[32,4096]{1,0:T(8,128)S(1)}, u32[]{:S(2)}, u32[]{:S(2)}) collective-permute-start(f32[32,4096]{1,0:T(8,128)S(1)} %collective-permute-done.4.refs_0_), channel_id=1, source_target_pairs={{0,63},{1,34},{2,33},{3,36},{4,35},{5,38},{6,37},{7,40},{8,39},{9,... | collective-permute-start | bytes 1572872 | tf_op jit(solution)/shard_map/ppermute | solution.py:234
  19.5 1.8 %collective-permute-start.7 = (f32[32,4096]{1,0:T(8,128)S(1)}, f32[32,4096]{1,0:T(8,128)S(1)}, u32[]{:S(2)}, u32[]{:S(2)}) collective-permute-start(f32[32,4096]{1,0:T(8,128)S(1)} %collective-permute-done.4.refs_0_), channel_id=1, source_target_pairs={{0,64},{1,65},{2,66},{3,67},{4,68},{5,69},{6,70},{7,71},{8,72},{9,... | collective-permute-start | bytes 1572872 | tf_op jit(solution)/shard_map/ppermute | solution.py:234
  21.2 1.4 %collective-permute-start.6 = (f32[32,4096]{1,0:T(8,128)}, f32[32,4096]{1,0:T(8,128)S(1)}, u32[]{:S(2)}, u32[]{:S(2)}) collective-permute-start(f32[32,4096]{1,0:T(8,128)} %get-tuple-element.73), channel_id=1, source_target_pairs={{0,32},{1,33},{2,34},{3,35},{4,36},{5,37},{6,38},{7,39},{8,40},{9,... | collective-permute-start | bytes 1572872 | tf_op jit(solution)/shard_map/ppermute | solution.py:234
  22.6 5.1 %collective-permute-done.2.refs_0_ = f32[32,4096]{1,0:T(8,128)S(1)} collective-permute-done((f32[32,4096]{1,0:T(8,128)}, f32[32,4096]{1,0:T(8,128)S(1)}, u32[]{:S(2)}, u32[]{:S(2)}) %collective-permute-start.2) | collective-permute-done | bytes 524320 | tf_op jit(solution)/shard_map/ppermute | solution.py:234
  27.7 4.7 %collective-permute-start.10 = (f32[32,4096]{1,0:T(8,128)S(1)}, f32[32,4096]{1,0:T(8,128)S(1)}, u32[]{:S(2)}, u32[]{:S(2)}) collective-permute-start(f32[32,4096]{1,0:T(8,128)S(1)} %collective-permute-done.2.refs_0_), channel_id=1, source_target_pairs={{0,63},{1,34},{2,33},{3,36},{4,35},{5,38},{6,37},{7,40},{8,39},{9,... | collective-permute-start | bytes 1572872 | tf_op jit(solution)/shard_map/ppermute | solution.py:234
  32.4 1.4 %collective-permute-start.9 = (f32[32,4096]{1,0:T(8,128)S(1)}, f32[32,4096]{1,0:T(8,128)S(1)}, u32[]{:S(2)}, u32[]{:S(2)}) collective-permute-start(f32[32,4096]{1,0:T(8,128)S(1)} %collective-permute-done.2.refs_0_), channel_id=1, source_target_pairs={{0,64},{1,65},{2,66},{3,67},{4,68},{5,69},{6,70},{7,71},{8,72},{9,... | collective-permute-start | bytes 1572872 | tf_op jit(solution)/shard_map/ppermute | solution.py:234
  33.9 6.6 %step_0.1.refs_7_ = f32[256,4096]{1,0:T(8,128)S(1)} custom-call(f32[32,4096]{1,0:T(8,128)S(1)} %collective-permute-done.4.refs_0_, f32[32,4096]{1,0:T(8,128)S(1)} %collective-permute-done.7.refs_1_, f32[32,4096]{1,0:T(8,128)S(1)} %collective-permute-done.8.refs_2_, bf16[256,4096]{1,0:T(8,128)(2,1)S(1)} %get-tuple-element.77.refs_3_.refs_4_, ...), custom_call_target="tpu_custom_call" | custom-call | flops 1048576 | bytes 65536 | tf_op jit(solution)/shard_map/step_0/pallas_call | solution.py:206
  40.5 3.1 %collective-permute-start.14 = (f32[32,4096]{1,0:T(8,128)S(1)}, f32[32,4096]{1,0:T(8,128)S(1)}, u32[]{:S(2)}, u32[]{:S(2)}) collective-permute-start(f32[32,4096]{1,0:T(8,128)S(1)} %collective-permute-done.6.refs_0_), channel_id=1, source_target_pairs={{0,63},{1,34},{2,33},{3,36},{4,35},{5,38},{6,37},{7,40},{8,39},{9,... | collective-permute-start | bytes 1572872 | tf_op jit(solution)/shard_map/ppermute | solution.py:234
  43.6 5.5 %collective-permute-start.13 = (f32[32,4096]{1,0:T(8,128)S(1)}, f32[32,4096]{1,0:T(8,128)S(1)}, u32[]{:S(2)}, u32[]{:S(2)}) collective-permute-start(f32[32,4096]{1,0:T(8,128)S(1)} %collective-permute-done.6.refs_0_), channel_id=1, source_target_pairs={{0,64},{1,65},{2,66},{3,67},{4,68},{5,69},{6,70},{7,71},{8,72},{9,... | collective-permute-start | bytes 1572872 | tf_op jit(solution)/shard_map/ppermute | solution.py:234
  49.2 5.0 %step_1.1.refs_7_ = f32[256,4096]{1,0:T(8,128)S(1)} custom-call(f32[32,4096]{1,0:T(8,128)S(1)} %collective-permute-done.2.refs_0_, f32[32,4096]{1,0:T(8,128)S(1)} %collective-permute-done.9.refs_1_, f32[32,4096]{1,0:T(8,128)S(1)} %collective-permute-done.10.refs_2_, ...), custom_call_target="tpu_custom_call", output_to_operand_aliasing={{}: (7, {})} | custom-call | flops 1048576 | bytes 65536 | tf_op jit(solution)/shard_map/step_1/pallas_call | solution.py:206
  54.2 2.6 %collective-permute-start.16 = (f32[32,4096]{1,0:T(8,128)S(1)}, f32[32,4096]{1,0:T(8,128)S(1)}, u32[]{:S(2)}, u32[]{:S(2)}) collective-permute-start(f32[32,4096]{1,0:T(8,128)S(1)} %collective-permute-done.3.refs_0_), channel_id=1, source_target_pairs={{0,63},{1,34},{2,33},{3,36},{4,35},{5,38},{6,37},{7,40},{8,39},{9,... | collective-permute-start | bytes 1572872 | tf_op jit(solution)/shard_map/ppermute | solution.py:234
  56.8 1.3 %collective-permute-start.15 = (f32[32,4096]{1,0:T(8,128)S(1)}, f32[32,4096]{1,0:T(8,128)S(1)}, u32[]{:S(2)}, u32[]{:S(2)}) collective-permute-start(f32[32,4096]{1,0:T(8,128)S(1)} %collective-permute-done.3.refs_0_), channel_id=1, source_target_pairs={{0,64},{1,65},{2,66},{3,67},{4,68},{5,69},{6,70},{7,71},{8,72},{9,... | collective-permute-start | bytes 1572872 | tf_op jit(solution)/shard_map/ppermute | solution.py:234
  58.1 3.5 %collective-permute-start.11 = (f32[32,4096]{1,0:T(8,128)S(1)}, f32[32,4096]{1,0:T(8,128)S(1)}, u32[]{:S(2)}, u32[]{:S(2)}) collective-permute-start(f32[32,4096]{1,0:T(8,128)S(1)} %copy-done.3), channel_id=1, source_target_pairs={{0,32},{1,33},{2,34},{3,35},{4,36},{5,37},{6,38},{7,39},{8,40},{9,... | collective-permute-start | bytes 1572872 | tf_op jit(solution)/shard_map/ppermute | solution.py:234
  61.6 5.0 %step_2.1.refs_7_ = f32[256,4096]{1,0:T(8,128)S(1)} custom-call(f32[32,4096]{1,0:T(8,128)S(1)} %collective-permute-done.6.refs_0_, f32[32,4096]{1,0:T(8,128)S(1)} %collective-permute-done.13.refs_1_, f32[32,4096]{1,0:T(8,128)S(1)} %collective-permute-done.14.refs_2_, ...), custom_call_target="tpu_custom_call", output_to_operand_aliasing={{}: (7, {})} | custom-call | flops 1048576 | bytes 65536 | tf_op jit(solution)/shard_map/step_2/pallas_call | solution.py:206
  66.7 3.4 %collective-permute-start.20 = (f32[32,4096]{1,0:T(8,128)S(1)}, f32[32,4096]{1,0:T(8,128)S(1)}, u32[]{:S(2)}, u32[]{:S(2)}) collective-permute-start(f32[32,4096]{1,0:T(8,128)S(1)} %collective-permute-done.12.refs_0_), channel_id=1, source_target_pairs={{0,63},{1,34},{2,33},{3,36},{4,35},{5,38},{6,37},{7,40},{8,39},{9,... | collective-permute-start | bytes 1572872 | tf_op jit(solution)/shard_map/ppermute | solution.py:234
  70.1 3.0 %collective-permute-start.19 = (f32[32,4096]{1,0:T(8,128)S(1)}, f32[32,4096]{1,0:T(8,128)S(1)}, u32[]{:S(2)}, u32[]{:S(2)}) collective-permute-start(f32[32,4096]{1,0:T(8,128)S(1)} %collective-permute-done.12.refs_0_), channel_id=1, source_target_pairs={{0,64},{1,65},{2,66},{3,67},{4,68},{5,69},{6,70},{7,71},{8,72},{9,... | collective-permute-start | bytes 1572872 | tf_op jit(solution)/shard_map/ppermute | solution.py:234
  73.2 5.0 %step_3.1.refs_7_ = f32[256,4096]{1,0:T(8,128)S(1)} custom-call(f32[32,4096]{1,0:T(8,128)S(1)} %collective-permute-done.3.refs_0_, f32[32,4096]{1,0:T(8,128)S(1)} %collective-permute-done.15.refs_1_, f32[32,4096]{1,0:T(8,128)S(1)} %collective-permute-done.16.refs_2_, ...), custom_call_target="tpu_custom_call", output_to_operand_aliasing={{}: (7, {})} | custom-call | flops 1048576 | bytes 65536 | tf_op jit(solution)/shard_map/step_3/pallas_call | solution.py:206
  78.2 3.6 %collective-permute-start.22 = (f32[32,4096]{1,0:T(8,128)S(1)}, f32[32,4096]{1,0:T(8,128)S(1)}, u32[]{:S(2)}, u32[]{:S(2)}) collective-permute-start(f32[32,4096]{1,0:T(8,128)S(1)} %collective-permute-done.11.refs_0_), channel_id=1, source_target_pairs={{0,63},{1,34},{2,33},{3,36},{4,35},{5,38},{6,37},{7,40},{8,39},{9,... | collective-permute-start | bytes 1572872 | tf_op jit(solution)/shard_map/ppermute | solution.py:234
  81.8 2.5 %collective-permute-start.21 = (f32[32,4096]{1,0:T(8,128)S(1)}, f32[32,4096]{1,0:T(8,128)S(1)}, u32[]{:S(2)}, u32[]{:S(2)}) collective-permute-start(f32[32,4096]{1,0:T(8,128)S(1)} %collective-permute-done.11.refs_0_), channel_id=1, source_target_pairs={{0,64},{1,65},{2,66},{3,67},{4,68},{5,69},{6,70},{7,71},{8,72},{9,... | collective-permute-start | bytes 1572872 | tf_op jit(solution)/shard_map/ppermute | solution.py:234
  85.2 5.0 %step_4.1.refs_7_ = f32[256,4096]{1,0:T(8,128)S(1)} custom-call(f32[32,4096]{1,0:T(8,128)S(1)} %collective-permute-done.12.refs_0_, f32[32,4096]{1,0:T(8,128)S(1)} %collective-permute-done.19.refs_1_, f32[32,4096]{1,0:T(8,128)S(1)} %collective-permute-done.20.refs_2_, ...), custom_call_target="tpu_custom_call", output_to_operand_aliasing={{}: (7, {})} | custom-call | flops 1048576 | bytes 65536 | tf_op jit(solution)/shard_map/step_4/pallas_call | solution.py:206
  90.1 2.7 %collective-permute-start.27 = (f32[32,4096]{1,0:T(8,128)S(1)}, f32[32,4096]{1,0:T(8,128)S(1)}, u32[]{:S(2)}, u32[]{:S(2)}) collective-permute-start(f32[32,4096]{1,0:T(8,128)S(1)} %collective-permute-done.18.refs_0_), channel_id=1, source_target_pairs={{0,63},{1,34},{2,33},{3,36},{4,35},{5,38},{6,37},{7,40},{8,39},{9,... | collective-permute-start | bytes 1572872 | tf_op jit(solution)/shard_map/ppermute | solution.py:234
  92.8 2.7 %collective-permute-start.26 = (f32[32,4096]{1,0:T(8,128)S(1)}, f32[32,4096]{1,0:T(8,128)S(1)}, u32[]{:S(2)}, u32[]{:S(2)}) collective-permute-start(f32[32,4096]{1,0:T(8,128)S(1)} %collective-permute-done.18.refs_0_), channel_id=1, source_target_pairs={{0,64},{1,65},{2,66},{3,67},{4,68},{5,69},{6,70},{7,71},{8,72},{9,... | collective-permute-start | bytes 1572872 | tf_op jit(solution)/shard_map/ppermute | solution.py:234
  96.6 3.3 %collective-permute-start.25 = (f32[32,4096]{1,0:T(8,128)S(1)}, f32[32,4096]{1,0:T(8,128)S(1)}, u32[]{:S(2)}, u32[]{:S(2)}) collective-permute-start(f32[32,4096]{1,0:T(8,128)S(1)} %pad_maximum_fusion), channel_id=1, source_target_pairs={{0,32},{1,33},{2,34},{3,35},{4,36},{5,37},{6,38},{7,39},{8,40},{9,... | collective-permute-start | bytes 1572872 | tf_op jit(solution)/shard_map/ppermute | solution.py:234
  99.9 5.0 %step_5.1.refs_7_ = f32[256,4096]{1,0:T(8,128)S(1)} custom-call(f32[32,4096]{1,0:T(8,128)S(1)} %collective-permute-done.11.refs_0_, f32[32,4096]{1,0:T(8,128)S(1)} %collective-permute-done.21.refs_1_, f32[32,4096]{1,0:T(8,128)S(1)} %collective-permute-done.22.refs_2_, ...), custom_call_target="tpu_custom_call", output_to_operand_aliasing={{}: (7, {})} | custom-call | flops 1048576 | bytes 65536 | tf_op jit(solution)/shard_map/step_5/pallas_call | solution.py:206
  104.9 1.5 %collective-permute-start.23 = (f32[16,4096]{1,0:T(8,128)S(1)}, f32[16,4096]{1,0:T(8,128)S(1)}, u32[]{:S(2)}, u32[]{:S(2)}) collective-permute-start(f32[16,4096]{1,0:T(8,128)S(1)} %slice.3), channel_id=1, source_target_pairs={{0,64},{1,65},{2,66},{3,67},{4,68},{5,69},{6,70},{7,71},{8,72},{9,... | collective-permute-start | bytes 786440 | tf_op jit(solution)/shard_map/ppermute | solution.py:234
  107.9 6.6 %step_6.1.refs_8_ = f32[256,4096]{1,0:T(8,128)S(1)} custom-call(f32[32,4096]{1,0:T(8,128)S(1)} %collective-permute-done.18.refs_0_, f32[32,4096]{1,0:T(8,128)S(1)} %collective-permute-done.26.refs_1_, f32[32,4096]{1,0:T(8,128)S(1)} %collective-permute-done.27.refs_2_, ...), custom_call_target="tpu_custom_call", output_to_operand_aliasing={{}: (7, {})} | custom-call | flops 1048576 | bytes 65536 | tf_op jit(solution)/shard_map/step_6/pallas_call | solution.py:206
  114.5 5.0 %step_7.1 = f32[256,4096]{1,0:T(8,128)} custom-call(f32[32,4096]{1,0:T(8,128)S(1)} %collective-permute-done.17.refs_0_, f32[16,4096]{1,0:T(8,128)S(1)} %collective-permute-done.23.refs_1_, f32[16,4096]{1,0:T(8,128)S(1)} %collective-permute-done.24.refs_2_, f32[32,4096]{1,0:T(8,128)S(1)} %collective-permute-done.25.refs_3_, ...), custom_call_target="tpu_custom_call" | custom-call | flops 1048576 | bytes 65536 | tf_op jit(solution)/shard_map/step_7/pallas_call | solution.py:206
  (52 shorter events, 7.2 us)
Async XLA Ops:
  1.1 16.8 %collective-permute-start.5 = (f32[8,32,4096]{2,1,0:T(8,128)}, f32[8,32,4096]{2,1,0:T(8,128)}, u32[]{:S(2)}, u32[]{:S(2)}) collective-permute-start(f32[8,32,4096]{2,1,0:T(8,128)} %param.3), channel_id=1, source_target_pairs={{0,1},{1,0},{2,3},{3,2},{4,5},{5,4},{6,7},{7,6},{8,9},{9,8},{10,11... | collective-permute-start | bytes 12582920 | tf_op jit(solution)/shard_map/ppermute | solution.py:234
  4.5 13.5 %collective-permute-start.4 = (f32[32,4096]{1,0:T(8,128)S(1)}, f32[32,4096]{1,0:T(8,128)S(1)}, u32[]{:S(2)}, u32[]{:S(2)}) collective-permute-start(f32[32,4096]{1,0:T(8,128)S(1)} %get-tuple-element.58), channel_id=1, source_target_pairs={{0,32},{1,33},{2,34},{3,35},{4,36},{5,37},{6,38},{7,39},{8,40},{9,... | collective-permute-start | bytes 1572872 | tf_op jit(solution)/shard_map/ppermute | solution.py:234
  4.5 9.2 %collective-permute-start = (f32[16,4096]{1,0:T(8,128)S(1)}, f32[16,4096]{1,0:T(8,128)S(1)}, u32[]{:S(2)}, u32[]{:S(2)}) collective-permute-start(f32[16,4096]{1,0:T(8,128)S(1)} %get-tuple-element.64), channel_id=1, source_target_pairs={{0,192},{1,193},{2,194},{3,195},{4,196},{5,197},{6,198},{7,199},{8... | collective-permute-start | bytes 786440 | tf_op jit(solution)/shard_map/ppermute | solution.py:234
  6.7 9.8 %collective-permute-start.1 = (f32[16,4096]{1,0:T(8,128)S(1)}, f32[16,4096]{1,0:T(8,128)S(1)}, u32[]{:S(2)}, u32[]{:S(2)}) collective-permute-start(f32[16,4096]{1,0:T(8,128)S(1)} %get-tuple-element.64), channel_id=1, source_target_pairs={{0,63},{1,34},{2,33},{3,36},{4,35},{5,38},{6,37},{7,40},{8,39},{9,... | collective-permute-start | bytes 786440 | tf_op jit(solution)/shard_map/ppermute | solution.py:234
  16.5 11.2 %collective-permute-start.2 = (f32[32,4096]{1,0:T(8,128)}, f32[32,4096]{1,0:T(8,128)S(1)}, u32[]{:S(2)}, u32[]{:S(2)}) collective-permute-start(f32[32,4096]{1,0:T(8,128)} %get-tuple-element.65), channel_id=1, source_target_pairs={{0,32},{1,33},{2,34},{3,35},{4,36},{5,37},{6,38},{7,39},{8,40},{9,... | collective-permute-start | bytes 1572872 | tf_op jit(solution)/shard_map/ppermute | solution.py:234
  18.0 15.8 %collective-permute-start.8 = (f32[32,4096]{1,0:T(8,128)S(1)}, f32[32,4096]{1,0:T(8,128)S(1)}, u32[]{:S(2)}, u32[]{:S(2)}) collective-permute-start(f32[32,4096]{1,0:T(8,128)S(1)} %collective-permute-done.4.refs_0_), channel_id=1, source_target_pairs={{0,63},{1,34},{2,33},{3,36},{4,35},{5,38},{6,37},{7,40},{8,39},{9,... | collective-permute-start | bytes 1572872 | tf_op jit(solution)/shard_map/ppermute | solution.py:234
  19.5 14.5 %collective-permute-start.7 = (f32[32,4096]{1,0:T(8,128)S(1)}, f32[32,4096]{1,0:T(8,128)S(1)}, u32[]{:S(2)}, u32[]{:S(2)}) collective-permute-start(f32[32,4096]{1,0:T(8,128)S(1)} %collective-permute-done.4.refs_0_), channel_id=1, source_target_pairs={{0,64},{1,65},{2,66},{3,67},{4,68},{5,69},{6,70},{7,71},{8,72},{9,... | collective-permute-start | bytes 1572872 | tf_op jit(solution)/shard_map/ppermute | solution.py:234
  21.2 19.3 %collective-permute-start.6 = (f32[32,4096]{1,0:T(8,128)}, f32[32,4096]{1,0:T(8,128)S(1)}, u32[]{:S(2)}, u32[]{:S(2)}) collective-permute-start(f32[32,4096]{1,0:T(8,128)} %get-tuple-element.73), channel_id=1, source_target_pairs={{0,32},{1,33},{2,34},{3,35},{4,36},{5,37},{6,38},{7,39},{8,40},{9,... | collective-permute-start | bytes 1572872 | tf_op jit(solution)/shard_map/ppermute | solution.py:234
  27.7 21.4 %collective-permute-start.10 = (f32[32,4096]{1,0:T(8,128)S(1)}, f32[32,4096]{1,0:T(8,128)S(1)}, u32[]{:S(2)}, u32[]{:S(2)}) collective-permute-start(f32[32,4096]{1,0:T(8,128)S(1)} %collective-permute-done.2.refs_0_), channel_id=1, source_target_pairs={{0,63},{1,34},{2,33},{3,36},{4,35},{5,38},{6,37},{7,40},{8,39},{9,... | collective-permute-start | bytes 1572872 | tf_op jit(solution)/shard_map/ppermute | solution.py:234
  32.4 16.8 %collective-permute-start.9 = (f32[32,4096]{1,0:T(8,128)S(1)}, f32[32,4096]{1,0:T(8,128)S(1)}, u32[]{:S(2)}, u32[]{:S(2)}) collective-permute-start(f32[32,4096]{1,0:T(8,128)S(1)} %collective-permute-done.2.refs_0_), channel_id=1, source_target_pairs={{0,64},{1,65},{2,66},{3,67},{4,68},{5,69},{6,70},{7,71},{8,72},{9,... | collective-permute-start | bytes 1572872 | tf_op jit(solution)/shard_map/ppermute | solution.py:234
  33.8 20.4 %collective-permute-start.3 = (f32[32,4096]{1,0:T(8,128)}, f32[32,4096]{1,0:T(8,128)S(1)}, u32[]{:S(2)}, u32[]{:S(2)}) collective-permute-start(f32[32,4096]{1,0:T(8,128)} %get-tuple-element.68), channel_id=1, source_target_pairs={{0,32},{1,33},{2,34},{3,35},{4,36},{5,37},{6,38},{7,39},{8,40},{9,... | collective-permute-start | bytes 1572872 | tf_op jit(solution)/shard_map/ppermute | solution.py:234
  33.9 15.1 %copy-start.4 = (f32[32,4096]{1,0:T(8,128)S(1)}, f32[32,4096]{1,0:T(8,128)}, u32[]{:S(2)}) copy-start(f32[32,4096]{1,0:T(8,128)} %get-tuple-element.87) | copy-start | bytes 1572868
  40.5 17.6 %collective-permute-start.14 = (f32[32,4096]{1,0:T(8,128)S(1)}, f32[32,4096]{1,0:T(8,128)S(1)}, u32[]{:S(2)}, u32[]{:S(2)}) collective-permute-start(f32[32,4096]{1,0:T(8,128)S(1)} %collective-permute-done.6.refs_0_), channel_id=1, source_target_pairs={{0,63},{1,34},{2,33},{3,36},{4,35},{5,38},{6,37},{7,40},{8,39},{9,... | collective-permute-start | bytes 1572872 | tf_op jit(solution)/shard_map/ppermute | solution.py:234
  43.6 18.0 %collective-permute-start.13 = (f32[32,4096]{1,0:T(8,128)S(1)}, f32[32,4096]{1,0:T(8,128)S(1)}, u32[]{:S(2)}, u32[]{:S(2)}) collective-permute-start(f32[32,4096]{1,0:T(8,128)S(1)} %collective-permute-done.6.refs_0_), channel_id=1, source_target_pairs={{0,64},{1,65},{2,66},{3,67},{4,68},{5,69},{6,70},{7,71},{8,72},{9,... | collective-permute-start | bytes 1572872 | tf_op jit(solution)/shard_map/ppermute | solution.py:234
  49.1 9.1 %copy-start.3 = (f32[32,4096]{1,0:T(8,128)S(1)}, f32[32,4096]{1,0:T(8,128)}, u32[]{:S(2)}) copy-start(f32[32,4096]{1,0:T(8,128)} %get-tuple-element.85) | copy-start | bytes 1572868
  49.1 17.6 %collective-permute-start.12 = (f32[32,4096]{1,0:T(8,128)S(1)}, f32[32,4096]{1,0:T(8,128)S(1)}, u32[]{:S(2)}, u32[]{:S(2)}) collective-permute-start(f32[32,4096]{1,0:T(8,128)S(1)} %copy-done.4), channel_id=1, source_target_pairs={{0,32},{1,33},{2,34},{3,35},{4,36},{5,37},{6,38},{7,39},{8,40},{9,... | collective-permute-start | bytes 1572872 | tf_op jit(solution)/shard_map/ppermute | solution.py:234
  54.2 18.8 %collective-permute-start.16 = (f32[32,4096]{1,0:T(8,128)S(1)}, f32[32,4096]{1,0:T(8,128)S(1)}, u32[]{:S(2)}, u32[]{:S(2)}) collective-permute-start(f32[32,4096]{1,0:T(8,128)S(1)} %collective-permute-done.3.refs_0_), channel_id=1, source_target_pairs={{0,63},{1,34},{2,33},{3,36},{4,35},{5,38},{6,37},{7,40},{8,39},{9,... | collective-permute-start | bytes 1572872 | tf_op jit(solution)/shard_map/ppermute | solution.py:234
  56.8 16.4 %collective-permute-start.15 = (f32[32,4096]{1,0:T(8,128)S(1)}, f32[32,4096]{1,0:T(8,128)S(1)}, u32[]{:S(2)}, u32[]{:S(2)}) collective-permute-start(f32[32,4096]{1,0:T(8,128)S(1)} %collective-permute-done.3.refs_0_), channel_id=1, source_target_pairs={{0,64},{1,65},{2,66},{3,67},{4,68},{5,69},{6,70},{7,71},{8,72},{9,... | collective-permute-start | bytes 1572872 | tf_op jit(solution)/shard_map/ppermute | solution.py:234
  58.1 15.0 %copy-start.2 = (f32[32,4096]{1,0:T(8,128)S(1)}, f32[32,4096]{1,0:T(8,128)}, u32[]{:S(2)}) copy-start(f32[32,4096]{1,0:T(8,128)} %get-tuple-element.98) | copy-start | bytes 1572868
  58.1 20.1 %collective-permute-start.11 = (f32[32,4096]{1,0:T(8,128)S(1)}, f32[32,4096]{1,0:T(8,128)S(1)}, u32[]{:S(2)}, u32[]{:S(2)}) collective-permute-start(f32[32,4096]{1,0:T(8,128)S(1)} %copy-done.3), channel_id=1, source_target_pairs={{0,32},{1,33},{2,34},{3,35},{4,36},{5,37},{6,38},{7,39},{8,40},{9,... | collective-permute-start | bytes 1572872 | tf_op jit(solution)/shard_map/ppermute | solution.py:234
  66.7 17.6 %collective-permute-start.20 = (f32[32,4096]{1,0:T(8,128)S(1)}, f32[32,4096]{1,0:T(8,128)S(1)}, u32[]{:S(2)}, u32[]{:S(2)}) collective-permute-start(f32[32,4096]{1,0:T(8,128)S(1)} %collective-permute-done.12.refs_0_), channel_id=1, source_target_pairs={{0,63},{1,34},{2,33},{3,36},{4,35},{5,38},{6,37},{7,40},{8,39},{9,... | collective-permute-start | bytes 1572872 | tf_op jit(solution)/shard_map/ppermute | solution.py:234
  70.1 15.1 %collective-permute-start.19 = (f32[32,4096]{1,0:T(8,128)S(1)}, f32[32,4096]{1,0:T(8,128)S(1)}, u32[]{:S(2)}, u32[]{:S(2)}) collective-permute-start(f32[32,4096]{1,0:T(8,128)S(1)} %collective-permute-done.12.refs_0_), channel_id=1, source_target_pairs={{0,64},{1,65},{2,66},{3,67},{4,68},{5,69},{6,70},{7,71},{8,72},{9,... | collective-permute-start | bytes 1572872 | tf_op jit(solution)/shard_map/ppermute | solution.py:234
  73.1 11.2 %copy-start.1 = (f32[32,4096]{1,0:T(8,128)S(1)}, f32[32,4096]{1,0:T(8,128)}, u32[]{:S(2)}) copy-start(f32[32,4096]{1,0:T(8,128)} %get-tuple-element.96) | copy-start | bytes 1572868
  73.1 17.0 %collective-permute-start.18 = (f32[32,4096]{1,0:T(8,128)S(1)}, f32[32,4096]{1,0:T(8,128)S(1)}, u32[]{:S(2)}, u32[]{:S(2)}) collective-permute-start(f32[32,4096]{1,0:T(8,128)S(1)} %copy-done.2), channel_id=1, source_target_pairs={{0,32},{1,33},{2,34},{3,35},{4,36},{5,37},{6,38},{7,39},{8,40},{9,... | collective-permute-start | bytes 1572872 | tf_op jit(solution)/shard_map/ppermute | solution.py:234
  78.2 17.3 %collective-permute-start.22 = (f32[32,4096]{1,0:T(8,128)S(1)}, f32[32,4096]{1,0:T(8,128)S(1)}, u32[]{:S(2)}, u32[]{:S(2)}) collective-permute-start(f32[32,4096]{1,0:T(8,128)S(1)} %collective-permute-done.11.refs_0_), channel_id=1, source_target_pairs={{0,63},{1,34},{2,33},{3,36},{4,35},{5,38},{6,37},{7,40},{8,39},{9,... | collective-permute-start | bytes 1572872 | tf_op jit(solution)/shard_map/ppermute | solution.py:234
  81.8 14.8 %collective-permute-start.21 = (f32[32,4096]{1,0:T(8,128)S(1)}, f32[32,4096]{1,0:T(8,128)S(1)}, u32[]{:S(2)}, u32[]{:S(2)}) collective-permute-start(f32[32,4096]{1,0:T(8,128)S(1)} %collective-permute-done.11.refs_0_), channel_id=1, source_target_pairs={{0,64},{1,65},{2,66},{3,67},{4,68},{5,69},{6,70},{7,71},{8,72},{9,... | collective-permute-start | bytes 1572872 | tf_op jit(solution)/shard_map/ppermute | solution.py:234
  84.3 20.5 %collective-permute-start.17 = (f32[32,4096]{1,0:T(8,128)S(1)}, f32[32,4096]{1,0:T(8,128)S(1)}, u32[]{:S(2)}, u32[]{:S(2)}) collective-permute-start(f32[32,4096]{1,0:T(8,128)S(1)} %copy-done.1), channel_id=1, source_target_pairs={{0,32},{1,33},{2,34},{3,35},{4,36},{5,37},{6,38},{7,39},{8,40},{9,... | collective-permute-start | bytes 1572872 | tf_op jit(solution)/shard_map/ppermute | solution.py:234
  90.1 17.4 %collective-permute-start.27 = (f32[32,4096]{1,0:T(8,128)S(1)}, f32[32,4096]{1,0:T(8,128)S(1)}, u32[]{:S(2)}, u32[]{:S(2)}) collective-permute-start(f32[32,4096]{1,0:T(8,128)S(1)} %collective-permute-done.18.refs_0_), channel_id=1, source_target_pairs={{0,63},{1,34},{2,33},{3,36},{4,35},{5,38},{6,37},{7,40},{8,39},{9,... | collective-permute-start | bytes 1572872 | tf_op jit(solution)/shard_map/ppermute | solution.py:234
  92.8 15.1 %collective-permute-start.26 = (f32[32,4096]{1,0:T(8,128)S(1)}, f32[32,4096]{1,0:T(8,128)S(1)}, u32[]{:S(2)}, u32[]{:S(2)}) collective-permute-start(f32[32,4096]{1,0:T(8,128)S(1)} %collective-permute-done.18.refs_0_), channel_id=1, source_target_pairs={{0,64},{1,65},{2,66},{3,67},{4,68},{5,69},{6,70},{7,71},{8,72},{9,... | collective-permute-start | bytes 1572872 | tf_op jit(solution)/shard_map/ppermute | solution.py:234
  96.6 17.9 %collective-permute-start.25 = (f32[32,4096]{1,0:T(8,128)S(1)}, f32[32,4096]{1,0:T(8,128)S(1)}, u32[]{:S(2)}, u32[]{:S(2)}) collective-permute-start(f32[32,4096]{1,0:T(8,128)S(1)} %pad_maximum_fusion), channel_id=1, source_target_pairs={{0,32},{1,33},{2,34},{3,35},{4,36},{5,37},{6,38},{7,39},{8,40},{9,... | collective-permute-start | bytes 1572872 | tf_op jit(solution)/shard_map/ppermute | solution.py:234
  104.9 9.6 %collective-permute-start.23 = (f32[16,4096]{1,0:T(8,128)S(1)}, f32[16,4096]{1,0:T(8,128)S(1)}, u32[]{:S(2)}, u32[]{:S(2)}) collective-permute-start(f32[16,4096]{1,0:T(8,128)S(1)} %slice.3), channel_id=1, source_target_pairs={{0,64},{1,65},{2,66},{3,67},{4,68},{5,69},{6,70},{7,71},{8,72},{9,... | collective-permute-start | bytes 786440 | tf_op jit(solution)/shard_map/ppermute | solution.py:234
  106.3 8.2 %collective-permute-start.24 = (f32[16,4096]{1,0:T(8,128)S(1)}, f32[16,4096]{1,0:T(8,128)S(1)}, u32[]{:S(2)}, u32[]{:S(2)}) collective-permute-start(f32[16,4096]{1,0:T(8,128)S(1)} %slice.3), channel_id=1, source_target_pairs={{0,63},{1,34},{2,33},{3,36},{4,35},{5,38},{6,37},{7,40},{8,39},{9,... | collective-permute-start | bytes 786440 | tf_op jit(solution)/shard_map/ppermute | solution.py:234
  (1 other events, 8.5 us)

commit v3 on v2

--- a/solution.py
+++ b/solution.py
@@ -8,6 +8,7 @@
 
 AXES = ("occ", "vir")
 PANEL = 1024
+INNER_ROWS = (1, 1, 1, 1, 2, 2, 0)
 NT = (((1,), (1,)), ((), ()))
 NN = (((1,), (0,)), ((), ()))
 
@@ -45,46 +46,59 @@
         copy.wait()
 
 
-def over_panels(width, body, start):
+def over_panels(width, body, start, unroll=2):
     def turn(at, state):
         return body(at, pl.ds(pl.multiple_of(at * PANEL, PANEL), PANEL), state)
 
-    return lax.fori_loop(0, width // PANEL, turn, start)
-
-
-def own_kernel(starts, mine_ref, gap_row_ref, gap_col_ref, *refs):
-    high_ref, low_ref, a_high_ref, a_low_ref, *parts, stage_ref, panel_sem, part_sem = refs
+    return lax.fori_loop(0, width // PANEL, turn, start, unroll=unroll)
+
+
+def split_kernel(starts, mine_ref, *refs):
+    *parts, stage_ref, in_sem, out_sem = refs
+    arrivals, departures = [], []
+    for at, (part, start) in enumerate(zip(parts, starts)):
+        rows = pl.ds(start, part.shape[0])
+        arrivals.append(fetch(mine_ref.at[rows], stage_ref.at[rows], in_sem.at[at]))
+    for at, (part, start) in enumerate(zip(parts, starts)):
+        arrivals[at].wait()
+        departures.append(fetch(stage_ref.at[pl.ds(start, part.shape[0])], part, out_sem.at[at]))
+    for copy in departures:
+        copy.wait()
+
+
+def own_kernel(mine_ref, gap_row_ref, gap_col_ref, high_ref, low_ref, gamma_ref, stage_ref, sem):
     rows, width = mine_ref.shape
     for at, cols in enumerate(panels(width)):
-        fetch(mine_ref.at[:, cols], stage_ref.at[:, cols], panel_sem.at[at])
-
-    def body(at, cols, state):
+        fetch(mine_ref.at[:, cols], stage_ref.at[:, cols], sem.at[at])
+
+    def gather(at, cols, state):
         integral, cross = state
-        pltpu.make_async_copy(mine_ref.at[:, cols], stage_ref.at[:, cols], panel_sem.at[at]).wait()
+        pltpu.make_async_copy(mine_ref.at[:, cols], stage_ref.at[:, cols], sem.at[at]).wait()
         high, low = halves(stage_ref[:, cols])
         high_ref[:, cols] = high
         low_ref[:, cols] = low
         return integral + mxu(high, high, NT), cross + mxu(high, low, NT)
 
     zero = jnp.zeros((rows, rows), jnp.float32)
-    integral, cross = over_panels(width, body, (zero, zero))
-    cuts = row_cuts(stage_ref, parts, starts, part_sem)
+    integral, cross = over_panels(width, gather, (zero, zero))
     integral = integral + (cross + cross.T)
     a_high, a_low = halves(integral / (gap_row_ref[...] + gap_col_ref[...]))
-    a_high_ref[...] = a_high
-    a_low_ref[...] = a_low
-    for copy in cuts:
-        copy.wait()
+
+    def spread(at, cols, state):
+        high, low = high_ref[:, cols], low_ref[:, cols]
+        gamma_ref[:, cols] = mxu(a_high, high) + (mxu(a_high, low) + mxu(a_low, high))
+        return state
+
+    over_panels(width, spread, 0)
 
 
 def step_kernel(plan, *refs):
-    count, own, inner_rows, gaps, final = plan
+    count, inner_rows, gaps, final, unroll = plan
     refs = list(refs)
     take = lambda number: [refs.pop(0) for _ in range(number)]
     others = take(count)
     high_ref, low_ref, gap_row_ref, table_ref = take(4)
-    a_own = take(2) if own else None
-    start_ref = None if own else take(1)[0]
+    start_ref = take(1)[0]
     inner_ref = take(1)[0] if inner_rows else None
     gamma_ref, both_ref = take(2)
     if inner_rows:
@@ -103,7 +117,7 @@
         return main + mxu(high_ref[:, cols], both, NT), rest + mxu(low_ref[:, cols], high, NT)
 
     start = (jnp.zeros((rows, 2 * extent), jnp.float32), jnp.zeros((rows, extent), jnp.float32))
-    main, rest = over_panels(width, gather, start)
+    main, rest = over_panels(width, gather, start, unroll)
     integral = main[:, :extent] + (main[:, extent:] + rest)
     gap_col = jnp.concatenate(
         [table_ref[row : row + 1, at : at + height] for row, at, height in gaps], axis=1
@@ -113,13 +127,7 @@
 
     def spread(at, cols, state):
         both = both_ref[:, cols]
-        gamma = mxu(a_twice, both) + mxu(a_low, both[:extent])
-        if own:
-            high, low = high_ref[:, cols], low_ref[:, cols]
-            a_high_own, a_low_own = a_own[0][...], a_own[1][...]
-            gamma += mxu(a_high_own, high) + (mxu(a_high_own, low) + mxu(a_low_own, high))
-        else:
-            gamma += start_ref[:, cols]
+        gamma = start_ref[:, cols] + (mxu(a_twice, both) + mxu(a_low, both[:extent]))
         if final:
             stage_ref, sem = refs
             stage_ref[:, cols] = gamma
@@ -128,7 +136,7 @@
             gamma_ref[:, cols] = gamma
         return state
 
-    over_panels(width, spread, 0)
+    over_panels(width, spread, 0, unroll)
     if final:
         stage_ref, sem = refs
         for at, cols in enumerate(panels(width)):
@@ -170,31 +178,45 @@
     )(in_hbm(mine))
 
 
-def own_call(mine, gap_row, gap_col, ranges):
+def split_call(mine, ranges):
     rows, width = mine.shape
     count = len(ranges)
+    return pl.pallas_call(
+        functools.partial(split_kernel, [start for start, _ in ranges]),
+        out_shape=tuple(pltpu.HBM((height, width), jnp.float32) for _, height in ranges),
+        in_specs=[HBM],
+        out_specs=(HBM,) * count,
+        scratch_shapes=[
+            pltpu.VMEM((rows, width), jnp.float32),
+            pltpu.SemaphoreType.DMA((count,)),
+            pltpu.SemaphoreType.DMA((count,)),
+        ],
+        compiler_params=params(6),
+        cost_estimate=cost(rows, rows, width),
+        name="other_cuts",
+    )(in_hbm(mine))
+
+
+def own_call(mine, gap_row, gap_col):
+    rows, width = mine.shape
     factor = pltpu.VMEM((rows, width), jnp.bfloat16)
-    amplitude = pltpu.VMEM((rows, rows), jnp.bfloat16)
     return pl.pallas_call(
-        functools.partial(own_kernel, [start for start, _ in ranges]),
-        out_shape=(factor, factor, amplitude, amplitude)
-        + tuple(pltpu.HBM((height, width), jnp.float32) for _, height in ranges),
+        own_kernel,
+        out_shape=(factor, factor, pltpu.VMEM((rows, width), jnp.float32)),
         in_specs=[HBM, VMEM, VMEM],
-        out_specs=(VMEM,) * 4 + (HBM,) * count,
+        out_specs=(VMEM,) * 3,
         scratch_shapes=[
             pltpu.VMEM((rows, width), jnp.float32),
             pltpu.SemaphoreType.DMA((width // PANEL,)),
-            pltpu.SemaphoreType.DMA((count,)),
         ],
         compiler_params=params(10),
-        cost_estimate=cost(rows, rows, width),
+        cost_estimate=pl.CostEstimate(flops=1 << 20, bytes_accessed=1 << 16, transcendentals=0),
         name="own_block",
     )(in_hbm(mine), gap_row, gap_col)
 
 
-def step_call(others, high, low, gap_row, table, gaps, begin, inner, inner_rows, final, name):
+def step_call(others, high, low, gap_row, table, gaps, begin, inner, inner_rows, final, unroll, name):
     rows, width = high.shape
-    own = len(begin) == 2
     extent = sum(other.shape[0] for other in others)
     scratch = []
     if inner_rows:
@@ -204,16 +226,16 @@
         scratch += [pltpu.VMEM((rows, width), jnp.float32), pltpu.SemaphoreType.DMA((width // PANEL,))]
     extra = [in_hbm(inner)] if inner_rows else []
     return pl.pallas_call(
-        functools.partial(step_kernel, (len(others), own, inner_rows, gaps, final)),
+        functools.partial(step_kernel, (len(others), inner_rows, gaps, final, unroll)),
         out_shape=(pltpu.HBM if final else pltpu.VMEM)((rows, width), jnp.float32),
-        in_specs=[VMEM] * (len(others) + 4 + len(begin)) + [HBM] * len(extra),
+        in_specs=[VMEM] * (len(others) + 5) + [HBM] * len(extra),
         out_specs=HBM if final else VMEM,
         scratch_shapes=[pltpu.VMEM((2 * extent, width), jnp.bfloat16)] + scratch,
-        input_output_aliases={} if final or own else {len(others) + 4: 0},
+        input_output_aliases={} if final else {len(others) + 4: 0},
         compiler_params=params(10),
         cost_estimate=pl.CostEstimate(flops=1 << 20, bytes_accessed=1 << 16, transcendentals=0),
         name=name,
-    )(*map(in_vmem, others), in_vmem(high), in_vmem(low), gap_row, table, *map(in_vmem, begin), *extra)
+    )(*map(in_vmem, others), in_vmem(high), in_vmem(low), gap_row, table, in_vmem(begin), *extra)
 
 
 def local(b_factors, occ_energy, vir_energy):
@@ -279,15 +301,15 @@
     first, ahead = cut_call(mine, [ranges[0], (size - early, early)])
     parts = [first]
     near = [moved(first, across)]
-    inner = moved(held(b_factors, first), inward).reshape(size, width)
+    inner = moved(b_factors, inward).reshape(size, width)
     ahead_back, ahead_out = moved(ahead, back), moved(ahead, outward)
-    high, low, a_high, a_low, *rest = own_call(held(mine, first), gap_row, gap.reshape(1, -1), ranges[1:])
-    parts += rest
+    parts += split_call(held(mine, first), ranges[1:])
     near.append(moved(held(parts[1], ahead_back, ahead_out), across))
-
-    done = [a_high, a_high]
+    high, low, gamma = own_call(held(mine, near[0], inner), gap_row, gap.reshape(1, -1))
+
+    done = [parts[1], gamma]
     far, outer = [], []
-    begin = [a_high, a_low]
+    begin = gamma
     inner_at = 0
 
     def step(k, *earlier):
@@ -302,21 +324,19 @@
             gaps += [(k, which * vir_block + shift, early) for shift in (0, at) for which in (1, 2)]
         else:
             others = [held(other, *earlier) for other in others]
-            height = vir_block if k < count - 2 else size - inner_at
-            rows = (inner_at, height)
+            height = INNER_ROWS[k] * vir_block
+            rows = (inner_at, height) if height else None
             gaps = [(k, 0, 3 * vir_block)]
             gaps += [(row, 3 * vir_block, vir_block) for row in range(inner_at // vir_block, (inner_at + height) // vir_block)]
             inner_at += height
-        gamma = step_call(others, high, low, gap_row, table, gaps, begin, inner, rows, final, "step_%d" % k)
-        begin = [gamma]
+        gamma = step_call(others, high, low, gap_row, table, gaps, begin, inner, rows, final, 4 if k > 3 else 2, "step_%d" % k)
+        begin = gamma
         done.append(gamma)
         return gamma
 
     late = None
     for k in range(count):
         part = held(near[k], done[k])
-        if k == 0:
-            part = held(part, inner)
         if k == count - 1:
             part = part[: vir_block - early]
         far.append(moved(part, along))

time: 120 us -> 122 us (1.017)
  waiting for transfers between devices: 11.2 us -> 35.6 us
  starting transfers between devices: 57.7 us -> 41.7 us
  Pallas kernels: 49 us -> 43.1 us
    ppermute x28, waiting for transfers between devices: 11.2 us -> 35.6 us  [moved(): return lax.ppermute(block, AXES, route)]
    ppermute x28, starting transfers between devices: 57.7 us -> 41.7 us  [moved(): return lax.ppermute(block, AXES, route)]
    pallas_call x9 -> x10, Pallas kernels: 47.9 us -> 41.9 us  [the longest x8 33.5 us: step_call(): pl.pallas_call(functools.partial(step_kernel, (len(others), inner_rows, g...]
  transfers between devices with their start and end apart: 28 -> 28, of which waited for: 6 -> 15; matrix products, arithmetic and copies ran while one was open for 1% -> 1% of each run, Pallas kernels for 36% -> 32%
where the time goes in v3:
time: 122 us
  Pallas kernels  43.1 us (35%)
  starting transfers between devices  41.7 us (34%)
  waiting for transfers between devices  35.6 us (29%)
    ppermute x28, starting transfers between devices, moved(): return lax.ppermute(block, AXES, route)  41.7 us
    ppermute x28, waiting for transfers between devices, moved(): return lax.ppermute(block, AXES, route)  35.6 us
    pallas_call x8, Pallas kernels, step_call(): pl.pallas_call(functools.partial(step_kernel, (len(others), inner_rows, g...  33.5 us
    pallas_call x1, Pallas kernels, own_call(): pl.pallas_call(own_kernel, out_shape=(factor, factor, pltpu.VMEM((rows, w...  5.43 us
    pallas_call x1, Pallas kernels, split_call(): pl.pallas_call(functools.partial(split_kernel, [start for start, _ in ran...  3.01 us
  transfers between devices with their start and end apart: 28, of which 15 were waited for; matrix products, arithmetic and copies ran while one was open for 1% of the time, Pallas kernels for 32%

profile of v3, /device:TPU:1, one launch (start us, length us, event | category | flops | bytes accessed | tf_op | source)
XLA Modules:
  0.0 122.1 jit_solution(8552244567367419232)
XLA Ops:
  0.0 3.2 %collective-permute-start.4 = (f32[8,32,4096]{2,1,0:T(8,128)}, f32[8,32,4096]{2,1,0:T(8,128)}, u32[]{:S(2)}, u32[]{:S(2)}) collective-permute-start(f32[8,32,4096]{2,1,0:T(8,128)} %param.3), channel_id=1, source_target_pairs={{0,1},{1,0},{2,3},{3,2},{4,5},{5,4},{6,7},{7,6},{8,9},{9,8},{10,11... | collective-permute-start | bytes 12582920 | tf_op jit(solution)/shard_map/ppermute | solution.py:256
  4.5 2.2 %collective-permute-start = (f32[16,4096]{1,0:T(8,128)S(1)}, f32[16,4096]{1,0:T(8,128)S(1)}, u32[]{:S(2)}, u32[]{:S(2)}) collective-permute-start(f32[16,4096]{1,0:T(8,128)S(1)} %get-tuple-element.62), channel_id=1, source_target_pairs={{0,192},{1,193},{2,194},{3,195},{4,196},{5,197},{6,198},{7,199},{8... | collective-permute-start | bytes 786440 | tf_op jit(solution)/shard_map/ppermute | solution.py:256
  7.5 3.0 %other_cuts.1 = (f32[32,4096]{1,0:T(8,128)}, f32[32,4096]{1,0:T(8,128)}, f32[32,4096]{1,0:T(8,128)}, f32[32,4096]{1,0:T(8,128)}, f32[32,4096]{1,0:T(8,128)}, /*index=5*/f32[32,4096]{1,0:T(8,128)}, f32[32,4096]{1,0:T(8,128)}) custom-call(f32[256,4096]{1,0:T(8,128)} %bitcast.4), custom_call_target="tpu_custom_call" | custom-call | flops 3221225472 | bytes 4194304 | tf_op jit(solution)/shard_map/other_cuts/pallas_call | solution.py:184
  10.5 2.0 %collective-permute-done = f32[16,4096]{1,0:T(8,128)S(1)} collective-permute-done((f32[16,4096]{1,0:T(8,128)S(1)}, f32[16,4096]{1,0:T(8,128)S(1)}, u32[]{:S(2)}, u32[]{:S(2)}) %collective-permute-start) | collective-permute-done | bytes 262176 | tf_op jit(solution)/shard_map/ppermute | solution.py:256
  12.5 4.0 %collective-permute-done.1 = f32[16,4096]{1,0:T(8,128)S(1)} collective-permute-done((f32[16,4096]{1,0:T(8,128)S(1)}, f32[16,4096]{1,0:T(8,128)S(1)}, u32[]{:S(2)}, u32[]{:S(2)}) %collective-permute-start.1) | collective-permute-done | bytes 262176 | tf_op jit(solution)/shard_map/ppermute | solution.py:256
  16.5 1.5 %collective-permute-done.3.refs_0_ = f32[32,4096]{1,0:T(8,128)S(1)} collective-permute-done((f32[32,4096]{1,0:T(8,128)S(1)}, f32[32,4096]{1,0:T(8,128)S(1)}, u32[]{:S(2)}, u32[]{:S(2)}) %collective-permute-start.3) | collective-permute-done | bytes 524320 | tf_op jit(solution)/shard_map/ppermute | solution.py:256
  18.0 1.8 %collective-permute-start.8 = (f32[32,4096]{1,0:T(8,128)S(1)}, f32[32,4096]{1,0:T(8,128)S(1)}, u32[]{:S(2)}, u32[]{:S(2)}) collective-permute-start(f32[32,4096]{1,0:T(8,128)S(1)} %collective-permute-done.3.refs_0_), channel_id=1, source_target_pairs={{0,63},{1,34},{2,33},{3,36},{4,35},{5,38},{6,37},{7,40},{8,39},{9,... | collective-permute-start | bytes 1572872 | tf_op jit(solution)/shard_map/ppermute | solution.py:256
  23.8 5.4 %own_block.1 = (bf16[256,4096]{1,0:T(8,128)(2,1)S(1)}, bf16[256,4096]{1,0:T(8,128)(2,1)S(1)}, f32[256,4096]{1,0:T(8,128)S(1)}) custom-call(f32[256,4096]{1,0:T(8,128)} %bitcast.5, f32[256,1]{1,0:T(8,128)S(1)} %sub.106.gap_row_ref.refs_5_.refs_6_, f32[1,256]{1,0:T(1,128)S(1)} %sub.93.gap_col_ref), custom_call_target="tpu_custom_call" | custom-call | flops 1048576 | bytes 65536 | tf_op jit(solution)/shard_map/own_block/pallas_call | solution.py:203
  29.8 2.6 %collective-permute-start.10 = (f32[32,4096]{1,0:T(8,128)S(1)}, f32[32,4096]{1,0:T(8,128)S(1)}, u32[]{:S(2)}, u32[]{:S(2)}) collective-permute-start(f32[32,4096]{1,0:T(8,128)S(1)} %collective-permute-done.2.refs_0_), channel_id=1, source_target_pairs={{0,63},{1,34},{2,33},{3,36},{4,35},{5,38},{6,37},{7,40},{8,39},{9,... | collective-permute-start | bytes 1572872 | tf_op jit(solution)/shard_map/ppermute | solution.py:256
  33.8 4.2 %step_0.1.refs_7_ = f32[256,4096]{1,0:T(8,128)S(1)} custom-call(f32[32,4096]{1,0:T(8,128)S(1)} %collective-permute-done.3.refs_0_, f32[32,4096]{1,0:T(8,128)S(1)} %collective-permute-done.7.refs_1_, f32[32,4096]{1,0:T(8,128)S(1)} %collective-permute-done.8.refs_2_, ...), custom_call_target="tpu_custom_call", output_to_operand_aliasing={{}: (7, {})} | custom-call | flops 1048576 | bytes 65536 | tf_op jit(solution)/shard_map/step_0/pallas_call | solution.py:228
  38.1 2.9 %collective-permute-done.6.refs_0_ = f32[32,4096]{1,0:T(8,128)S(1)} collective-permute-done((f32[32,4096]{1,0:T(8,128)}, f32[32,4096]{1,0:T(8,128)S(1)}, u32[]{:S(2)}, u32[]{:S(2)}) %collective-permute-start.6) | collective-permute-done | bytes 524320 | tf_op jit(solution)/shard_map/ppermute | solution.py:256
  41.0 2.6 %collective-permute-start.14 = (f32[32,4096]{1,0:T(8,128)S(1)}, f32[32,4096]{1,0:T(8,128)S(1)}, u32[]{:S(2)}, u32[]{:S(2)}) collective-permute-start(f32[32,4096]{1,0:T(8,128)S(1)} %collective-permute-done.6.refs_0_), channel_id=1, source_target_pairs={{0,63},{1,34},{2,33},{3,36},{4,35},{5,38},{6,37},{7,40},{8,39},{9,... | collective-permute-start | bytes 1572872 | tf_op jit(solution)/shard_map/ppermute | solution.py:256
  44.9 4.4 %collective-permute-done.10.refs_2_ = f32[32,4096]{1,0:T(8,128)S(1)} collective-permute-done((f32[32,4096]{1,0:T(8,128)S(1)}, f32[32,4096]{1,0:T(8,128)S(1)}, u32[]{:S(2)}, u32[]{:S(2)}) %collective-permute-start.10) | collective-permute-done | bytes 524320 | tf_op jit(solution)/shard_map/ppermute | solution.py:256
  50.2 4.2 %step_1.1.refs_7_ = f32[256,4096]{1,0:T(8,128)S(1)} custom-call(f32[32,4096]{1,0:T(8,128)S(1)} %collective-permute-done.2.refs_0_, f32[32,4096]{1,0:T(8,128)S(1)} %collective-permute-done.9.refs_1_, f32[32,4096]{1,0:T(8,128)S(1)} %collective-permute-done.10.refs_2_, ...), custom_call_target="tpu_custom_call", output_to_operand_aliasing={{}: (7, {})} | custom-call | flops 1048576 | bytes 65536 | tf_op jit(solution)/shard_map/step_1/pallas_call | solution.py:228
  54.4 3.5 %collective-permute-start.16 = (f32[32,4096]{1,0:T(8,128)S(1)}, f32[32,4096]{1,0:T(8,128)S(1)}, u32[]{:S(2)}, u32[]{:S(2)}) collective-permute-start(f32[32,4096]{1,0:T(8,128)S(1)} %collective-permute-done.5.refs_0_), channel_id=1, source_target_pairs={{0,63},{1,34},{2,33},{3,36},{4,35},{5,38},{6,37},{7,40},{8,39},{9,... | collective-permute-start | bytes 1572872 | tf_op jit(solution)/shard_map/ppermute | solution.py:256
  58.2 2.4 %collective-permute-done.14.refs_2_ = f32[32,4096]{1,0:T(8,128)S(1)} collective-permute-done((f32[32,4096]{1,0:T(8,128)S(1)}, f32[32,4096]{1,0:T(8,128)S(1)}, u32[]{:S(2)}, u32[]{:S(2)}) %collective-permute-start.14) | collective-permute-done | bytes 524320 | tf_op jit(solution)/shard_map/ppermute | solution.py:256
  61.4 4.2 %step_2.1.refs_7_ = f32[256,4096]{1,0:T(8,128)S(1)} custom-call(f32[32,4096]{1,0:T(8,128)S(1)} %collective-permute-done.6.refs_0_, f32[32,4096]{1,0:T(8,128)S(1)} %collective-permute-done.13.refs_1_, f32[32,4096]{1,0:T(8,128)S(1)} %collective-permute-done.14.refs_2_, ...), custom_call_target="tpu_custom_call", output_to_operand_aliasing={{}: (7, {})} | custom-call | flops 1048576 | bytes 65536 | tf_op jit(solution)/shard_map/step_2/pallas_call | solution.py:228
  65.7 3.5 %collective-permute-start.20 = (f32[32,4096]{1,0:T(8,128)S(1)}, f32[32,4096]{1,0:T(8,128)S(1)}, u32[]{:S(2)}, u32[]{:S(2)}) collective-permute-start(f32[32,4096]{1,0:T(8,128)S(1)} %collective-permute-done.12.refs_0_), channel_id=1, source_target_pairs={{0,63},{1,34},{2,33},{3,36},{4,35},{5,38},{6,37},{7,40},{8,39},{9,... | collective-permute-start | bytes 1572872 | tf_op jit(solution)/shard_map/ppermute | solution.py:256
  69.4 2.4 %collective-permute-done.16.refs_2_ = f32[32,4096]{1,0:T(8,128)S(1)} collective-permute-done((f32[32,4096]{1,0:T(8,128)S(1)}, f32[32,4096]{1,0:T(8,128)S(1)}, u32[]{:S(2)}, u32[]{:S(2)}) %collective-permute-start.16) | collective-permute-done | bytes 524320 | tf_op jit(solution)/shard_map/ppermute | solution.py:256
  71.8 4.2 %collective-permute-start.18 = (f32[32,4096]{1,0:T(8,128)S(1)}, f32[32,4096]{1,0:T(8,128)S(1)}, u32[]{:S(2)}, u32[]{:S(2)}) collective-permute-start(f32[32,4096]{1,0:T(8,128)S(1)} %copy-done.2), channel_id=1, source_target_pairs={{0,32},{1,33},{2,34},{3,35},{4,36},{5,37},{6,38},{7,39},{8,40},{9,... | collective-permute-start | bytes 1572872 | tf_op jit(solution)/shard_map/ppermute | solution.py:256
  76.0 4.2 %step_3.1.refs_7_ = f32[256,4096]{1,0:T(8,128)S(1)} custom-call(f32[32,4096]{1,0:T(8,128)S(1)} %collective-permute-done.5.refs_0_, f32[32,4096]{1,0:T(8,128)S(1)} %collective-permute-done.15.refs_1_, f32[32,4096]{1,0:T(8,128)S(1)} %collective-permute-done.16.refs_2_, ...), custom_call_target="tpu_custom_call", output_to_operand_aliasing={{}: (7, {})} | custom-call | flops 1048576 | bytes 65536 | tf_op jit(solution)/shard_map/step_3/pallas_call | solution.py:228
  80.7 2.4 %collective-permute-done.20.refs_2_ = f32[32,4096]{1,0:T(8,128)S(1)} collective-permute-done((f32[32,4096]{1,0:T(8,128)S(1)}, f32[32,4096]{1,0:T(8,128)S(1)}, u32[]{:S(2)}, u32[]{:S(2)}) %collective-permute-start.20) | collective-permute-done | bytes 524320 | tf_op jit(solution)/shard_map/ppermute | solution.py:256
  83.8 5.0 %step_4.1.refs_7_ = f32[256,4096]{1,0:T(8,128)S(1)} custom-call(f32[32,4096]{1,0:T(8,128)S(1)} %collective-permute-done.12.refs_0_, f32[32,4096]{1,0:T(8,128)S(1)} %collective-permute-done.19.refs_1_, f32[32,4096]{1,0:T(8,128)S(1)} %collective-permute-done.20.refs_2_, ...), custom_call_target="tpu_custom_call", output_to_operand_aliasing={{}: (7, {})} | custom-call | flops 1048576 | bytes 65536 | tf_op jit(solution)/shard_map/step_4/pallas_call | solution.py:228
  88.9 3.0 %collective-permute-start.27 = (f32[32,4096]{1,0:T(8,128)S(1)}, f32[32,4096]{1,0:T(8,128)S(1)}, u32[]{:S(2)}, u32[]{:S(2)}) collective-permute-start(f32[32,4096]{1,0:T(8,128)S(1)} %collective-permute-done.18.refs_0_), channel_id=1, source_target_pairs={{0,63},{1,34},{2,33},{3,36},{4,35},{5,38},{6,37},{7,40},{8,39},{9,... | collective-permute-start | bytes 1572872 | tf_op jit(solution)/shard_map/ppermute | solution.py:256
  92.8 2.1 %collective-permute-done.22.refs_2_ = f32[32,4096]{1,0:T(8,128)S(1)} collective-permute-done((f32[32,4096]{1,0:T(8,128)S(1)}, f32[32,4096]{1,0:T(8,128)S(1)}, u32[]{:S(2)}, u32[]{:S(2)}) %collective-permute-start.22) | collective-permute-done | bytes 524320 | tf_op jit(solution)/shard_map/ppermute | solution.py:256
  95.6 5.0 %step_5.1.refs_7_ = f32[256,4096]{1,0:T(8,128)S(1)} custom-call(f32[32,4096]{1,0:T(8,128)S(1)} %collective-permute-done.11.refs_0_, f32[32,4096]{1,0:T(8,128)S(1)} %collective-permute-done.21.refs_1_, f32[32,4096]{1,0:T(8,128)S(1)} %collective-permute-done.22.refs_2_, ...), custom_call_target="tpu_custom_call", output_to_operand_aliasing={{}: (7, {})} | custom-call | flops 1048576 | bytes 65536 | tf_op jit(solution)/shard_map/step_5/pallas_call | solution.py:228
  100.6 5.3 %collective-permute-done.17.refs_0_ = f32[32,4096]{1,0:T(8,128)S(1)} collective-permute-done((f32[32,4096]{1,0:T(8,128)S(1)}, f32[32,4096]{1,0:T(8,128)S(1)}, u32[]{:S(2)}, u32[]{:S(2)}) %collective-permute-start.17) | collective-permute-done | bytes 524320 | tf_op jit(solution)/shard_map/ppermute | solution.py:256
  105.9 1.5 %collective-permute-start.23 = (f32[16,4096]{1,0:T(8,128)S(1)}, f32[16,4096]{1,0:T(8,128)S(1)}, u32[]{:S(2)}, u32[]{:S(2)}) collective-permute-start(f32[16,4096]{1,0:T(8,128)S(1)} %slice.3), channel_id=1, source_target_pairs={{0,64},{1,65},{2,66},{3,67},{4,68},{5,69},{6,70},{7,71},{8,72},{9,... | collective-permute-start | bytes 786440 | tf_op jit(solution)/shard_map/ppermute | solution.py:256
  107.4 3.8 %collective-permute-start.24 = (f32[16,4096]{1,0:T(8,128)S(1)}, f32[16,4096]{1,0:T(8,128)S(1)}, u32[]{:S(2)}, u32[]{:S(2)}) collective-permute-start(f32[16,4096]{1,0:T(8,128)S(1)} %slice.3), channel_id=1, source_target_pairs={{0,63},{1,34},{2,33},{3,36},{4,35},{5,38},{6,37},{7,40},{8,39},{9,... | collective-permute-start | bytes 786440 | tf_op jit(solution)/shard_map/ppermute | solution.py:256
  111.2 2.8 %step_6.1.refs_8_ = f32[256,4096]{1,0:T(8,128)S(1)} custom-call(f32[32,4096]{1,0:T(8,128)S(1)} %collective-permute-done.18.refs_0_, f32[32,4096]{1,0:T(8,128)S(1)} %collective-permute-done.26.refs_1_, f32[32,4096]{1,0:T(8,128)S(1)} %collective-permute-done.27.refs_2_, ...), custom_call_target="tpu_custom_call", output_to_operand_aliasing={{}: (7, {})} | custom-call | flops 1048576 | bytes 65536 | tf_op jit(solution)/shard_map/step_6/pallas_call | solution.py:228
  114.1 4.0 %collective-permute-done.24.refs_2_ = f32[16,4096]{1,0:T(8,128)S(1)} collective-permute-done((f32[16,4096]{1,0:T(8,128)S(1)}, f32[16,4096]{1,0:T(8,128)S(1)}, u32[]{:S(2)}, u32[]{:S(2)}) %collective-permute-start.24) | collective-permute-done | bytes 262176 | tf_op jit(solution)/shard_map/ppermute | solution.py:256
  118.1 3.8 %step_7.1 = f32[256,4096]{1,0:T(8,128)} custom-call(f32[32,4096]{1,0:T(8,128)S(1)} %collective-permute-done.17.refs_0_, f32[16,4096]{1,0:T(8,128)S(1)} %collective-permute-done.23.refs_1_, f32[16,4096]{1,0:T(8,128)S(1)} %collective-permute-done.24.refs_2_, f32[32,4096]{1,0:T(8,128)S(1)} %collective-permute-done.25.refs_3_, ...), custom_call_target="tpu_custom_call" | custom-call | flops 1048576 | bytes 65536 | tf_op jit(solution)/shard_map/step_7/pallas_call | solution.py:228
  (55 shorter events, 14.5 us)
Async XLA Ops:
  0.0 23.8 %collective-permute-start.4 = (f32[8,32,4096]{2,1,0:T(8,128)}, f32[8,32,4096]{2,1,0:T(8,128)}, u32[]{:S(2)}, u32[]{:S(2)}) collective-permute-start(f32[8,32,4096]{2,1,0:T(8,128)} %param.3), channel_id=1, source_target_pairs={{0,1},{1,0},{2,3},{3,2},{4,5},{5,4},{6,7},{7,6},{8,9},{9,8},{10,11... | collective-permute-start | bytes 12582920 | tf_op jit(solution)/shard_map/ppermute | solution.py:256
  4.4 13.6 %collective-permute-start.3 = (f32[32,4096]{1,0:T(8,128)S(1)}, f32[32,4096]{1,0:T(8,128)S(1)}, u32[]{:S(2)}, u32[]{:S(2)}) collective-permute-start(f32[32,4096]{1,0:T(8,128)S(1)} %get-tuple-element.56), channel_id=1, source_target_pairs={{0,32},{1,33},{2,34},{3,35},{4,36},{5,37},{6,38},{7,39},{8,40},{9,... | collective-permute-start | bytes 1572872 | tf_op jit(solution)/shard_map/ppermute | solution.py:256
  4.5 16.2 %copy-start = (f32[64]{0:T(128)S(1)}, f32[64]{0:T(128)}, u32[]{:S(2)}) copy-start(f32[64]{0:T(128)} %param.4) | copy-start | bytes 772
  4.5 8.0 %collective-permute-start = (f32[16,4096]{1,0:T(8,128)S(1)}, f32[16,4096]{1,0:T(8,128)S(1)}, u32[]{:S(2)}, u32[]{:S(2)}) collective-permute-start(f32[16,4096]{1,0:T(8,128)S(1)} %get-tuple-element.62), channel_id=1, source_target_pairs={{0,192},{1,193},{2,194},{3,195},{4,196},{5,197},{6,198},{7,199},{8... | collective-permute-start | bytes 786440 | tf_op jit(solution)/shard_map/ppermute | solution.py:256
  6.7 9.8 %collective-permute-start.1 = (f32[16,4096]{1,0:T(8,128)S(1)}, f32[16,4096]{1,0:T(8,128)S(1)}, u32[]{:S(2)}, u32[]{:S(2)}) collective-permute-start(f32[16,4096]{1,0:T(8,128)S(1)} %get-tuple-element.62), channel_id=1, source_target_pairs={{0,63},{1,34},{2,33},{3,36},{4,35},{5,38},{6,37},{7,40},{8,39},{9,... | collective-permute-start | bytes 786440 | tf_op jit(solution)/shard_map/ppermute | solution.py:256
  16.5 13.3 %collective-permute-start.2 = (f32[32,4096]{1,0:T(8,128)}, f32[32,4096]{1,0:T(8,128)S(1)}, u32[]{:S(2)}, u32[]{:S(2)}) collective-permute-start(f32[32,4096]{1,0:T(8,128)} %get-tuple-element.63), channel_id=1, source_target_pairs={{0,32},{1,33},{2,34},{3,35},{4,36},{5,37},{6,38},{7,39},{8,40},{9,... | collective-permute-start | bytes 1572872 | tf_op jit(solution)/shard_map/ppermute | solution.py:256
  18.0 15.7 %collective-permute-start.8 = (f32[32,4096]{1,0:T(8,128)S(1)}, f32[32,4096]{1,0:T(8,128)S(1)}, u32[]{:S(2)}, u32[]{:S(2)}) collective-permute-start(f32[32,4096]{1,0:T(8,128)S(1)} %collective-permute-done.3.refs_0_), channel_id=1, source_target_pairs={{0,63},{1,34},{2,33},{3,36},{4,35},{5,38},{6,37},{7,40},{8,39},{9,... | collective-permute-start | bytes 1572872 | tf_op jit(solution)/shard_map/ppermute | solution.py:256
  20.8 13.1 %collective-permute-start.7 = (f32[32,4096]{1,0:T(8,128)S(1)}, f32[32,4096]{1,0:T(8,128)S(1)}, u32[]{:S(2)}, u32[]{:S(2)}) collective-permute-start(f32[32,4096]{1,0:T(8,128)S(1)} %collective-permute-done.3.refs_0_), channel_id=1, source_target_pairs={{0,64},{1,65},{2,66},{3,67},{4,68},{5,69},{6,70},{7,71},{8,72},{9,... | collective-permute-start | bytes 1572872 | tf_op jit(solution)/shard_map/ppermute | solution.py:256
  22.1 19.0 %collective-permute-start.6 = (f32[32,4096]{1,0:T(8,128)}, f32[32,4096]{1,0:T(8,128)S(1)}, u32[]{:S(2)}, u32[]{:S(2)}) collective-permute-start(f32[32,4096]{1,0:T(8,128)} %get-tuple-element.70), channel_id=1, source_target_pairs={{0,32},{1,33},{2,34},{3,35},{4,36},{5,37},{6,38},{7,39},{8,40},{9,... | collective-permute-start | bytes 1572872 | tf_op jit(solution)/shard_map/ppermute | solution.py:256
  29.8 19.6 %collective-permute-start.10 = (f32[32,4096]{1,0:T(8,128)S(1)}, f32[32,4096]{1,0:T(8,128)S(1)}, u32[]{:S(2)}, u32[]{:S(2)}) collective-permute-start(f32[32,4096]{1,0:T(8,128)S(1)} %collective-permute-done.2.refs_0_), channel_id=1, source_target_pairs={{0,63},{1,34},{2,33},{3,36},{4,35},{5,38},{6,37},{7,40},{8,39},{9,... | collective-permute-start | bytes 1572872 | tf_op jit(solution)/shard_map/ppermute | solution.py:256
  32.4 17.8 %collective-permute-start.9 = (f32[32,4096]{1,0:T(8,128)S(1)}, f32[32,4096]{1,0:T(8,128)S(1)}, u32[]{:S(2)}, u32[]{:S(2)}) collective-permute-start(f32[32,4096]{1,0:T(8,128)S(1)} %collective-permute-done.2.refs_0_), channel_id=1, source_target_pairs={{0,64},{1,65},{2,66},{3,67},{4,68},{5,69},{6,70},{7,71},{8,72},{9,... | collective-permute-start | bytes 1572872 | tf_op jit(solution)/shard_map/ppermute | solution.py:256
  33.7 20.7 %collective-permute-start.5 = (f32[32,4096]{1,0:T(8,128)S(1)}, f32[32,4096]{1,0:T(8,128)S(1)}, u32[]{:S(2)}, u32[]{:S(2)}) collective-permute-start(f32[32,4096]{1,0:T(8,128)S(1)} %copy-done.5), channel_id=1, source_target_pairs={{0,32},{1,33},{2,34},{3,35},{4,36},{5,37},{6,38},{7,39},{8,40},{9,... | collective-permute-start | bytes 1572872 | tf_op jit(solution)/shard_map/ppermute | solution.py:256
  33.8 15.5 %copy-start.4 = (f32[32,4096]{1,0:T(8,128)S(1)}, f32[32,4096]{1,0:T(8,128)}, u32[]{:S(2)}) copy-start(f32[32,4096]{1,0:T(8,128)} %get-tuple-element.83) | copy-start | bytes 1572868
  41.0 19.6 %collective-permute-start.14 = (f32[32,4096]{1,0:T(8,128)S(1)}, f32[32,4096]{1,0:T(8,128)S(1)}, u32[]{:S(2)}, u32[]{:S(2)}) collective-permute-start(f32[32,4096]{1,0:T(8,128)S(1)} %collective-permute-done.6.refs_0_), channel_id=1, source_target_pairs={{0,63},{1,34},{2,33},{3,36},{4,35},{5,38},{6,37},{7,40},{8,39},{9,... | collective-permute-start | bytes 1572872 | tf_op jit(solution)/shard_map/ppermute | solution.py:256
  43.6 17.8 %collective-permute-start.13 = (f32[32,4096]{1,0:T(8,128)S(1)}, f32[32,4096]{1,0:T(8,128)S(1)}, u32[]{:S(2)}, u32[]{:S(2)}) collective-permute-start(f32[32,4096]{1,0:T(8,128)S(1)} %collective-permute-done.6.refs_0_), channel_id=1, source_target_pairs={{0,64},{1,65},{2,66},{3,67},{4,68},{5,69},{6,70},{7,71},{8,72},{9,... | collective-permute-start | bytes 1572872 | tf_op jit(solution)/shard_map/ppermute | solution.py:256
  44.9 15.7 %copy-start.3 = (f32[32,4096]{1,0:T(8,128)S(1)}, f32[32,4096]{1,0:T(8,128)}, u32[]{:S(2)}) copy-start(f32[32,4096]{1,0:T(8,128)} %get-tuple-element.81) | copy-start | bytes 1572868
  49.3 16.3 %collective-permute-start.12 = (f32[32,4096]{1,0:T(8,128)S(1)}, f32[32,4096]{1,0:T(8,128)S(1)}, u32[]{:S(2)}, u32[]{:S(2)}) collective-permute-start(f32[32,4096]{1,0:T(8,128)S(1)} %copy-done.4), channel_id=1, source_target_pairs={{0,32},{1,33},{2,34},{3,35},{4,36},{5,37},{6,38},{7,39},{8,40},{9,... | collective-permute-start | bytes 1572872 | tf_op jit(solution)/shard_map/ppermute | solution.py:256
  54.4 17.4 %collective-permute-start.16 = (f32[32,4096]{1,0:T(8,128)S(1)}, f32[32,4096]{1,0:T(8,128)S(1)}, u32[]{:S(2)}, u32[]{:S(2)}) collective-permute-start(f32[32,4096]{1,0:T(8,128)S(1)} %collective-permute-done.5.refs_0_), channel_id=1, source_target_pairs={{0,63},{1,34},{2,33},{3,36},{4,35},{5,38},{6,37},{7,40},{8,39},{9,... | collective-permute-start | bytes 1572872 | tf_op jit(solution)/shard_map/ppermute | solution.py:256
  57.9 18.2 %collective-permute-start.15 = (f32[32,4096]{1,0:T(8,128)S(1)}, f32[32,4096]{1,0:T(8,128)S(1)}, u32[]{:S(2)}, u32[]{:S(2)}) collective-permute-start(f32[32,4096]{1,0:T(8,128)S(1)} %collective-permute-done.5.refs_0_), channel_id=1, source_target_pairs={{0,64},{1,65},{2,66},{3,67},{4,68},{5,69},{6,70},{7,71},{8,72},{9,... | collective-permute-start | bytes 1572872 | tf_op jit(solution)/shard_map/ppermute | solution.py:256
  58.2 13.6 %copy-start.2 = (f32[32,4096]{1,0:T(8,128)S(1)}, f32[32,4096]{1,0:T(8,128)}, u32[]{:S(2)}) copy-start(f32[32,4096]{1,0:T(8,128)} %get-tuple-element.94) | copy-start | bytes 1572868
  60.6 19.7 %collective-permute-start.11 = (f32[32,4096]{1,0:T(8,128)S(1)}, f32[32,4096]{1,0:T(8,128)S(1)}, u32[]{:S(2)}, u32[]{:S(2)}) collective-permute-start(f32[32,4096]{1,0:T(8,128)S(1)} %copy-done.3), channel_id=1, source_target_pairs={{0,32},{1,33},{2,34},{3,35},{4,36},{5,37},{6,38},{7,39},{8,40},{9,... | collective-permute-start | bytes 1572872 | tf_op jit(solution)/shard_map/ppermute | solution.py:256
  65.7 17.4 %collective-permute-start.20 = (f32[32,4096]{1,0:T(8,128)S(1)}, f32[32,4096]{1,0:T(8,128)S(1)}, u32[]{:S(2)}, u32[]{:S(2)}) collective-permute-start(f32[32,4096]{1,0:T(8,128)S(1)} %collective-permute-done.12.refs_0_), channel_id=1, source_target_pairs={{0,63},{1,34},{2,33},{3,36},{4,35},{5,38},{6,37},{7,40},{8,39},{9,... | collective-permute-start | bytes 1572872 | tf_op jit(solution)/shard_map/ppermute | solution.py:256
  69.1 14.7 %collective-permute-start.19 = (f32[32,4096]{1,0:T(8,128)S(1)}, f32[32,4096]{1,0:T(8,128)S(1)}, u32[]{:S(2)}, u32[]{:S(2)}) collective-permute-start(f32[32,4096]{1,0:T(8,128)S(1)} %collective-permute-done.12.refs_0_), channel_id=1, source_target_pairs={{0,64},{1,65},{2,66},{3,67},{4,68},{5,69},{6,70},{7,71},{8,72},{9,... | collective-permute-start | bytes 1572872 | tf_op jit(solution)/shard_map/ppermute | solution.py:256
  71.8 17.0 %collective-permute-start.18 = (f32[32,4096]{1,0:T(8,128)S(1)}, f32[32,4096]{1,0:T(8,128)S(1)}, u32[]{:S(2)}, u32[]{:S(2)}) collective-permute-start(f32[32,4096]{1,0:T(8,128)S(1)} %copy-done.2), channel_id=1, source_target_pairs={{0,32},{1,33},{2,34},{3,35},{4,36},{5,37},{6,38},{7,39},{8,40},{9,... | collective-permute-start | bytes 1572872 | tf_op jit(solution)/shard_map/ppermute | solution.py:256
  80.3 14.6 %collective-permute-start.22 = (f32[32,4096]{1,0:T(8,128)S(1)}, f32[32,4096]{1,0:T(8,128)S(1)}, u32[]{:S(2)}, u32[]{:S(2)}) collective-permute-start(f32[32,4096]{1,0:T(8,128)S(1)} %collective-permute-done.11.refs_0_), channel_id=1, source_target_pairs={{0,63},{1,34},{2,33},{3,36},{4,35},{5,38},{6,37},{7,40},{8,39},{9,... | collective-permute-start | bytes 1572872 | tf_op jit(solution)/shard_map/ppermute | solution.py:256
  80.4 15.2 %collective-permute-start.21 = (f32[32,4096]{1,0:T(8,128)S(1)}, f32[32,4096]{1,0:T(8,128)S(1)}, u32[]{:S(2)}, u32[]{:S(2)}) collective-permute-start(f32[32,4096]{1,0:T(8,128)S(1)} %collective-permute-done.11.refs_0_), channel_id=1, source_target_pairs={{0,64},{1,65},{2,66},{3,67},{4,68},{5,69},{6,70},{7,71},{8,72},{9,... | collective-permute-start | bytes 1572872 | tf_op jit(solution)/shard_map/ppermute | solution.py:256
  88.9 22.4 %collective-permute-start.27 = (f32[32,4096]{1,0:T(8,128)S(1)}, f32[32,4096]{1,0:T(8,128)S(1)}, u32[]{:S(2)}, u32[]{:S(2)}) collective-permute-start(f32[32,4096]{1,0:T(8,128)S(1)} %collective-permute-done.18.refs_0_), channel_id=1, source_target_pairs={{0,63},{1,34},{2,33},{3,36},{4,35},{5,38},{6,37},{7,40},{8,39},{9,... | collective-permute-start | bytes 1572872 | tf_op jit(solution)/shard_map/ppermute | solution.py:256
  91.9 19.3 %collective-permute-start.26 = (f32[32,4096]{1,0:T(8,128)S(1)}, f32[32,4096]{1,0:T(8,128)S(1)}, u32[]{:S(2)}, u32[]{:S(2)}) collective-permute-start(f32[32,4096]{1,0:T(8,128)S(1)} %collective-permute-done.18.refs_0_), channel_id=1, source_target_pairs={{0,64},{1,65},{2,66},{3,67},{4,68},{5,69},{6,70},{7,71},{8,72},{9,... | collective-permute-start | bytes 1572872 | tf_op jit(solution)/shard_map/ppermute | solution.py:256
  92.7 13.2 %collective-permute-start.17 = (f32[32,4096]{1,0:T(8,128)S(1)}, f32[32,4096]{1,0:T(8,128)S(1)}, u32[]{:S(2)}, u32[]{:S(2)}) collective-permute-start(f32[32,4096]{1,0:T(8,128)S(1)} %copy-done.1), channel_id=1, source_target_pairs={{0,32},{1,33},{2,34},{3,35},{4,36},{5,37},{6,38},{7,39},{8,40},{9,... | collective-permute-start | bytes 1572872 | tf_op jit(solution)/shard_map/ppermute | solution.py:256
  95.6 22.5 %collective-permute-start.25 = (f32[32,4096]{1,0:T(8,128)S(1)}, f32[32,4096]{1,0:T(8,128)S(1)}, u32[]{:S(2)}, u32[]{:S(2)}) collective-permute-start(f32[32,4096]{1,0:T(8,128)S(1)} %pad_maximum_fusion), channel_id=1, source_target_pairs={{0,32},{1,33},{2,34},{3,35},{4,36},{5,37},{6,38},{7,39},{8,40},{9,... | collective-permute-start | bytes 1572872 | tf_op jit(solution)/shard_map/ppermute | solution.py:256
  105.9 8.1 %collective-permute-start.23 = (f32[16,4096]{1,0:T(8,128)S(1)}, f32[16,4096]{1,0:T(8,128)S(1)}, u32[]{:S(2)}, u32[]{:S(2)}) collective-permute-start(f32[16,4096]{1,0:T(8,128)S(1)} %slice.3), channel_id=1, source_target_pairs={{0,64},{1,65},{2,66},{3,67},{4,68},{5,69},{6,70},{7,71},{8,72},{9,... | collective-permute-start | bytes 786440 | tf_op jit(solution)/shard_map/ppermute | solution.py:256
  107.4 10.6 %collective-permute-start.24 = (f32[16,4096]{1,0:T(8,128)S(1)}, f32[16,4096]{1,0:T(8,128)S(1)}, u32[]{:S(2)}, u32[]{:S(2)}) collective-permute-start(f32[16,4096]{1,0:T(8,128)S(1)} %slice.3), channel_id=1, source_target_pairs={{0,63},{1,34},{2,33},{3,36},{4,35},{5,38},{6,37},{7,40},{8,39},{9,... | collective-permute-start | bytes 786440 | tf_op jit(solution)/shard_map/ppermute | solution.py:256
  (2 other events, 22.5 us)

commit v4 on v3

--- a/solution.py
+++ b/solution.py
@@ -304,7 +304,7 @@
     inner = moved(b_factors, inward).reshape(size, width)
     ahead_back, ahead_out = moved(ahead, back), moved(ahead, outward)
     parts += split_call(held(mine, first), ranges[1:])
-    near.append(moved(held(parts[1], ahead_back, ahead_out), across))
+    near.append(moved(parts[1], across))
     high, low, gamma = own_call(held(mine, near[0], inner), gap_row, gap.reshape(1, -1))
 
     done = [parts[1], gamma]
@@ -334,9 +334,13 @@
         done.append(gamma)
         return gamma
 
-    late = None
+    relayed = jnp.concatenate([ahead_back, ahead_out], axis=0)
     for k in range(count):
         part = held(near[k], done[k])
+        if k == 0:
+            part = held(part, ahead_back, ahead_out)
+        if k == 1:
+            part = held(part, relayed)
         if k == count - 1:
             part = part[: vir_block - early]
         far.append(moved(part, along))
@@ -344,8 +348,7 @@
         if k + 2 < count:
             near.append(moved(held(parts[k + 2], part), across))
         elif k + 2 == count:
-            relayed = held(jnp.concatenate([ahead_back, ahead_out], axis=0), part, far[k - 1], outer[k - 1])
-            late = moved(relayed, across)
+            late = moved(held(relayed, part, far[k - 1], outer[k - 1]), across)
         if k > 0:
             step(k - 1, part)
     gamma = step(count - 1)

time: 122 us -> 119 us (0.975)
  the two profiles are of different devices: /device:TPU:1 before, /device:TPU:8 now
where the time goes in v4:
time: 119 us; the launch traced here: 118 us
  waiting for transfers between devices  48.6 us (41%)
  Pallas kernels  43.1 us (36%)
  starting transfers between devices  24.8 us (21%)
  local copies, waits for them, and re-layouts  1.24 us (1%)
    ppermute x28, waiting for transfers between devices, moved(): return lax.ppermute(block, AXES, route)  48.6 us
    pallas_call x8, Pallas kernels, step_call(): pl.pallas_call(functools.partial(step_kernel, (len(others), inner_rows, g...  33.6 us
    ppermute x28, starting transfers between devices, moved(): return lax.ppermute(block, AXES, route)  24.8 us
    pallas_call x1, Pallas kernels, own_call(): pl.pallas_call(own_kernel, out_shape=(factor, factor, pltpu.VMEM((rows, w...  5.37 us
    pallas_call x1, Pallas kernels, split_call(): pl.pallas_call(functools.partial(split_kernel, [start for start, _ in ran...  3.02 us
  transfers between devices with their start and end apart: 28, of which 10 were waited for; matrix products, arithmetic and copies ran while one was open for 1% of the time, Pallas kernels for 33%

profile of v4, /device:TPU:8, one launch (start us, length us, event | category | flops | bytes accessed | tf_op | source)
XLA Modules:
  0.0 118.3 jit_solution(3453248496412885843)
XLA Ops:
  0.0 1.1 first_cuts.1
  1.1 2.3 %collective-permute-start.3 = (f32[16,4096]{1,0:T(8,128)S(1)}, f32[16,4096]{1,0:T(8,128)S(1)}, u32[]{:S(2)}, u32[]{:S(2)}) collective-permute-start(f32[16,4096]{1,0:T(8,128)S(1)} %get-tuple-element.66), channel_id=1, source_target_pairs={{0,192},{1,193},{2,194},{3,195},{4,196},{5,197},{6,198},{7,199},{8... | collective-permute-start | bytes 786440 | tf_op jit(solution)/shard_map/ppermute | solution.py:256
  3.4 7.3 %collective-permute-start.4 = (f32[16,4096]{1,0:T(8,128)S(1)}, f32[16,4096]{1,0:T(8,128)S(1)}, u32[]{:S(2)}, u32[]{:S(2)}) collective-permute-start(f32[16,4096]{1,0:T(8,128)S(1)} %get-tuple-element.66), channel_id=1, source_target_pairs={{0,63},{1,34},{2,33},{3,36},{4,35},{5,38},{6,37},{7,40},{8,39},{9,... | collective-permute-start | bytes 786440 | tf_op jit(solution)/shard_map/ppermute | solution.py:256
  10.7 3.0 %other_cuts.1 = (f32[32,4096]{1,0:T(8,128)}, f32[32,4096]{1,0:T(8,128)}, f32[32,4096]{1,0:T(8,128)}, f32[32,4096]{1,0:T(8,128)}, f32[32,4096]{1,0:T(8,128)}, /*index=5*/f32[32,4096]{1,0:T(8,128)}, f32[32,4096]{1,0:T(8,128)}) custom-call(f32[256,4096]{1,0:T(8,128)} %bitcast.4), custom_call_target="tpu_custom_call" | custom-call | flops 3221225472 | bytes 4194304 | tf_op jit(solution)/shard_map/other_cuts/pallas_call | solution.py:184
  13.7 2.1 %collective-permute-start = (f32[32,4096]{1,0:T(8,128)}, f32[32,4096]{1,0:T(8,128)S(1)}, u32[]{:S(2)}, u32[]{:S(2)}) collective-permute-start(f32[32,4096]{1,0:T(8,128)} %get-tuple-element.62), channel_id=1, source_target_pairs={{0,32},{1,33},{2,34},{3,35},{4,36},{5,37},{6,38},{7,39},{8,40},{9,... | collective-permute-start | bytes 1572872 | tf_op jit(solution)/shard_map/ppermute | solution.py:256
  17.1 8.4 %collective-permute-done.1.refs_0_ = f32[32,4096]{1,0:T(8,128)S(1)} collective-permute-done((f32[32,4096]{1,0:T(8,128)S(1)}, f32[32,4096]{1,0:T(8,128)S(1)}, u32[]{:S(2)}, u32[]{:S(2)}) %collective-permute-start.1) | collective-permute-done | bytes 524320 | tf_op jit(solution)/shard_map/ppermute | solution.py:256
  25.5 1.3 %collective-permute-start.7 = (f32[32,4096]{1,0:T(8,128)S(1)}, f32[32,4096]{1,0:T(8,128)S(1)}, u32[]{:S(2)}, u32[]{:S(2)}) collective-permute-start(f32[32,4096]{1,0:T(8,128)S(1)} %collective-permute-done.1.refs_0_), channel_id=1, source_target_pairs={{0,64},{1,65},{2,66},{3,67},{4,68},{5,69},{6,70},{7,71},{8,72},{9,... | collective-permute-start | bytes 1572872 | tf_op jit(solution)/shard_map/ppermute | solution.py:256
  27.7 5.4 %own_block.1 = (bf16[256,4096]{1,0:T(8,128)(2,1)S(1)}, bf16[256,4096]{1,0:T(8,128)(2,1)S(1)}, f32[256,4096]{1,0:T(8,128)S(1)}) custom-call(f32[256,4096]{1,0:T(8,128)} %bitcast.5, f32[256,1]{1,0:T(8,128)S(1)} %sub.106.gap_row_ref.refs_5_.refs_6_, f32[1,256]{1,0:T(1,128)S(1)} %sub.93.gap_col_ref), custom_call_target="tpu_custom_call" | custom-call | flops 1048576 | bytes 65536 | tf_op jit(solution)/shard_map/own_block/pallas_call | solution.py:203
  33.1 3.7 %collective-permute-done.refs_0_ = f32[32,4096]{1,0:T(8,128)S(1)} collective-permute-done((f32[32,4096]{1,0:T(8,128)}, f32[32,4096]{1,0:T(8,128)S(1)}, u32[]{:S(2)}, u32[]{:S(2)}) %collective-permute-start) | collective-permute-done | bytes 524320 | tf_op jit(solution)/shard_map/ppermute | solution.py:256
  36.9 1.3 %collective-permute-start.9 = (f32[32,4096]{1,0:T(8,128)S(1)}, f32[32,4096]{1,0:T(8,128)S(1)}, u32[]{:S(2)}, u32[]{:S(2)}) collective-permute-start(f32[32,4096]{1,0:T(8,128)S(1)} %collective-permute-done.refs_0_), channel_id=1, source_target_pairs={{0,64},{1,65},{2,66},{3,67},{4,68},{5,69},{6,70},{7,71},{8,72},{9,... | collective-permute-start | bytes 1572872 | tf_op jit(solution)/shard_map/ppermute | solution.py:256
  39.0 4.2 %step_0.1.refs_7_ = f32[256,4096]{1,0:T(8,128)S(1)} custom-call(f32[32,4096]{1,0:T(8,128)S(1)} %collective-permute-done.1.refs_0_, f32[32,4096]{1,0:T(8,128)S(1)} %collective-permute-done.7.refs_1_, f32[32,4096]{1,0:T(8,128)S(1)} %collective-permute-done.8.refs_2_, ...), custom_call_target="tpu_custom_call", output_to_operand_aliasing={{}: (7, {})} | custom-call | flops 1048576 | bytes 65536 | tf_op jit(solution)/shard_map/step_0/pallas_call | solution.py:228
  43.2 4.8 %collective-permute-done.6.refs_0_ = f32[32,4096]{1,0:T(8,128)S(1)} collective-permute-done((f32[32,4096]{1,0:T(8,128)}, f32[32,4096]{1,0:T(8,128)S(1)}, u32[]{:S(2)}, u32[]{:S(2)}) %collective-permute-start.6) | collective-permute-done | bytes 524320 | tf_op jit(solution)/shard_map/ppermute | solution.py:256
  48.0 1.3 %collective-permute-start.13 = (f32[32,4096]{1,0:T(8,128)S(1)}, f32[32,4096]{1,0:T(8,128)S(1)}, u32[]{:S(2)}, u32[]{:S(2)}) collective-permute-start(f32[32,4096]{1,0:T(8,128)S(1)} %collective-permute-done.6.refs_0_), channel_id=1, source_target_pairs={{0,64},{1,65},{2,66},{3,67},{4,68},{5,69},{6,70},{7,71},{8,72},{9,... | collective-permute-start | bytes 1572872 | tf_op jit(solution)/shard_map/ppermute | solution.py:256
  50.0 4.2 %step_1.1.refs_7_ = f32[256,4096]{1,0:T(8,128)S(1)} custom-call(f32[32,4096]{1,0:T(8,128)S(1)} %collective-permute-done.refs_0_, f32[32,4096]{1,0:T(8,128)S(1)} %collective-permute-done.9.refs_1_, f32[32,4096]{1,0:T(8,128)S(1)} %collective-permute-done.10.refs_2_, ...), custom_call_target="tpu_custom_call", output_to_operand_aliasing={{}: (7, {})} | custom-call | flops 1048576 | bytes 65536 | tf_op jit(solution)/shard_map/step_1/pallas_call | solution.py:228
  54.2 5.1 %collective-permute-done.5.refs_0_ = f32[32,4096]{1,0:T(8,128)S(1)} collective-permute-done((f32[32,4096]{1,0:T(8,128)S(1)}, f32[32,4096]{1,0:T(8,128)S(1)}, u32[]{:S(2)}, u32[]{:S(2)}) %collective-permute-start.5) | collective-permute-done | bytes 524320 | tf_op jit(solution)/shard_map/ppermute | solution.py:256
  59.2 1.3 %collective-permute-start.15 = (f32[32,4096]{1,0:T(8,128)S(1)}, f32[32,4096]{1,0:T(8,128)S(1)}, u32[]{:S(2)}, u32[]{:S(2)}) collective-permute-start(f32[32,4096]{1,0:T(8,128)S(1)} %collective-permute-done.5.refs_0_), channel_id=1, source_target_pairs={{0,64},{1,65},{2,66},{3,67},{4,68},{5,69},{6,70},{7,71},{8,72},{9,... | collective-permute-start | bytes 1572872 | tf_op jit(solution)/shard_map/ppermute | solution.py:256
  60.6 4.2 %step_2.1.refs_7_ = f32[256,4096]{1,0:T(8,128)S(1)} custom-call(f32[32,4096]{1,0:T(8,128)S(1)} %collective-permute-done.6.refs_0_, f32[32,4096]{1,0:T(8,128)S(1)} %collective-permute-done.13.refs_1_, f32[32,4096]{1,0:T(8,128)S(1)} %collective-permute-done.14.refs_2_, ...), custom_call_target="tpu_custom_call", output_to_operand_aliasing={{}: (7, {})} | custom-call | flops 1048576 | bytes 65536 | tf_op jit(solution)/shard_map/step_2/pallas_call | solution.py:228
  64.9 5.6 %collective-permute-done.12.refs_0_ = f32[32,4096]{1,0:T(8,128)S(1)} collective-permute-done((f32[32,4096]{1,0:T(8,128)S(1)}, f32[32,4096]{1,0:T(8,128)S(1)}, u32[]{:S(2)}, u32[]{:S(2)}) %collective-permute-start.12) | collective-permute-done | bytes 524320 | tf_op jit(solution)/shard_map/ppermute | solution.py:256
  70.5 1.3 %collective-permute-start.19 = (f32[32,4096]{1,0:T(8,128)S(1)}, f32[32,4096]{1,0:T(8,128)S(1)}, u32[]{:S(2)}, u32[]{:S(2)}) collective-permute-start(f32[32,4096]{1,0:T(8,128)S(1)} %collective-permute-done.12.refs_0_), channel_id=1, source_target_pairs={{0,64},{1,65},{2,66},{3,67},{4,68},{5,69},{6,70},{7,71},{8,72},{9,... | collective-permute-start | bytes 1572872 | tf_op jit(solution)/shard_map/ppermute | solution.py:256
  71.9 4.2 %step_3.1.refs_7_ = f32[256,4096]{1,0:T(8,128)S(1)} custom-call(f32[32,4096]{1,0:T(8,128)S(1)} %collective-permute-done.5.refs_0_, f32[32,4096]{1,0:T(8,128)S(1)} %collective-permute-done.15.refs_1_, f32[32,4096]{1,0:T(8,128)S(1)} %collective-permute-done.16.refs_2_, ...), custom_call_target="tpu_custom_call", output_to_operand_aliasing={{}: (7, {})} | custom-call | flops 1048576 | bytes 65536 | tf_op jit(solution)/shard_map/step_3/pallas_call | solution.py:228
  76.1 5.6 %collective-permute-done.11.refs_0_ = f32[32,4096]{1,0:T(8,128)S(1)} collective-permute-done((f32[32,4096]{1,0:T(8,128)S(1)}, f32[32,4096]{1,0:T(8,128)S(1)}, u32[]{:S(2)}, u32[]{:S(2)}) %collective-permute-start.11) | collective-permute-done | bytes 524320 | tf_op jit(solution)/shard_map/ppermute | solution.py:256
  81.7 1.3 %collective-permute-start.21 = (f32[32,4096]{1,0:T(8,128)S(1)}, f32[32,4096]{1,0:T(8,128)S(1)}, u32[]{:S(2)}, u32[]{:S(2)}) collective-permute-start(f32[32,4096]{1,0:T(8,128)S(1)} %collective-permute-done.11.refs_0_), channel_id=1, source_target_pairs={{0,64},{1,65},{2,66},{3,67},{4,68},{5,69},{6,70},{7,71},{8,72},{9,... | collective-permute-start | bytes 1572872 | tf_op jit(solution)/shard_map/ppermute | solution.py:256
  83.0 5.0 %step_4.1.refs_7_ = f32[256,4096]{1,0:T(8,128)S(1)} custom-call(f32[32,4096]{1,0:T(8,128)S(1)} %collective-permute-done.12.refs_0_, f32[32,4096]{1,0:T(8,128)S(1)} %collective-permute-done.19.refs_1_, f32[32,4096]{1,0:T(8,128)S(1)} %collective-permute-done.20.refs_2_, ...), custom_call_target="tpu_custom_call", output_to_operand_aliasing={{}: (7, {})} | custom-call | flops 1048576 | bytes 65536 | tf_op jit(solution)/shard_map/step_4/pallas_call | solution.py:228
  88.1 4.9 %collective-permute-done.18.refs_0_ = f32[32,4096]{1,0:T(8,128)S(1)} collective-permute-done((f32[32,4096]{1,0:T(8,128)S(1)}, f32[32,4096]{1,0:T(8,128)S(1)}, u32[]{:S(2)}, u32[]{:S(2)}) %collective-permute-start.18) | collective-permute-done | bytes 524320 | tf_op jit(solution)/shard_map/ppermute | solution.py:256
  93.0 1.3 %collective-permute-start.26 = (f32[32,4096]{1,0:T(8,128)S(1)}, f32[32,4096]{1,0:T(8,128)S(1)}, u32[]{:S(2)}, u32[]{:S(2)}) collective-permute-start(f32[32,4096]{1,0:T(8,128)S(1)} %collective-permute-done.18.refs_0_), channel_id=1, source_target_pairs={{0,64},{1,65},{2,66},{3,67},{4,68},{5,69},{6,70},{7,71},{8,72},{9,... | collective-permute-start | bytes 1572872 | tf_op jit(solution)/shard_map/ppermute | solution.py:256
  94.2 5.0 %step_5.1.refs_7_ = f32[256,4096]{1,0:T(8,128)S(1)} custom-call(f32[32,4096]{1,0:T(8,128)S(1)} %collective-permute-done.11.refs_0_, f32[32,4096]{1,0:T(8,128)S(1)} %collective-permute-done.21.refs_1_, f32[32,4096]{1,0:T(8,128)S(1)} %collective-permute-done.22.refs_2_, ...), custom_call_target="tpu_custom_call", output_to_operand_aliasing={{}: (7, {})} | custom-call | flops 1048576 | bytes 65536 | tf_op jit(solution)/shard_map/step_5/pallas_call | solution.py:228
  99.3 4.5 %collective-permute-done.17.refs_0_ = f32[32,4096]{1,0:T(8,128)S(1)} collective-permute-done((f32[32,4096]{1,0:T(8,128)S(1)}, f32[32,4096]{1,0:T(8,128)S(1)}, u32[]{:S(2)}, u32[]{:S(2)}) %collective-permute-start.17) | collective-permute-done | bytes 524320 | tf_op jit(solution)/shard_map/ppermute | solution.py:256
  103.8 1.4 %collective-permute-start.23 = (f32[16,4096]{1,0:T(8,128)S(1)}, f32[16,4096]{1,0:T(8,128)S(1)}, u32[]{:S(2)}, u32[]{:S(2)}) collective-permute-start(f32[16,4096]{1,0:T(8,128)S(1)} %slice.3), channel_id=1, source_target_pairs={{0,64},{1,65},{2,66},{3,67},{4,68},{5,69},{6,70},{7,71},{8,72},{9,... | collective-permute-start | bytes 786440 | tf_op jit(solution)/shard_map/ppermute | solution.py:256
  105.4 2.8 %step_6.1.refs_8_ = f32[256,4096]{1,0:T(8,128)S(1)} custom-call(f32[32,4096]{1,0:T(8,128)S(1)} %collective-permute-done.18.refs_0_, f32[32,4096]{1,0:T(8,128)S(1)} %collective-permute-done.26.refs_1_, f32[32,4096]{1,0:T(8,128)S(1)} %collective-permute-done.27.refs_2_, ...), custom_call_target="tpu_custom_call", output_to_operand_aliasing={{}: (7, {})} | custom-call | flops 1048576 | bytes 65536 | tf_op jit(solution)/shard_map/step_6/pallas_call | solution.py:228
  108.2 2.0 %collective-permute-done.23.refs_1_ = f32[16,4096]{1,0:T(8,128)S(1)} collective-permute-done((f32[16,4096]{1,0:T(8,128)S(1)}, f32[16,4096]{1,0:T(8,128)S(1)}, u32[]{:S(2)}, u32[]{:S(2)}) %collective-permute-start.23) | collective-permute-done | bytes 262176 | tf_op jit(solution)/shard_map/ppermute | solution.py:256
  110.2 4.0 %collective-permute-done.24.refs_2_ = f32[16,4096]{1,0:T(8,128)S(1)} collective-permute-done((f32[16,4096]{1,0:T(8,128)S(1)}, f32[16,4096]{1,0:T(8,128)S(1)}, u32[]{:S(2)}, u32[]{:S(2)}) %collective-permute-start.24) | collective-permute-done | bytes 262176 | tf_op jit(solution)/shard_map/ppermute | solution.py:256
  114.3 3.8 %step_7.1 = f32[256,4096]{1,0:T(8,128)} custom-call(f32[32,4096]{1,0:T(8,128)S(1)} %collective-permute-done.17.refs_0_, f32[16,4096]{1,0:T(8,128)S(1)} %collective-permute-done.23.refs_1_, f32[16,4096]{1,0:T(8,128)S(1)} %collective-permute-done.24.refs_2_, f32[32,4096]{1,0:T(8,128)S(1)} %collective-permute-done.25.refs_3_, ...), custom_call_target="tpu_custom_call" | custom-call | flops 1048576 | bytes 65536 | tf_op jit(solution)/shard_map/step_7/pallas_call | solution.py:228
  (56 shorter events, 4.2 us)
Async XLA Ops:
  0.0 27.7 %collective-permute-start.2 = (f32[8,32,4096]{2,1,0:T(8,128)}, f32[8,32,4096]{2,1,0:T(8,128)}, u32[]{:S(2)}, u32[]{:S(2)}) collective-permute-start(f32[8,32,4096]{2,1,0:T(8,128)} %param.3), channel_id=1, source_target_pairs={{0,1},{1,0},{2,3},{3,2},{4,5},{5,4},{6,7},{7,6},{8,9},{9,8},{10,11... | collective-permute-start | bytes 12582920 | tf_op jit(solution)/shard_map/ppermute | solution.py:256
  1.1 15.9 %collective-permute-start.3 = (f32[16,4096]{1,0:T(8,128)S(1)}, f32[16,4096]{1,0:T(8,128)S(1)}, u32[]{:S(2)}, u32[]{:S(2)}) collective-permute-start(f32[16,4096]{1,0:T(8,128)S(1)} %get-tuple-element.66), channel_id=1, source_target_pairs={{0,192},{1,193},{2,194},{3,195},{4,196},{5,197},{6,198},{7,199},{8... | collective-permute-start | bytes 786440 | tf_op jit(solution)/shard_map/ppermute | solution.py:256
  3.4 22.1 %collective-permute-start.4 = (f32[16,4096]{1,0:T(8,128)S(1)}, f32[16,4096]{1,0:T(8,128)S(1)}, u32[]{:S(2)}, u32[]{:S(2)}) collective-permute-start(f32[16,4096]{1,0:T(8,128)S(1)} %get-tuple-element.66), channel_id=1, source_target_pairs={{0,63},{1,34},{2,33},{3,36},{4,35},{5,38},{6,37},{7,40},{8,39},{9,... | collective-permute-start | bytes 786440 | tf_op jit(solution)/shard_map/ppermute | solution.py:256
  10.7 14.9 %collective-permute-start.1 = (f32[32,4096]{1,0:T(8,128)S(1)}, f32[32,4096]{1,0:T(8,128)S(1)}, u32[]{:S(2)}, u32[]{:S(2)}) collective-permute-start(f32[32,4096]{1,0:T(8,128)S(1)} %get-tuple-element.57), channel_id=1, source_target_pairs={{0,32},{1,33},{2,34},{3,35},{4,36},{5,37},{6,38},{7,39},{8,40},{9,... | collective-permute-start | bytes 1572872 | tf_op jit(solution)/shard_map/ppermute | solution.py:256
  13.7 24.5 %copy-start.5 = (f32[32,4096]{1,0:T(8,128)S(1)}, f32[32,4096]{1,0:T(8,128)}, u32[]{:S(2)}) copy-start(f32[32,4096]{1,0:T(8,128)} %get-tuple-element.68) | copy-start | bytes 1572868
  13.7 23.1 %collective-permute-start = (f32[32,4096]{1,0:T(8,128)}, f32[32,4096]{1,0:T(8,128)S(1)}, u32[]{:S(2)}, u32[]{:S(2)}) collective-permute-start(f32[32,4096]{1,0:T(8,128)} %get-tuple-element.62), channel_id=1, source_target_pairs={{0,32},{1,33},{2,34},{3,35},{4,36},{5,37},{6,38},{7,39},{8,40},{9,... | collective-permute-start | bytes 1572872 | tf_op jit(solution)/shard_map/ppermute | solution.py:256
  25.5 12.6 %collective-permute-start.8 = (f32[32,4096]{1,0:T(8,128)S(1)}, f32[32,4096]{1,0:T(8,128)S(1)}, u32[]{:S(2)}, u32[]{:S(2)}) collective-permute-start(f32[32,4096]{1,0:T(8,128)S(1)} %collective-permute-done.1.refs_0_), channel_id=1, source_target_pairs={{0,63},{1,34},{2,33},{3,36},{4,35},{5,38},{6,37},{7,40},{8,39},{9,... | collective-permute-start | bytes 1572872 | tf_op jit(solution)/shard_map/ppermute | solution.py:256
  25.5 13.4 %collective-permute-start.7 = (f32[32,4096]{1,0:T(8,128)S(1)}, f32[32,4096]{1,0:T(8,128)S(1)}, u32[]{:S(2)}, u32[]{:S(2)}) collective-permute-start(f32[32,4096]{1,0:T(8,128)S(1)} %collective-permute-done.1.refs_0_), channel_id=1, source_target_pairs={{0,64},{1,65},{2,66},{3,67},{4,68},{5,69},{6,70},{7,71},{8,72},{9,... | collective-permute-start | bytes 1572872 | tf_op jit(solution)/shard_map/ppermute | solution.py:256
  26.8 21.2 %collective-permute-start.6 = (f32[32,4096]{1,0:T(8,128)}, f32[32,4096]{1,0:T(8,128)S(1)}, u32[]{:S(2)}, u32[]{:S(2)}) collective-permute-start(f32[32,4096]{1,0:T(8,128)} %get-tuple-element.72), channel_id=1, source_target_pairs={{0,32},{1,33},{2,34},{3,35},{4,36},{5,37},{6,38},{7,39},{8,40},{9,... | collective-permute-start | bytes 1572872 | tf_op jit(solution)/shard_map/ppermute | solution.py:256
  36.8 12.5 %collective-permute-start.10 = (f32[32,4096]{1,0:T(8,128)S(1)}, f32[32,4096]{1,0:T(8,128)S(1)}, u32[]{:S(2)}, u32[]{:S(2)}) collective-permute-start(f32[32,4096]{1,0:T(8,128)S(1)} %collective-permute-done.refs_0_), channel_id=1, source_target_pairs={{0,63},{1,34},{2,33},{3,36},{4,35},{5,38},{6,37},{7,40},{8,39},{9,... | collective-permute-start | bytes 1572872 | tf_op jit(solution)/shard_map/ppermute | solution.py:256
  36.9 13.1 %collective-permute-start.9 = (f32[32,4096]{1,0:T(8,128)S(1)}, f32[32,4096]{1,0:T(8,128)S(1)}, u32[]{:S(2)}, u32[]{:S(2)}) collective-permute-start(f32[32,4096]{1,0:T(8,128)S(1)} %collective-permute-done.refs_0_), channel_id=1, source_target_pairs={{0,64},{1,65},{2,66},{3,67},{4,68},{5,69},{6,70},{7,71},{8,72},{9,... | collective-permute-start | bytes 1572872 | tf_op jit(solution)/shard_map/ppermute | solution.py:256
  38.2 21.1 %collective-permute-start.5 = (f32[32,4096]{1,0:T(8,128)S(1)}, f32[32,4096]{1,0:T(8,128)S(1)}, u32[]{:S(2)}, u32[]{:S(2)}) collective-permute-start(f32[32,4096]{1,0:T(8,128)S(1)} %copy-done.5), channel_id=1, source_target_pairs={{0,32},{1,33},{2,34},{3,35},{4,36},{5,37},{6,38},{7,39},{8,40},{9,... | collective-permute-start | bytes 1572872 | tf_op jit(solution)/shard_map/ppermute | solution.py:256
  48.0 12.5 %collective-permute-start.14 = (f32[32,4096]{1,0:T(8,128)S(1)}, f32[32,4096]{1,0:T(8,128)S(1)}, u32[]{:S(2)}, u32[]{:S(2)}) collective-permute-start(f32[32,4096]{1,0:T(8,128)S(1)} %collective-permute-done.6.refs_0_), channel_id=1, source_target_pairs={{0,63},{1,34},{2,33},{3,36},{4,35},{5,38},{6,37},{7,40},{8,39},{9,... | collective-permute-start | bytes 1572872 | tf_op jit(solution)/shard_map/ppermute | solution.py:256
  48.0 12.6 %collective-permute-start.13 = (f32[32,4096]{1,0:T(8,128)S(1)}, f32[32,4096]{1,0:T(8,128)S(1)}, u32[]{:S(2)}, u32[]{:S(2)}) collective-permute-start(f32[32,4096]{1,0:T(8,128)S(1)} %collective-permute-done.6.refs_0_), channel_id=1, source_target_pairs={{0,64},{1,65},{2,66},{3,67},{4,68},{5,69},{6,70},{7,71},{8,72},{9,... | collective-permute-start | bytes 1572872 | tf_op jit(solution)/shard_map/ppermute | solution.py:256
  49.3 11.2 %copy-start.3 = (f32[32,4096]{1,0:T(8,128)S(1)}, f32[32,4096]{1,0:T(8,128)}, u32[]{:S(2)}) copy-start(f32[32,4096]{1,0:T(8,128)} %get-tuple-element.83) | copy-start | bytes 1572868
  49.3 21.2 %collective-permute-start.12 = (f32[32,4096]{1,0:T(8,128)S(1)}, f32[32,4096]{1,0:T(8,128)S(1)}, u32[]{:S(2)}, u32[]{:S(2)}) collective-permute-start(f32[32,4096]{1,0:T(8,128)S(1)} %copy-done.4), channel_id=1, source_target_pairs={{0,32},{1,33},{2,34},{3,35},{4,36},{5,37},{6,38},{7,39},{8,40},{9,... | collective-permute-start | bytes 1572872 | tf_op jit(solution)/shard_map/ppermute | solution.py:256
  59.2 12.5 %collective-permute-start.16 = (f32[32,4096]{1,0:T(8,128)S(1)}, f32[32,4096]{1,0:T(8,128)S(1)}, u32[]{:S(2)}, u32[]{:S(2)}) collective-permute-start(f32[32,4096]{1,0:T(8,128)S(1)} %collective-permute-done.5.refs_0_), channel_id=1, source_target_pairs={{0,63},{1,34},{2,33},{3,36},{4,35},{5,38},{6,37},{7,40},{8,39},{9,... | collective-permute-start | bytes 1572872 | tf_op jit(solution)/shard_map/ppermute | solution.py:256
  59.2 12.6 %collective-permute-start.15 = (f32[32,4096]{1,0:T(8,128)S(1)}, f32[32,4096]{1,0:T(8,128)S(1)}, u32[]{:S(2)}, u32[]{:S(2)}) collective-permute-start(f32[32,4096]{1,0:T(8,128)S(1)} %collective-permute-done.5.refs_0_), channel_id=1, source_target_pairs={{0,64},{1,65},{2,66},{3,67},{4,68},{5,69},{6,70},{7,71},{8,72},{9,... | collective-permute-start | bytes 1572872 | tf_op jit(solution)/shard_map/ppermute | solution.py:256
  60.5 11.2 %copy-start.2 = (f32[32,4096]{1,0:T(8,128)S(1)}, f32[32,4096]{1,0:T(8,128)}, u32[]{:S(2)}) copy-start(f32[32,4096]{1,0:T(8,128)} %get-tuple-element.96) | copy-start | bytes 1572868
  60.5 21.2 %collective-permute-start.11 = (f32[32,4096]{1,0:T(8,128)S(1)}, f32[32,4096]{1,0:T(8,128)S(1)}, u32[]{:S(2)}, u32[]{:S(2)}) collective-permute-start(f32[32,4096]{1,0:T(8,128)S(1)} %copy-done.3), channel_id=1, source_target_pairs={{0,32},{1,33},{2,34},{3,35},{4,36},{5,37},{6,38},{7,39},{8,40},{9,... | collective-permute-start | bytes 1572872 | tf_op jit(solution)/shard_map/ppermute | solution.py:256
  70.5 12.5 %collective-permute-start.20 = (f32[32,4096]{1,0:T(8,128)S(1)}, f32[32,4096]{1,0:T(8,128)S(1)}, u32[]{:S(2)}, u32[]{:S(2)}) collective-permute-start(f32[32,4096]{1,0:T(8,128)S(1)} %collective-permute-done.12.refs_0_), channel_id=1, source_target_pairs={{0,63},{1,34},{2,33},{3,36},{4,35},{5,38},{6,37},{7,40},{8,39},{9,... | collective-permute-start | bytes 1572872 | tf_op jit(solution)/shard_map/ppermute | solution.py:256
  70.5 12.5 %collective-permute-start.19 = (f32[32,4096]{1,0:T(8,128)S(1)}, f32[32,4096]{1,0:T(8,128)S(1)}, u32[]{:S(2)}, u32[]{:S(2)}) collective-permute-start(f32[32,4096]{1,0:T(8,128)S(1)} %collective-permute-done.12.refs_0_), channel_id=1, source_target_pairs={{0,64},{1,65},{2,66},{3,67},{4,68},{5,69},{6,70},{7,71},{8,72},{9,... | collective-permute-start | bytes 1572872 | tf_op jit(solution)/shard_map/ppermute | solution.py:256
  71.8 11.2 %copy-start.1 = (f32[32,4096]{1,0:T(8,128)S(1)}, f32[32,4096]{1,0:T(8,128)}, u32[]{:S(2)}) copy-start(f32[32,4096]{1,0:T(8,128)} %get-tuple-element.94) | copy-start | bytes 1572868
  71.8 21.2 %collective-permute-start.18 = (f32[32,4096]{1,0:T(8,128)S(1)}, f32[32,4096]{1,0:T(8,128)S(1)}, u32[]{:S(2)}, u32[]{:S(2)}) collective-permute-start(f32[32,4096]{1,0:T(8,128)S(1)} %copy-done.2), channel_id=1, source_target_pairs={{0,32},{1,33},{2,34},{3,35},{4,36},{5,37},{6,38},{7,39},{8,40},{9,... | collective-permute-start | bytes 1572872 | tf_op jit(solution)/shard_map/ppermute | solution.py:256
  81.7 12.5 %collective-permute-start.22 = (f32[32,4096]{1,0:T(8,128)S(1)}, f32[32,4096]{1,0:T(8,128)S(1)}, u32[]{:S(2)}, u32[]{:S(2)}) collective-permute-start(f32[32,4096]{1,0:T(8,128)S(1)} %collective-permute-done.11.refs_0_), channel_id=1, source_target_pairs={{0,63},{1,34},{2,33},{3,36},{4,35},{5,38},{6,37},{7,40},{8,39},{9,... | collective-permute-start | bytes 1572872 | tf_op jit(solution)/shard_map/ppermute | solution.py:256
  81.7 12.5 %collective-permute-start.21 = (f32[32,4096]{1,0:T(8,128)S(1)}, f32[32,4096]{1,0:T(8,128)S(1)}, u32[]{:S(2)}, u32[]{:S(2)}) collective-permute-start(f32[32,4096]{1,0:T(8,128)S(1)} %collective-permute-done.11.refs_0_), channel_id=1, source_target_pairs={{0,64},{1,65},{2,66},{3,67},{4,68},{5,69},{6,70},{7,71},{8,72},{9,... | collective-permute-start | bytes 1572872 | tf_op jit(solution)/shard_map/ppermute | solution.py:256
  83.0 20.8 %collective-permute-start.17 = (f32[32,4096]{1,0:T(8,128)S(1)}, f32[32,4096]{1,0:T(8,128)S(1)}, u32[]{:S(2)}, u32[]{:S(2)}) collective-permute-start(f32[32,4096]{1,0:T(8,128)S(1)} %copy-done.1), channel_id=1, source_target_pairs={{0,32},{1,33},{2,34},{3,35},{4,36},{5,37},{6,38},{7,39},{8,40},{9,... | collective-permute-start | bytes 1572872 | tf_op jit(solution)/shard_map/ppermute | solution.py:256
  92.9 12.4 %collective-permute-start.27 = (f32[32,4096]{1,0:T(8,128)S(1)}, f32[32,4096]{1,0:T(8,128)S(1)}, u32[]{:S(2)}, u32[]{:S(2)}) collective-permute-start(f32[32,4096]{1,0:T(8,128)S(1)} %collective-permute-done.18.refs_0_), channel_id=1, source_target_pairs={{0,63},{1,34},{2,33},{3,36},{4,35},{5,38},{6,37},{7,40},{8,39},{9,... | collective-permute-start | bytes 1572872 | tf_op jit(solution)/shard_map/ppermute | solution.py:256
  93.0 12.4 %collective-permute-start.26 = (f32[32,4096]{1,0:T(8,128)S(1)}, f32[32,4096]{1,0:T(8,128)S(1)}, u32[]{:S(2)}, u32[]{:S(2)}) collective-permute-start(f32[32,4096]{1,0:T(8,128)S(1)} %collective-permute-done.18.refs_0_), channel_id=1, source_target_pairs={{0,64},{1,65},{2,66},{3,67},{4,68},{5,69},{6,70},{7,71},{8,72},{9,... | collective-permute-start | bytes 1572872 | tf_op jit(solution)/shard_map/ppermute | solution.py:256
  94.2 20.0 %collective-permute-start.25 = (f32[32,4096]{1,0:T(8,128)S(1)}, f32[32,4096]{1,0:T(8,128)S(1)}, u32[]{:S(2)}, u32[]{:S(2)}) collective-permute-start(f32[32,4096]{1,0:T(8,128)S(1)} %constant_dynamic-update-slice_fusion), channel_id=1, source_target_pairs={{0,32},{1,33},{2,34},{3,35},{4,36},{5,37},{6,38},{7,39},{8,40},{9,... | collective-permute-start | bytes 1572872 | tf_op jit(solution)/shard_map/ppermute | solution.py:256
  103.8 6.4 %collective-permute-start.23 = (f32[16,4096]{1,0:T(8,128)S(1)}, f32[16,4096]{1,0:T(8,128)S(1)}, u32[]{:S(2)}, u32[]{:S(2)}) collective-permute-start(f32[16,4096]{1,0:T(8,128)S(1)} %slice.3), channel_id=1, source_target_pairs={{0,64},{1,65},{2,66},{3,67},{4,68},{5,69},{6,70},{7,71},{8,72},{9,... | collective-permute-start | bytes 786440 | tf_op jit(solution)/shard_map/ppermute | solution.py:256
  105.1 9.1 %collective-permute-start.24 = (f32[16,4096]{1,0:T(8,128)S(1)}, f32[16,4096]{1,0:T(8,128)S(1)}, u32[]{:S(2)}, u32[]{:S(2)}) collective-permute-start(f32[16,4096]{1,0:T(8,128)S(1)} %slice.3), channel_id=1, source_target_pairs={{0,63},{1,34},{2,33},{3,36},{4,35},{5,38},{6,37},{7,40},{8,39},{9,... | collective-permute-start | bytes 786440 | tf_op jit(solution)/shard_map/ppermute | solution.py:256
  (2 other events, 16.3 us)

commit v5 on v4

--- a/solution.py
+++ b/solution.py
@@ -56,11 +56,15 @@
 def split_kernel(starts, mine_ref, *refs):
     *parts, stage_ref, in_sem, out_sem = refs
     arrivals, departures = [], []
+    reached = starts[0]
     for at, (part, start) in enumerate(zip(parts, starts)):
-        rows = pl.ds(start, part.shape[0])
-        arrivals.append(fetch(mine_ref.at[rows], stage_ref.at[rows], in_sem.at[at]))
+        if start >= reached:
+            reached = start + part.shape[0]
+            rows = pl.ds(start, part.shape[0])
+            arrivals.append(fetch(mine_ref.at[rows], stage_ref.at[rows], in_sem.at[at]))
     for at, (part, start) in enumerate(zip(parts, starts)):
-        arrivals[at].wait()
+        if at < len(arrivals):
+            arrivals[at].wait()
         departures.append(fetch(stage_ref.at[pl.ds(start, part.shape[0])], part, out_sem.at[at]))
     for copy in departures:
         copy.wait()
@@ -298,13 +302,14 @@
     count = occ_block
     ranges = [(k * vir_block, vir_block) for k in range(count)]
 
-    first, ahead = cut_call(mine, [ranges[0], (size - early, early)])
+    [first] = cut_call(mine, ranges[:1])
     parts = [first]
     near = [moved(first, across)]
     inner = moved(b_factors, inward).reshape(size, width)
+    *rest, ahead = split_call(held(mine, first), ranges[1:] + [(size - early, early)])
+    parts += rest
+    near.append(moved(parts[1], across))
     ahead_back, ahead_out = moved(ahead, back), moved(ahead, outward)
-    parts += split_call(held(mine, first), ranges[1:])
-    near.append(moved(parts[1], across))
     high, low, gamma = own_call(held(mine, near[0], inner), gap_row, gap.reshape(1, -1))
 
     done = [parts[1], gamma]

time: 119 us -> 116 us (0.975)
  the two profiles are of different devices: /device:TPU:8 before, /device:TPU:1 now
where the time goes in v5:
time: 116 us; the launch traced here: 115 us
  Pallas kernels  42.8 us (37%)
  starting transfers between devices  41.2 us (36%)
  waiting for transfers between devices  29.5 us (25%)
  local copies, waits for them, and re-layouts  1.24 us (1%)
    ppermute x28, starting transfers between devices, moved(): return lax.ppermute(block, AXES, route)  41.2 us
    pallas_call x8, Pallas kernels, step_call(): pl.pallas_call(functools.partial(step_kernel, (len(others), inner_rows, g...  33.3 us
    ppermute x28, waiting for transfers between devices, moved(): return lax.ppermute(block, AXES, route)  29.5 us
    pallas_call x1, Pallas kernels, own_call(): pl.pallas_call(own_kernel, out_shape=(factor, factor, pltpu.VMEM((rows, w...  5.35 us
    pallas_call x1, Pallas kernels, split_call(): pl.pallas_call(functools.partial(split_kernel, [start for start, _ in ran...  3.13 us
  transfers between devices with their start and end apart: 28, of which 13 were waited for; matrix products, arithmetic and copies ran while one was open for 1% of the time, Pallas kernels for 34%

profile of v5, /device:TPU:1, one launch (start us, length us, event | category | flops | bytes accessed | tf_op | source)
XLA Modules:
  0.0 115.4 jit_solution(13017853144033322402)
XLA Ops:
  0.0 3.2 %collective-permute-start.2 = (f32[8,32,4096]{2,1,0:T(8,128)}, f32[8,32,4096]{2,1,0:T(8,128)}, u32[]{:S(2)}, u32[]{:S(2)}) collective-permute-start(f32[8,32,4096]{2,1,0:T(8,128)} %param.3), channel_id=1, source_target_pairs={{0,1},{1,0},{2,3},{3,2},{4,5},{5,4},{6,7},{7,6},{8,9},{9,8},{10,11... | collective-permute-start | bytes 12582920 | tf_op jit(solution)/shard_map/ppermute | solution.py:260
  4.4 3.1 %other_cuts.1 = (f32[32,4096]{1,0:T(8,128)}, f32[32,4096]{1,0:T(8,128)}, f32[32,4096]{1,0:T(8,128)}, f32[32,4096]{1,0:T(8,128)}, f32[32,4096]{1,0:T(8,128)}, /*i...) custom-call(f32[256,4096]{1,0:T(8,128)} %bitcast.4), custom_call_target="tpu_custom_call" | custom-call | flops 3221225472 | bytes 4194304 | tf_op jit(solution)/shard_map/other_cuts/pallas_call | solution.py:188
  7.6 2.3 %collective-permute-start.3 = (f32[16,4096]{1,0:T(8,128)}, f32[16,4096]{1,0:T(8,128)S(1)}, u32[]{:S(2)}, u32[]{:S(2)}) collective-permute-start(f32[16,4096]{1,0:T(8,128)} %get-tuple-element.64), channel_id=1, source_target_pairs={{0,192},{1,193},{2,194},{3,195},{4,196},{5,197},{6,198},{7,199},{8... | collective-permute-start | bytes 786440 | tf_op jit(solution)/shard_map/ppermute | solution.py:260
  10.6 1.8 %collective-permute-start = (f32[32,4096]{1,0:T(8,128)}, f32[32,4096]{1,0:T(8,128)S(1)}, u32[]{:S(2)}, u32[]{:S(2)}) collective-permute-start(f32[32,4096]{1,0:T(8,128)} %get-tuple-element.60), channel_id=1, source_target_pairs={{0,32},{1,33},{2,34},{3,35},{4,36},{5,37},{6,38},{7,39},{8,40},{9,... | collective-permute-start | bytes 1572872 | tf_op jit(solution)/shard_map/ppermute | solution.py:260
  13.6 2.1 %collective-permute-done.3 = f32[16,4096]{1,0:T(8,128)S(1)} collective-permute-done((f32[16,4096]{1,0:T(8,128)}, f32[16,4096]{1,0:T(8,128)S(1)}, u32[]{:S(2)}, u32[]{:S(2)}) %collective-permute-start.3) | collective-permute-done | bytes 262176 | tf_op jit(solution)/shard_map/ppermute | solution.py:260
  15.8 2.1 %collective-permute-done.1.refs_0_ = f32[32,4096]{1,0:T(8,128)S(1)} collective-permute-done((f32[32,4096]{1,0:T(8,128)S(1)}, f32[32,4096]{1,0:T(8,128)S(1)}, u32[]{:S(2)}, u32[]{:S(2)}) %collective-permute-start.1) | collective-permute-done | bytes 524320 | tf_op jit(solution)/shard_map/ppermute | solution.py:260
  18.0 1.9 %collective-permute-done.4 = f32[16,4096]{1,0:T(8,128)S(1)} collective-permute-done((f32[16,4096]{1,0:T(8,128)}, f32[16,4096]{1,0:T(8,128)S(1)}, u32[]{:S(2)}, u32[]{:S(2)}) %collective-permute-start.4) | collective-permute-done | bytes 262176 | tf_op jit(solution)/shard_map/ppermute | solution.py:260
  22.5 5.3 %own_block.1 = (bf16[256,4096]{1,0:T(8,128)(2,1)S(1)}, bf16[256,4096]{1,0:T(8,128)(2,1)S(1)}, f32[256,4096]{1,0:T(8,128)S(1)}) custom-call(f32[256,4096]{1,0:T(8,128)} %bitcast.5, f32[256,1]{1,0:T(8,128)S(1)} %sub.106.gap_row_ref.refs_5_.refs_6_, f32[1,256]{1,0:T(1,128)S(1)} %sub.93.gap_col_ref), custom_call_target="tpu_custom_call" | custom-call | flops 1048576 | bytes 65536 | tf_op jit(solution)/shard_map/own_block/pallas_call | solution.py:207
  28.6 2.4 %collective-permute-start.10 = (f32[32,4096]{1,0:T(8,128)S(1)}, f32[32,4096]{1,0:T(8,128)S(1)}, u32[]{:S(2)}, u32[]{:S(2)}) collective-permute-start(f32[32,4096]{1,0:T(8,128)S(1)} %collective-permute-done.refs_0_), channel_id=1, source_target_pairs={{0,63},{1,34},{2,33},{3,36},{4,35},{5,38},{6,37},{7,40},{8,39},{9,... | collective-permute-start | bytes 1572872 | tf_op jit(solution)/shard_map/ppermute | solution.py:260
  32.4 3.2 %collective-permute-done.8.refs_2_ = f32[32,4096]{1,0:T(8,128)S(1)} collective-permute-done((f32[32,4096]{1,0:T(8,128)S(1)}, f32[32,4096]{1,0:T(8,128)S(1)}, u32[]{:S(2)}, u32[]{:S(2)}) %collective-permute-start.8) | collective-permute-done | bytes 524320 | tf_op jit(solution)/shard_map/ppermute | solution.py:260
  35.6 4.2 %step_0.1.refs_7_ = f32[256,4096]{1,0:T(8,128)S(1)} custom-call(f32[32,4096]{1,0:T(8,128)S(1)} %collective-permute-done.1.refs_0_, f32[32,4096]{1,0:T(8,128)S(1)} %collective-permute-done.7.refs_1_, f32[32,4096]{1,0:T(8,128)S(1)} %collective-permute-done.8.refs_2_, ...), custom_call_target="tpu_custom_call", output_to_operand_aliasing={{}: (7, {})} | custom-call | flops 1048576 | bytes 65536 | tf_op jit(solution)/shard_map/step_0/pallas_call | solution.py:232
  39.8 2.4 %collective-permute-start.14 = (f32[32,4096]{1,0:T(8,128)S(1)}, f32[32,4096]{1,0:T(8,128)S(1)}, u32[]{:S(2)}, u32[]{:S(2)}) collective-permute-start(f32[32,4096]{1,0:T(8,128)S(1)} %collective-permute-done.6.refs_0_), channel_id=1, source_target_pairs={{0,63},{1,34},{2,33},{3,36},{4,35},{5,38},{6,37},{7,40},{8,39},{9,... | collective-permute-start | bytes 1572872 | tf_op jit(solution)/shard_map/ppermute | solution.py:260
  43.5 3.3 %collective-permute-done.10.refs_2_ = f32[32,4096]{1,0:T(8,128)S(1)} collective-permute-done((f32[32,4096]{1,0:T(8,128)S(1)}, f32[32,4096]{1,0:T(8,128)S(1)}, u32[]{:S(2)}, u32[]{:S(2)}) %collective-permute-start.10) | collective-permute-done | bytes 524320 | tf_op jit(solution)/shard_map/ppermute | solution.py:260
  46.8 2.2 %collective-permute-start.12 = (f32[32,4096]{1,0:T(8,128)S(1)}, f32[32,4096]{1,0:T(8,128)S(1)}, u32[]{:S(2)}, u32[]{:S(2)}) collective-permute-start(f32[32,4096]{1,0:T(8,128)S(1)} %copy-done.4), channel_id=1, source_target_pairs={{0,32},{1,33},{2,34},{3,35},{4,36},{5,37},{6,38},{7,39},{8,40},{9,... | collective-permute-start | bytes 1572872 | tf_op jit(solution)/shard_map/ppermute | solution.py:260
  49.0 4.2 %step_1.1.refs_7_ = f32[256,4096]{1,0:T(8,128)S(1)} custom-call(f32[32,4096]{1,0:T(8,128)S(1)} %collective-permute-done.refs_0_, f32[32,4096]{1,0:T(8,128)S(1)} %collective-permute-done.9.refs_1_, f32[32,4096]{1,0:T(8,128)S(1)} %collective-permute-done.10.refs_2_, ...), custom_call_target="tpu_custom_call", output_to_operand_aliasing={{}: (7, {})} | custom-call | flops 1048576 | bytes 65536 | tf_op jit(solution)/shard_map/step_1/pallas_call | solution.py:232
  53.2 3.5 %collective-permute-start.16 = (f32[32,4096]{1,0:T(8,128)S(1)}, f32[32,4096]{1,0:T(8,128)S(1)}, u32[]{:S(2)}, u32[]{:S(2)}) collective-permute-start(f32[32,4096]{1,0:T(8,128)S(1)} %collective-permute-done.5.refs_0_), channel_id=1, source_target_pairs={{0,63},{1,34},{2,33},{3,36},{4,35},{5,38},{6,37},{7,40},{8,39},{9,... | collective-permute-start | bytes 1572872 | tf_op jit(solution)/shard_map/ppermute | solution.py:260
  58.1 2.2 %collective-permute-start.11 = (f32[32,4096]{1,0:T(8,128)S(1)}, f32[32,4096]{1,0:T(8,128)S(1)}, u32[]{:S(2)}, u32[]{:S(2)}) collective-permute-start(f32[32,4096]{1,0:T(8,128)S(1)} %copy-done.3), channel_id=1, source_target_pairs={{0,32},{1,33},{2,34},{3,35},{4,36},{5,37},{6,38},{7,39},{8,40},{9,... | collective-permute-start | bytes 1572872 | tf_op jit(solution)/shard_map/ppermute | solution.py:260
  60.3 4.2 %step_2.1.refs_7_ = f32[256,4096]{1,0:T(8,128)S(1)} custom-call(f32[32,4096]{1,0:T(8,128)S(1)} %collective-permute-done.6.refs_0_, f32[32,4096]{1,0:T(8,128)S(1)} %collective-permute-done.13.refs_1_, f32[32,4096]{1,0:T(8,128)S(1)} %collective-permute-done.14.refs_2_, ...), custom_call_target="tpu_custom_call", output_to_operand_aliasing={{}: (7, {})} | custom-call | flops 1048576 | bytes 65536 | tf_op jit(solution)/shard_map/step_2/pallas_call | solution.py:232
  64.5 3.4 %collective-permute-start.20 = (f32[32,4096]{1,0:T(8,128)S(1)}, f32[32,4096]{1,0:T(8,128)S(1)}, u32[]{:S(2)}, u32[]{:S(2)}) collective-permute-start(f32[32,4096]{1,0:T(8,128)S(1)} %collective-permute-done.12.refs_0_), channel_id=1, source_target_pairs={{0,63},{1,34},{2,33},{3,36},{4,35},{5,38},{6,37},{7,40},{8,39},{9,... | collective-permute-start | bytes 1572872 | tf_op jit(solution)/shard_map/ppermute | solution.py:260
  67.9 3.3 %collective-permute-done.16.refs_2_ = f32[32,4096]{1,0:T(8,128)S(1)} collective-permute-done((f32[32,4096]{1,0:T(8,128)S(1)}, f32[32,4096]{1,0:T(8,128)S(1)}, u32[]{:S(2)}, u32[]{:S(2)}) %collective-permute-start.16) | collective-permute-done | bytes 524320 | tf_op jit(solution)/shard_map/ppermute | solution.py:260
  71.5 4.2 %step_3.1.refs_7_ = f32[256,4096]{1,0:T(8,128)S(1)} custom-call(f32[32,4096]{1,0:T(8,128)S(1)} %collective-permute-done.5.refs_0_, f32[32,4096]{1,0:T(8,128)S(1)} %collective-permute-done.15.refs_1_, f32[32,4096]{1,0:T(8,128)S(1)} %collective-permute-done.16.refs_2_, ...), custom_call_target="tpu_custom_call", output_to_operand_aliasing={{}: (7, {})} | custom-call | flops 1048576 | bytes 65536 | tf_op jit(solution)/shard_map/step_3/pallas_call | solution.py:232
  75.7 3.5 %collective-permute-start.22 = (f32[32,4096]{1,0:T(8,128)S(1)}, f32[32,4096]{1,0:T(8,128)S(1)}, u32[]{:S(2)}, u32[]{:S(2)}) collective-permute-start(f32[32,4096]{1,0:T(8,128)S(1)} %collective-permute-done.11.refs_0_), channel_id=1, source_target_pairs={{0,63},{1,34},{2,33},{3,36},{4,35},{5,38},{6,37},{7,40},{8,39},{9,... | collective-permute-start | bytes 1572872 | tf_op jit(solution)/shard_map/ppermute | solution.py:260
  79.2 3.3 %collective-permute-done.20.refs_2_ = f32[32,4096]{1,0:T(8,128)S(1)} collective-permute-done((f32[32,4096]{1,0:T(8,128)S(1)}, f32[32,4096]{1,0:T(8,128)S(1)}, u32[]{:S(2)}, u32[]{:S(2)}) %collective-permute-start.20) | collective-permute-done | bytes 524320 | tf_op jit(solution)/shard_map/ppermute | solution.py:260
  82.7 5.0 %step_4.1.refs_7_ = f32[256,4096]{1,0:T(8,128)S(1)} custom-call(f32[32,4096]{1,0:T(8,128)S(1)} %collective-permute-done.12.refs_0_, f32[32,4096]{1,0:T(8,128)S(1)} %collective-permute-done.19.refs_1_, f32[32,4096]{1,0:T(8,128)S(1)} %collective-permute-done.20.refs_2_, ...), custom_call_target="tpu_custom_call", output_to_operand_aliasing={{}: (7, {})} | custom-call | flops 1048576 | bytes 65536 | tf_op jit(solution)/shard_map/step_4/pallas_call | solution.py:232
  87.8 3.5 %collective-permute-start.27 = (f32[32,4096]{1,0:T(8,128)S(1)}, f32[32,4096]{1,0:T(8,128)S(1)}, u32[]{:S(2)}, u32[]{:S(2)}) collective-permute-start(f32[32,4096]{1,0:T(8,128)S(1)} %collective-permute-done.18.refs_0_), channel_id=1, source_target_pairs={{0,63},{1,34},{2,33},{3,36},{4,35},{5,38},{6,37},{7,40},{8,39},{9,... | collective-permute-start | bytes 1572872 | tf_op jit(solution)/shard_map/ppermute | solution.py:260
  91.3 2.4 %collective-permute-done.22.refs_2_ = f32[32,4096]{1,0:T(8,128)S(1)} collective-permute-done((f32[32,4096]{1,0:T(8,128)S(1)}, f32[32,4096]{1,0:T(8,128)S(1)}, u32[]{:S(2)}, u32[]{:S(2)}) %collective-permute-start.22) | collective-permute-done | bytes 524320 | tf_op jit(solution)/shard_map/ppermute | solution.py:260
  94.1 5.0 %step_5.1.refs_7_ = f32[256,4096]{1,0:T(8,128)S(1)} custom-call(f32[32,4096]{1,0:T(8,128)S(1)} %collective-permute-done.11.refs_0_, f32[32,4096]{1,0:T(8,128)S(1)} %collective-permute-done.21.refs_1_, f32[32,4096]{1,0:T(8,128)S(1)} %collective-permute-done.22.refs_2_, ...), custom_call_target="tpu_custom_call", output_to_operand_aliasing={{}: (7, {})} | custom-call | flops 1048576 | bytes 65536 | tf_op jit(solution)/shard_map/step_5/pallas_call | solution.py:232
  99.3 3.6 %collective-permute-start.24 = (f32[16,4096]{1,0:T(8,128)S(1)}, f32[16,4096]{1,0:T(8,128)S(1)}, u32[]{:S(2)}, u32[]{:S(2)}) collective-permute-start(f32[16,4096]{1,0:T(8,128)S(1)} %slice.3), channel_id=1, source_target_pairs={{0,63},{1,34},{2,33},{3,36},{4,35},{5,38},{6,37},{7,40},{8,39},{9,... | collective-permute-start | bytes 786440 | tf_op jit(solution)/shard_map/ppermute | solution.py:260
  104.1 1.7 %collective-permute-done.26.refs_1_ = f32[32,4096]{1,0:T(8,128)S(1)} collective-permute-done((f32[32,4096]{1,0:T(8,128)S(1)}, f32[32,4096]{1,0:T(8,128)S(1)}, u32[]{:S(2)}, u32[]{:S(2)}) %collective-permute-start.26) | collective-permute-done | bytes 524320 | tf_op jit(solution)/shard_map/ppermute | solution.py:260
  105.7 2.8 %step_6.1.refs_8_ = f32[256,4096]{1,0:T(8,128)S(1)} custom-call(f32[32,4096]{1,0:T(8,128)S(1)} %collective-permute-done.18.refs_0_, f32[32,4096]{1,0:T(8,128)S(1)} %collective-permute-done.26.refs_1_, f32[32,4096]{1,0:T(8,128)S(1)} %collective-permute-done.27.refs_2_, ...), custom_call_target="tpu_custom_call", output_to_operand_aliasing={{}: (7, {})} | custom-call | flops 1048576 | bytes 65536 | tf_op jit(solution)/shard_map/step_6/pallas_call | solution.py:232
  108.6 2.8 %collective-permute-done.23.refs_1_ = f32[16,4096]{1,0:T(8,128)S(1)} collective-permute-done((f32[16,4096]{1,0:T(8,128)S(1)}, f32[16,4096]{1,0:T(8,128)S(1)}, u32[]{:S(2)}, u32[]{:S(2)}) %collective-permute-start.23) | collective-permute-done | bytes 262176 | tf_op jit(solution)/shard_map/ppermute | solution.py:260
  111.4 3.8 %step_7.1 = f32[256,4096]{1,0:T(8,128)} custom-call(f32[32,4096]{1,0:T(8,128)S(1)} %collective-permute-done.17.refs_0_, f32[16,4096]{1,0:T(8,128)S(1)} %collective-permute-done.23.refs_1_, f32[16,4096]{1,0:T(8,128)S(1)} %collective-permute-done.24.refs_2_, f32[32,4096]{1,0:T(8,128)S(1)} %collective-permute-done.25.refs_3_, ...), custom_call_target="tpu_custom_call" | custom-call | flops 1048576 | bytes 65536 | tf_op jit(solution)/shard_map/step_7/pallas_call | solution.py:232
  (56 shorter events, 12.9 us)
Async XLA Ops:
  0.0 22.5 %collective-permute-start.2 = (f32[8,32,4096]{2,1,0:T(8,128)}, f32[8,32,4096]{2,1,0:T(8,128)}, u32[]{:S(2)}, u32[]{:S(2)}) collective-permute-start(f32[8,32,4096]{2,1,0:T(8,128)} %param.3), channel_id=1, source_target_pairs={{0,1},{1,0},{2,3},{3,2},{4,5},{5,4},{6,7},{7,6},{8,9},{9,8},{10,11... | collective-permute-start | bytes 12582920 | tf_op jit(solution)/shard_map/ppermute | solution.py:260
  4.3 13.6 %collective-permute-start.1 = (f32[32,4096]{1,0:T(8,128)S(1)}, f32[32,4096]{1,0:T(8,128)S(1)}, u32[]{:S(2)}, u32[]{:S(2)}) collective-permute-start(f32[32,4096]{1,0:T(8,128)S(1)} %first_cuts.1), channel_id=1, source_target_pairs={{0,32},{1,33},{2,34},{3,35},{4,36},{5,37},{6,38},{7,39},{8,40},{9,... | collective-permute-start | bytes 1572872 | tf_op jit(solution)/shard_map/ppermute | solution.py:260
  7.5 28.0 %copy-start.5 = (f32[32,4096]{1,0:T(8,128)S(1)}, f32[32,4096]{1,0:T(8,128)}, u32[]{:S(2)}) copy-start(f32[32,4096]{1,0:T(8,128)} %get-tuple-element.66) | copy-start | bytes 1572868
  7.6 8.2 %collective-permute-start.3 = (f32[16,4096]{1,0:T(8,128)}, f32[16,4096]{1,0:T(8,128)S(1)}, u32[]{:S(2)}, u32[]{:S(2)}) collective-permute-start(f32[16,4096]{1,0:T(8,128)} %get-tuple-element.64), channel_id=1, source_target_pairs={{0,192},{1,193},{2,194},{3,195},{4,196},{5,197},{6,198},{7,199},{8... | collective-permute-start | bytes 786440 | tf_op jit(solution)/shard_map/ppermute | solution.py:260
  9.8 10.0 %collective-permute-start.4 = (f32[16,4096]{1,0:T(8,128)}, f32[16,4096]{1,0:T(8,128)S(1)}, u32[]{:S(2)}, u32[]{:S(2)}) collective-permute-start(f32[16,4096]{1,0:T(8,128)} %get-tuple-element.64), channel_id=1, source_target_pairs={{0,63},{1,34},{2,33},{3,36},{4,35},{5,38},{6,37},{7,40},{8,39},{9,... | collective-permute-start | bytes 786440 | tf_op jit(solution)/shard_map/ppermute | solution.py:260
  10.6 17.9 %collective-permute-start = (f32[32,4096]{1,0:T(8,128)}, f32[32,4096]{1,0:T(8,128)S(1)}, u32[]{:S(2)}, u32[]{:S(2)}) collective-permute-start(f32[32,4096]{1,0:T(8,128)} %get-tuple-element.60), channel_id=1, source_target_pairs={{0,32},{1,33},{2,34},{3,35},{4,36},{5,37},{6,38},{7,39},{8,40},{9,... | collective-permute-start | bytes 1572872 | tf_op jit(solution)/shard_map/ppermute | solution.py:260
  19.9 15.7 %collective-permute-start.8 = (f32[32,4096]{1,0:T(8,128)S(1)}, f32[32,4096]{1,0:T(8,128)S(1)}, u32[]{:S(2)}, u32[]{:S(2)}) collective-permute-start(f32[32,4096]{1,0:T(8,128)S(1)} %collective-permute-done.1.refs_0_), channel_id=1, source_target_pairs={{0,63},{1,34},{2,33},{3,36},{4,35},{5,38},{6,37},{7,40},{8,39},{9,... | collective-permute-start | bytes 1572872 | tf_op jit(solution)/shard_map/ppermute | solution.py:260
  20.7 14.9 %collective-permute-start.7 = (f32[32,4096]{1,0:T(8,128)S(1)}, f32[32,4096]{1,0:T(8,128)S(1)}, u32[]{:S(2)}, u32[]{:S(2)}) collective-permute-start(f32[32,4096]{1,0:T(8,128)S(1)} %collective-permute-done.1.refs_0_), channel_id=1, source_target_pairs={{0,64},{1,65},{2,66},{3,67},{4,68},{5,69},{6,70},{7,71},{8,72},{9,... | collective-permute-start | bytes 1572872 | tf_op jit(solution)/shard_map/ppermute | solution.py:260
  22.0 17.9 %collective-permute-start.6 = (f32[32,4096]{1,0:T(8,128)}, f32[32,4096]{1,0:T(8,128)S(1)}, u32[]{:S(2)}, u32[]{:S(2)}) collective-permute-start(f32[32,4096]{1,0:T(8,128)} %get-tuple-element.70), channel_id=1, source_target_pairs={{0,32},{1,33},{2,34},{3,35},{4,36},{5,37},{6,38},{7,39},{8,40},{9,... | collective-permute-start | bytes 1572872 | tf_op jit(solution)/shard_map/ppermute | solution.py:260
  28.6 18.2 %collective-permute-start.10 = (f32[32,4096]{1,0:T(8,128)S(1)}, f32[32,4096]{1,0:T(8,128)S(1)}, u32[]{:S(2)}, u32[]{:S(2)}) collective-permute-start(f32[32,4096]{1,0:T(8,128)S(1)} %collective-permute-done.refs_0_), channel_id=1, source_target_pairs={{0,63},{1,34},{2,33},{3,36},{4,35},{5,38},{6,37},{7,40},{8,39},{9,... | collective-permute-start | bytes 1572872 | tf_op jit(solution)/shard_map/ppermute | solution.py:260
  31.1 18.0 %collective-permute-start.9 = (f32[32,4096]{1,0:T(8,128)S(1)}, f32[32,4096]{1,0:T(8,128)S(1)}, u32[]{:S(2)}, u32[]{:S(2)}) collective-permute-start(f32[32,4096]{1,0:T(8,128)S(1)} %collective-permute-done.refs_0_), channel_id=1, source_target_pairs={{0,64},{1,65},{2,66},{3,67},{4,68},{5,69},{6,70},{7,71},{8,72},{9,... | collective-permute-start | bytes 1572872 | tf_op jit(solution)/shard_map/ppermute | solution.py:260
  35.6 17.6 %collective-permute-start.5 = (f32[32,4096]{1,0:T(8,128)S(1)}, f32[32,4096]{1,0:T(8,128)S(1)}, u32[]{:S(2)}, u32[]{:S(2)}) collective-permute-start(f32[32,4096]{1,0:T(8,128)S(1)} %copy-done.5), channel_id=1, source_target_pairs={{0,32},{1,33},{2,34},{3,35},{4,36},{5,37},{6,38},{7,39},{8,40},{9,... | collective-permute-start | bytes 1572872 | tf_op jit(solution)/shard_map/ppermute | solution.py:260
  39.8 18.2 %collective-permute-start.14 = (f32[32,4096]{1,0:T(8,128)S(1)}, f32[32,4096]{1,0:T(8,128)S(1)}, u32[]{:S(2)}, u32[]{:S(2)}) collective-permute-start(f32[32,4096]{1,0:T(8,128)S(1)} %collective-permute-done.6.refs_0_), channel_id=1, source_target_pairs={{0,63},{1,34},{2,33},{3,36},{4,35},{5,38},{6,37},{7,40},{8,39},{9,... | collective-permute-start | bytes 1572872 | tf_op jit(solution)/shard_map/ppermute | solution.py:260
  42.2 18.1 %collective-permute-start.13 = (f32[32,4096]{1,0:T(8,128)S(1)}, f32[32,4096]{1,0:T(8,128)S(1)}, u32[]{:S(2)}, u32[]{:S(2)}) collective-permute-start(f32[32,4096]{1,0:T(8,128)S(1)} %collective-permute-done.6.refs_0_), channel_id=1, source_target_pairs={{0,64},{1,65},{2,66},{3,67},{4,68},{5,69},{6,70},{7,71},{8,72},{9,... | collective-permute-start | bytes 1572872 | tf_op jit(solution)/shard_map/ppermute | solution.py:260
  43.5 14.5 %copy-start.3 = (f32[32,4096]{1,0:T(8,128)S(1)}, f32[32,4096]{1,0:T(8,128)}, u32[]{:S(2)}) copy-start(f32[32,4096]{1,0:T(8,128)} %get-tuple-element.81) | copy-start | bytes 1572868
  46.8 17.6 %collective-permute-start.12 = (f32[32,4096]{1,0:T(8,128)S(1)}, f32[32,4096]{1,0:T(8,128)S(1)}, u32[]{:S(2)}, u32[]{:S(2)}) collective-permute-start(f32[32,4096]{1,0:T(8,128)S(1)} %copy-done.4), channel_id=1, source_target_pairs={{0,32},{1,33},{2,34},{3,35},{4,36},{5,37},{6,38},{7,39},{8,40},{9,... | collective-permute-start | bytes 1572872 | tf_op jit(solution)/shard_map/ppermute | solution.py:260
  53.2 18.0 %collective-permute-start.16 = (f32[32,4096]{1,0:T(8,128)S(1)}, f32[32,4096]{1,0:T(8,128)S(1)}, u32[]{:S(2)}, u32[]{:S(2)}) collective-permute-start(f32[32,4096]{1,0:T(8,128)S(1)} %collective-permute-done.5.refs_0_), channel_id=1, source_target_pairs={{0,63},{1,34},{2,33},{3,36},{4,35},{5,38},{6,37},{7,40},{8,39},{9,... | collective-permute-start | bytes 1572872 | tf_op jit(solution)/shard_map/ppermute | solution.py:260
  56.7 14.8 %collective-permute-start.15 = (f32[32,4096]{1,0:T(8,128)S(1)}, f32[32,4096]{1,0:T(8,128)S(1)}, u32[]{:S(2)}, u32[]{:S(2)}) collective-permute-start(f32[32,4096]{1,0:T(8,128)S(1)} %collective-permute-done.5.refs_0_), channel_id=1, source_target_pairs={{0,64},{1,65},{2,66},{3,67},{4,68},{5,69},{6,70},{7,71},{8,72},{9,... | collective-permute-start | bytes 1572872 | tf_op jit(solution)/shard_map/ppermute | solution.py:260
  56.7 14.6 %copy-start.2 = (f32[32,4096]{1,0:T(8,128)S(1)}, f32[32,4096]{1,0:T(8,128)}, u32[]{:S(2)}) copy-start(f32[32,4096]{1,0:T(8,128)} %get-tuple-element.94) | copy-start | bytes 1572868
  58.1 17.6 %collective-permute-start.11 = (f32[32,4096]{1,0:T(8,128)S(1)}, f32[32,4096]{1,0:T(8,128)S(1)}, u32[]{:S(2)}, u32[]{:S(2)}) collective-permute-start(f32[32,4096]{1,0:T(8,128)S(1)} %copy-done.3), channel_id=1, source_target_pairs={{0,32},{1,33},{2,34},{3,35},{4,36},{5,37},{6,38},{7,39},{8,40},{9,... | collective-permute-start | bytes 1572872 | tf_op jit(solution)/shard_map/ppermute | solution.py:260
  64.5 18.0 %collective-permute-start.20 = (f32[32,4096]{1,0:T(8,128)S(1)}, f32[32,4096]{1,0:T(8,128)S(1)}, u32[]{:S(2)}, u32[]{:S(2)}) collective-permute-start(f32[32,4096]{1,0:T(8,128)S(1)} %collective-permute-done.12.refs_0_), channel_id=1, source_target_pairs={{0,63},{1,34},{2,33},{3,36},{4,35},{5,38},{6,37},{7,40},{8,39},{9,... | collective-permute-start | bytes 1572872 | tf_op jit(solution)/shard_map/ppermute | solution.py:260
  67.9 14.8 %collective-permute-start.19 = (f32[32,4096]{1,0:T(8,128)S(1)}, f32[32,4096]{1,0:T(8,128)S(1)}, u32[]{:S(2)}, u32[]{:S(2)}) collective-permute-start(f32[32,4096]{1,0:T(8,128)S(1)} %collective-permute-done.12.refs_0_), channel_id=1, source_target_pairs={{0,64},{1,65},{2,66},{3,67},{4,68},{5,69},{6,70},{7,71},{8,72},{9,... | collective-permute-start | bytes 1572872 | tf_op jit(solution)/shard_map/ppermute | solution.py:260
  67.9 14.6 %copy-start.1 = (f32[32,4096]{1,0:T(8,128)S(1)}, f32[32,4096]{1,0:T(8,128)}, u32[]{:S(2)}) copy-start(f32[32,4096]{1,0:T(8,128)} %get-tuple-element.92) | copy-start | bytes 1572868
  71.2 16.5 %collective-permute-start.18 = (f32[32,4096]{1,0:T(8,128)S(1)}, f32[32,4096]{1,0:T(8,128)S(1)}, u32[]{:S(2)}, u32[]{:S(2)}) collective-permute-start(f32[32,4096]{1,0:T(8,128)S(1)} %copy-done.2), channel_id=1, source_target_pairs={{0,32},{1,33},{2,34},{3,35},{4,36},{5,37},{6,38},{7,39},{8,40},{9,... | collective-permute-start | bytes 1572872 | tf_op jit(solution)/shard_map/ppermute | solution.py:260
  75.7 18.0 %collective-permute-start.22 = (f32[32,4096]{1,0:T(8,128)S(1)}, f32[32,4096]{1,0:T(8,128)S(1)}, u32[]{:S(2)}, u32[]{:S(2)}) collective-permute-start(f32[32,4096]{1,0:T(8,128)S(1)} %collective-permute-done.11.refs_0_), channel_id=1, source_target_pairs={{0,63},{1,34},{2,33},{3,36},{4,35},{5,38},{6,37},{7,40},{8,39},{9,... | collective-permute-start | bytes 1572872 | tf_op jit(solution)/shard_map/ppermute | solution.py:260
  79.2 14.5 %collective-permute-start.21 = (f32[32,4096]{1,0:T(8,128)S(1)}, f32[32,4096]{1,0:T(8,128)S(1)}, u32[]{:S(2)}, u32[]{:S(2)}) collective-permute-start(f32[32,4096]{1,0:T(8,128)S(1)} %collective-permute-done.11.refs_0_), channel_id=1, source_target_pairs={{0,64},{1,65},{2,66},{3,67},{4,68},{5,69},{6,70},{7,71},{8,72},{9,... | collective-permute-start | bytes 1572872 | tf_op jit(solution)/shard_map/ppermute | solution.py:260
  82.5 16.7 %collective-permute-start.17 = (f32[32,4096]{1,0:T(8,128)S(1)}, f32[32,4096]{1,0:T(8,128)S(1)}, u32[]{:S(2)}, u32[]{:S(2)}) collective-permute-start(f32[32,4096]{1,0:T(8,128)S(1)} %copy-done.1), channel_id=1, source_target_pairs={{0,32},{1,33},{2,34},{3,35},{4,36},{5,37},{6,38},{7,39},{8,40},{9,... | collective-permute-start | bytes 1572872 | tf_op jit(solution)/shard_map/ppermute | solution.py:260
  87.8 16.3 %collective-permute-start.27 = (f32[32,4096]{1,0:T(8,128)S(1)}, f32[32,4096]{1,0:T(8,128)S(1)}, u32[]{:S(2)}, u32[]{:S(2)}) collective-permute-start(f32[32,4096]{1,0:T(8,128)S(1)} %collective-permute-done.18.refs_0_), channel_id=1, source_target_pairs={{0,63},{1,34},{2,33},{3,36},{4,35},{5,38},{6,37},{7,40},{8,39},{9,... | collective-permute-start | bytes 1572872 | tf_op jit(solution)/shard_map/ppermute | solution.py:260
  91.3 14.5 %collective-permute-start.26 = (f32[32,4096]{1,0:T(8,128)S(1)}, f32[32,4096]{1,0:T(8,128)S(1)}, u32[]{:S(2)}, u32[]{:S(2)}) collective-permute-start(f32[32,4096]{1,0:T(8,128)S(1)} %collective-permute-done.18.refs_0_), channel_id=1, source_target_pairs={{0,64},{1,65},{2,66},{3,67},{4,68},{5,69},{6,70},{7,71},{8,72},{9,... | collective-permute-start | bytes 1572872 | tf_op jit(solution)/shard_map/ppermute | solution.py:260
  93.7 17.7 %collective-permute-start.25 = (f32[32,4096]{1,0:T(8,128)S(1)}, f32[32,4096]{1,0:T(8,128)S(1)}, u32[]{:S(2)}, u32[]{:S(2)}) collective-permute-start(f32[32,4096]{1,0:T(8,128)S(1)} %constant_dynamic-update-slice_fusion), channel_id=1, source_target_pairs={{0,32},{1,33},{2,34},{3,35},{4,36},{5,37},{6,38},{7,39},{8,40},{9,... | collective-permute-start | bytes 1572872 | tf_op jit(solution)/shard_map/ppermute | solution.py:260
  99.2 12.2 %collective-permute-start.23 = (f32[16,4096]{1,0:T(8,128)S(1)}, f32[16,4096]{1,0:T(8,128)S(1)}, u32[]{:S(2)}, u32[]{:S(2)}) collective-permute-start(f32[16,4096]{1,0:T(8,128)S(1)} %slice.3), channel_id=1, source_target_pairs={{0,64},{1,65},{2,66},{3,67},{4,68},{5,69},{6,70},{7,71},{8,72},{9,... | collective-permute-start | bytes 786440 | tf_op jit(solution)/shard_map/ppermute | solution.py:260
  99.3 12.1 %collective-permute-start.24 = (f32[16,4096]{1,0:T(8,128)S(1)}, f32[16,4096]{1,0:T(8,128)S(1)}, u32[]{:S(2)}, u32[]{:S(2)}) collective-permute-start(f32[16,4096]{1,0:T(8,128)S(1)} %slice.3), channel_id=1, source_target_pairs={{0,63},{1,34},{2,33},{3,36},{4,35},{5,38},{6,37},{7,40},{8,39},{9,... | collective-permute-start | bytes 786440 | tf_op jit(solution)/shard_map/ppermute | solution.py:260
  (2 other events, 20.2 us)

commit v6 on v5

--- a/solution.py
+++ b/solution.py
@@ -111,13 +111,16 @@
         fetch(inner_ref.at[pl.ds(at, height)], inner_stage_ref, inner_sem).wait()
         others.append(inner_stage_ref)
     rows, width = high_ref.shape
-    extent = both_ref.shape[0] // 2
+    extent = sum(ref.shape[0] for ref in others)
+    triple = both_ref.shape[0] == 3 * extent
 
     def gather(at, cols, state):
         main, rest = state
         high, low = halves(jnp.concatenate([ref[:, cols] for ref in others], axis=0))
         both = jnp.concatenate([high, low], axis=0)
-        both_ref[:, cols] = both
+        both_ref[: 2 * extent, cols] = both
+        if triple:
+            both_ref[2 * extent :, cols] = high
         return main + mxu(high_ref[:, cols], both, NT), rest + mxu(low_ref[:, cols], high, NT)
 
     start = (jnp.zeros((rows, 2 * extent), jnp.float32), jnp.zeros((rows, extent), jnp.float32))
@@ -127,11 +130,14 @@
         [table_ref[row : row + 1, at : at + height] for row, at, height in gaps], axis=1
     )
     a_high, a_low = halves(integral / (gap_row_ref[...] + gap_col))
-    a_twice = jnp.concatenate([a_high, a_high], axis=1)
+    a_twice = jnp.concatenate([a_high, a_high] + [a_low] * triple, axis=1)
 
     def spread(at, cols, state):
         both = both_ref[:, cols]
-        gamma = start_ref[:, cols] + (mxu(a_twice, both) + mxu(a_low, both[:extent]))
+        gamma = mxu(a_twice, both)
+        if not triple:
+            gamma += mxu(a_low, both[:extent])
+        gamma += start_ref[:, cols]
         if final:
             stage_ref, sem = refs
             stage_ref[:, cols] = gamma
@@ -228,13 +234,14 @@
         scratch += [pltpu.VMEM((inner_rows[1], width), jnp.float32), pltpu.SemaphoreType.DMA]
     if final:
         scratch += [pltpu.VMEM((rows, width), jnp.float32), pltpu.SemaphoreType.DMA((width // PANEL,))]
+    pieces = 3 if 3 * extent <= rows else 2
     extra = [in_hbm(inner)] if inner_rows else []
     return pl.pallas_call(
         functools.partial(step_kernel, (len(others), inner_rows, gaps, final, unroll)),
         out_shape=(pltpu.HBM if final else pltpu.VMEM)((rows, width), jnp.float32),
         in_specs=[VMEM] * (len(others) + 5) + [HBM] * len(extra),
         out_specs=HBM if final else VMEM,
-        scratch_shapes=[pltpu.VMEM((2 * extent, width), jnp.bfloat16)] + scratch,
+        scratch_shapes=[pltpu.VMEM((pieces * extent, width), jnp.bfloat16)] + scratch,
         input_output_aliases={} if final else {len(others) + 4: 0},
         compiler_params=params(10),
         cost_estimate=pl.CostEstimate(flops=1 << 20, bytes_accessed=1 << 16, transcendentals=0),
@@ -323,15 +330,17 @@
         others = [near[k], far[k], outer[k]]
         rows = None
         if final:
-            others.append(late)
+            others = [far[k], outer[k], late]
             at = vir_block - early
-            gaps = [(k, 0, vir_block)]
-            gaps += [(k, which * vir_block + shift, early) for shift in (0, at) for which in (1, 2)]
+            gaps = [(k, which * vir_block + shift, early) for shift in (0, at) for which in (1, 2)]
         else:
             others = [held(other, *earlier) for other in others]
             height = INNER_ROWS[k] * vir_block
             rows = (inner_at, height) if height else None
             gaps = [(k, 0, 3 * vir_block)]
+            if k == count - 2:
+                others.append(near[k + 1])
+                gaps.append((k + 1, 0, vir_block))
             gaps += [(row, 3 * vir_block, vir_block) for row in range(inner_at // vir_block, (inner_at + height) // vir_block)]
             inner_at += height
         gamma = step_call(others, high, low, gap_row, table, gaps, begin, inner, rows, final, 4 if k > 3 else 2, "step_%d" % k)

time: 116 us -> 116 us (level)
  no operation moved by 1% of the time
where the time goes in v6:
time: 116 us; the launch traced here: 115 us
  Pallas kernels  42.7 us (37%)
  starting transfers between devices  41.2 us (36%)
  waiting for transfers between devices  29.5 us (25%)
  local copies, waits for them, and re-layouts  1.24 us (1%)
    ppermute x28, starting transfers between devices, moved(): return lax.ppermute(block, AXES, route)  41.2 us
    pallas_call x8, Pallas kernels, step_call(): pl.pallas_call(functools.partial(step_kernel, (len(others), inner_rows, g...  33.2 us
    ppermute x28, waiting for transfers between devices, moved(): return lax.ppermute(block, AXES, route)  29.5 us
    pallas_call x1, Pallas kernels, own_call(): pl.pallas_call(own_kernel, out_shape=(factor, factor, pltpu.VMEM((rows, w...  5.35 us
    pallas_call x1, Pallas kernels, split_call(): pl.pallas_call(functools.partial(split_kernel, [start for start, _ in ran...  3.13 us
  transfers between devices with their start and end apart: 28, of which 13 were waited for; matrix products, arithmetic and copies ran while one was open for 1% of the time, Pallas kernels for 34%

profile of v6, /device:TPU:1, one launch (start us, length us, event | category | flops | bytes accessed | tf_op | source)
XLA Modules:
  0.0 115.3 jit_solution(5812236827626483933)
XLA Ops:
  0.0 3.2 %collective-permute-start.2 = (f32[8,32,4096]{2,1,0:T(8,128)}, f32[8,32,4096]{2,1,0:T(8,128)}, u32[]{:S(2)}, u32[]{:S(2)}) collective-permute-start(f32[8,32,4096]{2,1,0:T(8,128)} %param.3), channel_id=1, source_target_pairs={{0,1},{1,0},{2,3},{3,2},{4,5},{5,4},{6,7},{7,6},{8,9},{9,8},{10,11... | collective-permute-start | bytes 12582920 | tf_op jit(solution)/shard_map/ppermute | solution.py:267
  4.4 3.1 %other_cuts.1 = (f32[32,4096]{1,0:T(8,128)}, f32[32,4096]{1,0:T(8,128)}, f32[32,4096]{1,0:T(8,128)}, f32[32,4096]{1,0:T(8,128)}, f32[32,4096]{1,0:T(8,128)}, /*i...) custom-call(f32[256,4096]{1,0:T(8,128)} %bitcast.4), custom_call_target="tpu_custom_call" | custom-call | flops 3221225472 | bytes 4194304 | tf_op jit(solution)/shard_map/other_cuts/pallas_call | solution.py:194
  7.6 2.3 %collective-permute-start.3 = (f32[16,4096]{1,0:T(8,128)}, f32[16,4096]{1,0:T(8,128)S(1)}, u32[]{:S(2)}, u32[]{:S(2)}) collective-permute-start(f32[16,4096]{1,0:T(8,128)} %get-tuple-element.64), channel_id=1, source_target_pairs={{0,192},{1,193},{2,194},{3,195},{4,196},{5,197},{6,198},{7,199},{8... | collective-permute-start | bytes 786440 | tf_op jit(solution)/shard_map/ppermute | solution.py:267
  10.6 1.8 %collective-permute-start = (f32[32,4096]{1,0:T(8,128)}, f32[32,4096]{1,0:T(8,128)S(1)}, u32[]{:S(2)}, u32[]{:S(2)}) collective-permute-start(f32[32,4096]{1,0:T(8,128)} %get-tuple-element.60), channel_id=1, source_target_pairs={{0,32},{1,33},{2,34},{3,35},{4,36},{5,37},{6,38},{7,39},{8,40},{9,... | collective-permute-start | bytes 1572872 | tf_op jit(solution)/shard_map/ppermute | solution.py:267
  13.6 2.1 %collective-permute-done.3 = f32[16,4096]{1,0:T(8,128)S(1)} collective-permute-done((f32[16,4096]{1,0:T(8,128)}, f32[16,4096]{1,0:T(8,128)S(1)}, u32[]{:S(2)}, u32[]{:S(2)}) %collective-permute-start.3) | collective-permute-done | bytes 262176 | tf_op jit(solution)/shard_map/ppermute | solution.py:267
  15.8 2.1 %collective-permute-done.1.refs_0_ = f32[32,4096]{1,0:T(8,128)S(1)} collective-permute-done((f32[32,4096]{1,0:T(8,128)S(1)}, f32[32,4096]{1,0:T(8,128)S(1)}, u32[]{:S(2)}, u32[]{:S(2)}) %collective-permute-start.1) | collective-permute-done | bytes 524320 | tf_op jit(solution)/shard_map/ppermute | solution.py:267
  18.0 1.9 %collective-permute-done.4 = f32[16,4096]{1,0:T(8,128)S(1)} collective-permute-done((f32[16,4096]{1,0:T(8,128)}, f32[16,4096]{1,0:T(8,128)S(1)}, u32[]{:S(2)}, u32[]{:S(2)}) %collective-permute-start.4) | collective-permute-done | bytes 262176 | tf_op jit(solution)/shard_map/ppermute | solution.py:267
  22.5 5.3 %own_block.1 = (bf16[256,4096]{1,0:T(8,128)(2,1)S(1)}, bf16[256,4096]{1,0:T(8,128)(2,1)S(1)}, f32[256,4096]{1,0:T(8,128)S(1)}) custom-call(f32[256,4096]{1,0:T(8,128)} %bitcast.5, f32[256,1]{1,0:T(8,128)S(1)} %sub.106.gap_row_ref.refs_5_.refs_6_, f32[1,256]{1,0:T(1,128)S(1)} %sub.93.gap_col_ref), custom_call_target="tpu_custom_call" | custom-call | flops 1048576 | bytes 65536 | tf_op jit(solution)/shard_map/own_block/pallas_call | solution.py:213
  28.6 2.4 %collective-permute-start.10 = (f32[32,4096]{1,0:T(8,128)S(1)}, f32[32,4096]{1,0:T(8,128)S(1)}, u32[]{:S(2)}, u32[]{:S(2)}) collective-permute-start(f32[32,4096]{1,0:T(8,128)S(1)} %collective-permute-done.refs_0_), channel_id=1, source_target_pairs={{0,63},{1,34},{2,33},{3,36},{4,35},{5,38},{6,37},{7,40},{8,39},{9,... | collective-permute-start | bytes 1572872 | tf_op jit(solution)/shard_map/ppermute | solution.py:267
  32.4 3.2 %collective-permute-done.8.refs_2_ = f32[32,4096]{1,0:T(8,128)S(1)} collective-permute-done((f32[32,4096]{1,0:T(8,128)S(1)}, f32[32,4096]{1,0:T(8,128)S(1)}, u32[]{:S(2)}, u32[]{:S(2)}) %collective-permute-start.8) | collective-permute-done | bytes 524320 | tf_op jit(solution)/shard_map/ppermute | solution.py:267
  35.6 4.2 %step_0.1.refs_7_ = f32[256,4096]{1,0:T(8,128)S(1)} custom-call(f32[32,4096]{1,0:T(8,128)S(1)} %collective-permute-done.1.refs_0_, f32[32,4096]{1,0:T(8,128)S(1)} %collective-permute-done.7.refs_1_, f32[32,4096]{1,0:T(8,128)S(1)} %collective-permute-done.8.refs_2_, ...), custom_call_target="tpu_custom_call", output_to_operand_aliasing={{}: (7, {})} | custom-call | flops 1048576 | bytes 65536 | tf_op jit(solution)/shard_map/step_0/pallas_call | solution.py:239
  39.8 2.4 %collective-permute-start.14 = (f32[32,4096]{1,0:T(8,128)S(1)}, f32[32,4096]{1,0:T(8,128)S(1)}, u32[]{:S(2)}, u32[]{:S(2)}) collective-permute-start(f32[32,4096]{1,0:T(8,128)S(1)} %collective-permute-done.6.refs_0_), channel_id=1, source_target_pairs={{0,63},{1,34},{2,33},{3,36},{4,35},{5,38},{6,37},{7,40},{8,39},{9,... | collective-permute-start | bytes 1572872 | tf_op jit(solution)/shard_map/ppermute | solution.py:267
  43.5 3.3 %collective-permute-done.10.refs_2_ = f32[32,4096]{1,0:T(8,128)S(1)} collective-permute-done((f32[32,4096]{1,0:T(8,128)S(1)}, f32[32,4096]{1,0:T(8,128)S(1)}, u32[]{:S(2)}, u32[]{:S(2)}) %collective-permute-start.10) | collective-permute-done | bytes 524320 | tf_op jit(solution)/shard_map/ppermute | solution.py:267
  46.8 2.2 %collective-permute-start.12 = (f32[32,4096]{1,0:T(8,128)S(1)}, f32[32,4096]{1,0:T(8,128)S(1)}, u32[]{:S(2)}, u32[]{:S(2)}) collective-permute-start(f32[32,4096]{1,0:T(8,128)S(1)} %copy-done.4), channel_id=1, source_target_pairs={{0,32},{1,33},{2,34},{3,35},{4,36},{5,37},{6,38},{7,39},{8,40},{9,... | collective-permute-start | bytes 1572872 | tf_op jit(solution)/shard_map/ppermute | solution.py:267
  49.0 4.2 %step_1.1.refs_7_ = f32[256,4096]{1,0:T(8,128)S(1)} custom-call(f32[32,4096]{1,0:T(8,128)S(1)} %collective-permute-done.refs_0_, f32[32,4096]{1,0:T(8,128)S(1)} %collective-permute-done.9.refs_1_, f32[32,4096]{1,0:T(8,128)S(1)} %collective-permute-done.10.refs_2_, ...), custom_call_target="tpu_custom_call", output_to_operand_aliasing={{}: (7, {})} | custom-call | flops 1048576 | bytes 65536 | tf_op jit(solution)/shard_map/step_1/pallas_call | solution.py:239
  53.2 3.5 %collective-permute-start.16 = (f32[32,4096]{1,0:T(8,128)S(1)}, f32[32,4096]{1,0:T(8,128)S(1)}, u32[]{:S(2)}, u32[]{:S(2)}) collective-permute-start(f32[32,4096]{1,0:T(8,128)S(1)} %collective-permute-done.5.refs_0_), channel_id=1, source_target_pairs={{0,63},{1,34},{2,33},{3,36},{4,35},{5,38},{6,37},{7,40},{8,39},{9,... | collective-permute-start | bytes 1572872 | tf_op jit(solution)/shard_map/ppermute | solution.py:267
  58.1 2.2 %collective-permute-start.11 = (f32[32,4096]{1,0:T(8,128)S(1)}, f32[32,4096]{1,0:T(8,128)S(1)}, u32[]{:S(2)}, u32[]{:S(2)}) collective-permute-start(f32[32,4096]{1,0:T(8,128)S(1)} %copy-done.3), channel_id=1, source_target_pairs={{0,32},{1,33},{2,34},{3,35},{4,36},{5,37},{6,38},{7,39},{8,40},{9,... | collective-permute-start | bytes 1572872 | tf_op jit(solution)/shard_map/ppermute | solution.py:267
  60.3 4.2 %step_2.1.refs_7_ = f32[256,4096]{1,0:T(8,128)S(1)} custom-call(f32[32,4096]{1,0:T(8,128)S(1)} %collective-permute-done.6.refs_0_, f32[32,4096]{1,0:T(8,128)S(1)} %collective-permute-done.13.refs_1_, f32[32,4096]{1,0:T(8,128)S(1)} %collective-permute-done.14.refs_2_, ...), custom_call_target="tpu_custom_call", output_to_operand_aliasing={{}: (7, {})} | custom-call | flops 1048576 | bytes 65536 | tf_op jit(solution)/shard_map/step_2/pallas_call | solution.py:239
  64.5 3.4 %collective-permute-start.20 = (f32[32,4096]{1,0:T(8,128)S(1)}, f32[32,4096]{1,0:T(8,128)S(1)}, u32[]{:S(2)}, u32[]{:S(2)}) collective-permute-start(f32[32,4096]{1,0:T(8,128)S(1)} %collective-permute-done.12.refs_0_), channel_id=1, source_target_pairs={{0,63},{1,34},{2,33},{3,36},{4,35},{5,38},{6,37},{7,40},{8,39},{9,... | collective-permute-start | bytes 1572872 | tf_op jit(solution)/shard_map/ppermute | solution.py:267
  67.9 3.3 %collective-permute-done.16.refs_2_ = f32[32,4096]{1,0:T(8,128)S(1)} collective-permute-done((f32[32,4096]{1,0:T(8,128)S(1)}, f32[32,4096]{1,0:T(8,128)S(1)}, u32[]{:S(2)}, u32[]{:S(2)}) %collective-permute-start.16) | collective-permute-done | bytes 524320 | tf_op jit(solution)/shard_map/ppermute | solution.py:267
  71.5 4.2 %step_3.1.refs_7_ = f32[256,4096]{1,0:T(8,128)S(1)} custom-call(f32[32,4096]{1,0:T(8,128)S(1)} %collective-permute-done.5.refs_0_, f32[32,4096]{1,0:T(8,128)S(1)} %collective-permute-done.15.refs_1_, f32[32,4096]{1,0:T(8,128)S(1)} %collective-permute-done.16.refs_2_, ...), custom_call_target="tpu_custom_call", output_to_operand_aliasing={{}: (7, {})} | custom-call | flops 1048576 | bytes 65536 | tf_op jit(solution)/shard_map/step_3/pallas_call | solution.py:239
  75.7 3.5 %collective-permute-start.22 = (f32[32,4096]{1,0:T(8,128)S(1)}, f32[32,4096]{1,0:T(8,128)S(1)}, u32[]{:S(2)}, u32[]{:S(2)}) collective-permute-start(f32[32,4096]{1,0:T(8,128)S(1)} %collective-permute-done.11.refs_0_), channel_id=1, source_target_pairs={{0,63},{1,34},{2,33},{3,36},{4,35},{5,38},{6,37},{7,40},{8,39},{9,... | collective-permute-start | bytes 1572872 | tf_op jit(solution)/shard_map/ppermute | solution.py:267
  79.2 3.3 %collective-permute-done.20.refs_2_ = f32[32,4096]{1,0:T(8,128)S(1)} collective-permute-done((f32[32,4096]{1,0:T(8,128)S(1)}, f32[32,4096]{1,0:T(8,128)S(1)}, u32[]{:S(2)}, u32[]{:S(2)}) %collective-permute-start.20) | collective-permute-done | bytes 524320 | tf_op jit(solution)/shard_map/ppermute | solution.py:267
  82.7 5.0 %step_4.1.refs_7_ = f32[256,4096]{1,0:T(8,128)S(1)} custom-call(f32[32,4096]{1,0:T(8,128)S(1)} %collective-permute-done.12.refs_0_, f32[32,4096]{1,0:T(8,128)S(1)} %collective-permute-done.19.refs_1_, f32[32,4096]{1,0:T(8,128)S(1)} %collective-permute-done.20.refs_2_, ...), custom_call_target="tpu_custom_call", output_to_operand_aliasing={{}: (7, {})} | custom-call | flops 1048576 | bytes 65536 | tf_op jit(solution)/shard_map/step_4/pallas_call | solution.py:239
  87.8 3.5 %collective-permute-start.27 = (f32[32,4096]{1,0:T(8,128)S(1)}, f32[32,4096]{1,0:T(8,128)S(1)}, u32[]{:S(2)}, u32[]{:S(2)}) collective-permute-start(f32[32,4096]{1,0:T(8,128)S(1)} %collective-permute-done.18.refs_0_), channel_id=1, source_target_pairs={{0,63},{1,34},{2,33},{3,36},{4,35},{5,38},{6,37},{7,40},{8,39},{9,... | collective-permute-start | bytes 1572872 | tf_op jit(solution)/shard_map/ppermute | solution.py:267
  91.3 2.4 %collective-permute-done.22.refs_2_ = f32[32,4096]{1,0:T(8,128)S(1)} collective-permute-done((f32[32,4096]{1,0:T(8,128)S(1)}, f32[32,4096]{1,0:T(8,128)S(1)}, u32[]{:S(2)}, u32[]{:S(2)}) %collective-permute-start.22) | collective-permute-done | bytes 524320 | tf_op jit(solution)/shard_map/ppermute | solution.py:267
  94.1 5.0 %step_5.1.refs_8_ = f32[256,4096]{1,0:T(8,128)S(1)} custom-call(f32[32,4096]{1,0:T(8,128)S(1)} %collective-permute-done.11.refs_0_, f32[32,4096]{1,0:T(8,128)S(1)} %collective-permute-done.21.refs_1_, f32[32,4096]{1,0:T(8,128)S(1)} %collective-permute-done.22.refs_2_, ...), custom_call_target="tpu_custom_call", output_to_operand_aliasing={{}: (7, {})} | custom-call | flops 1048576 | bytes 65536 | tf_op jit(solution)/shard_map/step_5/pallas_call | solution.py:239
  99.3 3.6 %collective-permute-start.24 = (f32[16,4096]{1,0:T(8,128)S(1)}, f32[16,4096]{1,0:T(8,128)S(1)}, u32[]{:S(2)}, u32[]{:S(2)}) collective-permute-start(f32[16,4096]{1,0:T(8,128)S(1)} %slice.3), channel_id=1, source_target_pairs={{0,63},{1,34},{2,33},{3,36},{4,35},{5,38},{6,37},{7,40},{8,39},{9,... | collective-permute-start | bytes 786440 | tf_op jit(solution)/shard_map/ppermute | solution.py:267
  104.1 1.7 %collective-permute-done.26.refs_1_ = f32[32,4096]{1,0:T(8,128)S(1)} collective-permute-done((f32[32,4096]{1,0:T(8,128)S(1)}, f32[32,4096]{1,0:T(8,128)S(1)}, u32[]{:S(2)}, u32[]{:S(2)}) %collective-permute-start.26) | collective-permute-done | bytes 524320 | tf_op jit(solution)/shard_map/ppermute | solution.py:267
  105.8 2.8 %step_6.1.refs_7_ = f32[256,4096]{1,0:T(8,128)S(1)} custom-call(f32[32,4096]{1,0:T(8,128)S(1)} %collective-permute-done.18.refs_0_, f32[32,4096]{1,0:T(8,128)S(1)} %collective-permute-done.26.refs_1_, f32[32,4096]{1,0:T(8,128)S(1)} %collective-permute-done.27.refs_2_, ...), custom_call_target="tpu_custom_call", output_to_operand_aliasing={{}: (8, {})} | custom-call | flops 1048576 | bytes 65536 | tf_op jit(solution)/shard_map/step_6/pallas_call | solution.py:239
  108.5 2.8 %collective-permute-done.23.refs_0_ = f32[16,4096]{1,0:T(8,128)S(1)} collective-permute-done((f32[16,4096]{1,0:T(8,128)S(1)}, f32[16,4096]{1,0:T(8,128)S(1)}, u32[]{:S(2)}, u32[]{:S(2)}) %collective-permute-start.23) | collective-permute-done | bytes 262176 | tf_op jit(solution)/shard_map/ppermute | solution.py:267
  111.4 3.7 %step_7.1 = f32[256,4096]{1,0:T(8,128)} custom-call(f32[16,4096]{1,0:T(8,128)S(1)} %collective-permute-done.23.refs_0_, f32[16,4096]{1,0:T(8,128)S(1)} %collective-permute-done.24.refs_1_, f32[32,4096]{1,0:T(8,128)S(1)} %collective-permute-done.25.refs_2_, bf16[256,4096]{1,0:T(8,128)(2,1)S(1)} %get-tuple-element.74.refs_3_.refs_4_, ...), custom_call_target="tpu_custom_call" | custom-call | flops 1048576 | bytes 65536 | tf_op jit(solution)/shard_map/step_7/pallas_call | solution.py:239
  (56 shorter events, 12.9 us)
Async XLA Ops:
  0.0 22.5 %collective-permute-start.2 = (f32[8,32,4096]{2,1,0:T(8,128)}, f32[8,32,4096]{2,1,0:T(8,128)}, u32[]{:S(2)}, u32[]{:S(2)}) collective-permute-start(f32[8,32,4096]{2,1,0:T(8,128)} %param.3), channel_id=1, source_target_pairs={{0,1},{1,0},{2,3},{3,2},{4,5},{5,4},{6,7},{7,6},{8,9},{9,8},{10,11... | collective-permute-start | bytes 12582920 | tf_op jit(solution)/shard_map/ppermute | solution.py:267
  4.3 13.6 %collective-permute-start.1 = (f32[32,4096]{1,0:T(8,128)S(1)}, f32[32,4096]{1,0:T(8,128)S(1)}, u32[]{:S(2)}, u32[]{:S(2)}) collective-permute-start(f32[32,4096]{1,0:T(8,128)S(1)} %first_cuts.1), channel_id=1, source_target_pairs={{0,32},{1,33},{2,34},{3,35},{4,36},{5,37},{6,38},{7,39},{8,40},{9,... | collective-permute-start | bytes 1572872 | tf_op jit(solution)/shard_map/ppermute | solution.py:267
  7.5 28.0 %copy-start.5 = (f32[32,4096]{1,0:T(8,128)S(1)}, f32[32,4096]{1,0:T(8,128)}, u32[]{:S(2)}) copy-start(f32[32,4096]{1,0:T(8,128)} %get-tuple-element.66) | copy-start | bytes 1572868
  7.6 8.2 %collective-permute-start.3 = (f32[16,4096]{1,0:T(8,128)}, f32[16,4096]{1,0:T(8,128)S(1)}, u32[]{:S(2)}, u32[]{:S(2)}) collective-permute-start(f32[16,4096]{1,0:T(8,128)} %get-tuple-element.64), channel_id=1, source_target_pairs={{0,192},{1,193},{2,194},{3,195},{4,196},{5,197},{6,198},{7,199},{8... | collective-permute-start | bytes 786440 | tf_op jit(solution)/shard_map/ppermute | solution.py:267
  9.8 10.0 %collective-permute-start.4 = (f32[16,4096]{1,0:T(8,128)}, f32[16,4096]{1,0:T(8,128)S(1)}, u32[]{:S(2)}, u32[]{:S(2)}) collective-permute-start(f32[16,4096]{1,0:T(8,128)} %get-tuple-element.64), channel_id=1, source_target_pairs={{0,63},{1,34},{2,33},{3,36},{4,35},{5,38},{6,37},{7,40},{8,39},{9,... | collective-permute-start | bytes 786440 | tf_op jit(solution)/shard_map/ppermute | solution.py:267
  10.6 17.9 %collective-permute-start = (f32[32,4096]{1,0:T(8,128)}, f32[32,4096]{1,0:T(8,128)S(1)}, u32[]{:S(2)}, u32[]{:S(2)}) collective-permute-start(f32[32,4096]{1,0:T(8,128)} %get-tuple-element.60), channel_id=1, source_target_pairs={{0,32},{1,33},{2,34},{3,35},{4,36},{5,37},{6,38},{7,39},{8,40},{9,... | collective-permute-start | bytes 1572872 | tf_op jit(solution)/shard_map/ppermute | solution.py:267
  19.9 15.7 %collective-permute-start.8 = (f32[32,4096]{1,0:T(8,128)S(1)}, f32[32,4096]{1,0:T(8,128)S(1)}, u32[]{:S(2)}, u32[]{:S(2)}) collective-permute-start(f32[32,4096]{1,0:T(8,128)S(1)} %collective-permute-done.1.refs_0_), channel_id=1, source_target_pairs={{0,63},{1,34},{2,33},{3,36},{4,35},{5,38},{6,37},{7,40},{8,39},{9,... | collective-permute-start | bytes 1572872 | tf_op jit(solution)/shard_map/ppermute | solution.py:267
  20.7 14.9 %collective-permute-start.7 = (f32[32,4096]{1,0:T(8,128)S(1)}, f32[32,4096]{1,0:T(8,128)S(1)}, u32[]{:S(2)}, u32[]{:S(2)}) collective-permute-start(f32[32,4096]{1,0:T(8,128)S(1)} %collective-permute-done.1.refs_0_), channel_id=1, source_target_pairs={{0,64},{1,65},{2,66},{3,67},{4,68},{5,69},{6,70},{7,71},{8,72},{9,... | collective-permute-start | bytes 1572872 | tf_op jit(solution)/shard_map/ppermute | solution.py:267
  22.0 17.9 %collective-permute-start.6 = (f32[32,4096]{1,0:T(8,128)}, f32[32,4096]{1,0:T(8,128)S(1)}, u32[]{:S(2)}, u32[]{:S(2)}) collective-permute-start(f32[32,4096]{1,0:T(8,128)} %get-tuple-element.70), channel_id=1, source_target_pairs={{0,32},{1,33},{2,34},{3,35},{4,36},{5,37},{6,38},{7,39},{8,40},{9,... | collective-permute-start | bytes 1572872 | tf_op jit(solution)/shard_map/ppermute | solution.py:267
  28.6 18.2 %collective-permute-start.10 = (f32[32,4096]{1,0:T(8,128)S(1)}, f32[32,4096]{1,0:T(8,128)S(1)}, u32[]{:S(2)}, u32[]{:S(2)}) collective-permute-start(f32[32,4096]{1,0:T(8,128)S(1)} %collective-permute-done.refs_0_), channel_id=1, source_target_pairs={{0,63},{1,34},{2,33},{3,36},{4,35},{5,38},{6,37},{7,40},{8,39},{9,... | collective-permute-start | bytes 1572872 | tf_op jit(solution)/shard_map/ppermute | solution.py:267
  31.1 18.0 %collective-permute-start.9 = (f32[32,4096]{1,0:T(8,128)S(1)}, f32[32,4096]{1,0:T(8,128)S(1)}, u32[]{:S(2)}, u32[]{:S(2)}) collective-permute-start(f32[32,4096]{1,0:T(8,128)S(1)} %collective-permute-done.refs_0_), channel_id=1, source_target_pairs={{0,64},{1,65},{2,66},{3,67},{4,68},{5,69},{6,70},{7,71},{8,72},{9,... | collective-permute-start | bytes 1572872 | tf_op jit(solution)/shard_map/ppermute | solution.py:267
  35.6 17.6 %collective-permute-start.5 = (f32[32,4096]{1,0:T(8,128)S(1)}, f32[32,4096]{1,0:T(8,128)S(1)}, u32[]{:S(2)}, u32[]{:S(2)}) collective-permute-start(f32[32,4096]{1,0:T(8,128)S(1)} %copy-done.5), channel_id=1, source_target_pairs={{0,32},{1,33},{2,34},{3,35},{4,36},{5,37},{6,38},{7,39},{8,40},{9,... | collective-permute-start | bytes 1572872 | tf_op jit(solution)/shard_map/ppermute | solution.py:267
  39.8 18.2 %collective-permute-start.14 = (f32[32,4096]{1,0:T(8,128)S(1)}, f32[32,4096]{1,0:T(8,128)S(1)}, u32[]{:S(2)}, u32[]{:S(2)}) collective-permute-start(f32[32,4096]{1,0:T(8,128)S(1)} %collective-permute-done.6.refs_0_), channel_id=1, source_target_pairs={{0,63},{1,34},{2,33},{3,36},{4,35},{5,38},{6,37},{7,40},{8,39},{9,... | collective-permute-start | bytes 1572872 | tf_op jit(solution)/shard_map/ppermute | solution.py:267
  42.2 18.1 %collective-permute-start.13 = (f32[32,4096]{1,0:T(8,128)S(1)}, f32[32,4096]{1,0:T(8,128)S(1)}, u32[]{:S(2)}, u32[]{:S(2)}) collective-permute-start(f32[32,4096]{1,0:T(8,128)S(1)} %collective-permute-done.6.refs_0_), channel_id=1, source_target_pairs={{0,64},{1,65},{2,66},{3,67},{4,68},{5,69},{6,70},{7,71},{8,72},{9,... | collective-permute-start | bytes 1572872 | tf_op jit(solution)/shard_map/ppermute | solution.py:267
  43.5 14.5 %copy-start.3 = (f32[32,4096]{1,0:T(8,128)S(1)}, f32[32,4096]{1,0:T(8,128)}, u32[]{:S(2)}) copy-start(f32[32,4096]{1,0:T(8,128)} %get-tuple-element.81) | copy-start | bytes 1572868
  46.8 17.6 %collective-permute-start.12 = (f32[32,4096]{1,0:T(8,128)S(1)}, f32[32,4096]{1,0:T(8,128)S(1)}, u32[]{:S(2)}, u32[]{:S(2)}) collective-permute-start(f32[32,4096]{1,0:T(8,128)S(1)} %copy-done.4), channel_id=1, source_target_pairs={{0,32},{1,33},{2,34},{3,35},{4,36},{5,37},{6,38},{7,39},{8,40},{9,... | collective-permute-start | bytes 1572872 | tf_op jit(solution)/shard_map/ppermute | solution.py:267
  53.2 18.0 %collective-permute-start.16 = (f32[32,4096]{1,0:T(8,128)S(1)}, f32[32,4096]{1,0:T(8,128)S(1)}, u32[]{:S(2)}, u32[]{:S(2)}) collective-permute-start(f32[32,4096]{1,0:T(8,128)S(1)} %collective-permute-done.5.refs_0_), channel_id=1, source_target_pairs={{0,63},{1,34},{2,33},{3,36},{4,35},{5,38},{6,37},{7,40},{8,39},{9,... | collective-permute-start | bytes 1572872 | tf_op jit(solution)/shard_map/ppermute | solution.py:267
  56.7 14.8 %collective-permute-start.15 = (f32[32,4096]{1,0:T(8,128)S(1)}, f32[32,4096]{1,0:T(8,128)S(1)}, u32[]{:S(2)}, u32[]{:S(2)}) collective-permute-start(f32[32,4096]{1,0:T(8,128)S(1)} %collective-permute-done.5.refs_0_), channel_id=1, source_target_pairs={{0,64},{1,65},{2,66},{3,67},{4,68},{5,69},{6,70},{7,71},{8,72},{9,... | collective-permute-start | bytes 1572872 | tf_op jit(solution)/shard_map/ppermute | solution.py:267
  56.7 14.6 %copy-start.2 = (f32[32,4096]{1,0:T(8,128)S(1)}, f32[32,4096]{1,0:T(8,128)}, u32[]{:S(2)}) copy-start(f32[32,4096]{1,0:T(8,128)} %get-tuple-element.94) | copy-start | bytes 1572868
  58.1 17.6 %collective-permute-start.11 = (f32[32,4096]{1,0:T(8,128)S(1)}, f32[32,4096]{1,0:T(8,128)S(1)}, u32[]{:S(2)}, u32[]{:S(2)}) collective-permute-start(f32[32,4096]{1,0:T(8,128)S(1)} %copy-done.3), channel_id=1, source_target_pairs={{0,32},{1,33},{2,34},{3,35},{4,36},{5,37},{6,38},{7,39},{8,40},{9,... | collective-permute-start | bytes 1572872 | tf_op jit(solution)/shard_map/ppermute | solution.py:267
  64.5 18.0 %collective-permute-start.20 = (f32[32,4096]{1,0:T(8,128)S(1)}, f32[32,4096]{1,0:T(8,128)S(1)}, u32[]{:S(2)}, u32[]{:S(2)}) collective-permute-start(f32[32,4096]{1,0:T(8,128)S(1)} %collective-permute-done.12.refs_0_), channel_id=1, source_target_pairs={{0,63},{1,34},{2,33},{3,36},{4,35},{5,38},{6,37},{7,40},{8,39},{9,... | collective-permute-start | bytes 1572872 | tf_op jit(solution)/shard_map/ppermute | solution.py:267
  67.9 14.8 %collective-permute-start.19 = (f32[32,4096]{1,0:T(8,128)S(1)}, f32[32,4096]{1,0:T(8,128)S(1)}, u32[]{:S(2)}, u32[]{:S(2)}) collective-permute-start(f32[32,4096]{1,0:T(8,128)S(1)} %collective-permute-done.12.refs_0_), channel_id=1, source_target_pairs={{0,64},{1,65},{2,66},{3,67},{4,68},{5,69},{6,70},{7,71},{8,72},{9,... | collective-permute-start | bytes 1572872 | tf_op jit(solution)/shard_map/ppermute | solution.py:267
  67.9 14.6 %copy-start.1 = (f32[32,4096]{1,0:T(8,128)S(1)}, f32[32,4096]{1,0:T(8,128)}, u32[]{:S(2)}) copy-start(f32[32,4096]{1,0:T(8,128)} %get-tuple-element.92) | copy-start | bytes 1572868
  71.2 16.5 %collective-permute-start.18 = (f32[32,4096]{1,0:T(8,128)S(1)}, f32[32,4096]{1,0:T(8,128)S(1)}, u32[]{:S(2)}, u32[]{:S(2)}) collective-permute-start(f32[32,4096]{1,0:T(8,128)S(1)} %copy-done.2), channel_id=1, source_target_pairs={{0,32},{1,33},{2,34},{3,35},{4,36},{5,37},{6,38},{7,39},{8,40},{9,... | collective-permute-start | bytes 1572872 | tf_op jit(solution)/shard_map/ppermute | solution.py:267
  75.7 18.0 %collective-permute-start.22 = (f32[32,4096]{1,0:T(8,128)S(1)}, f32[32,4096]{1,0:T(8,128)S(1)}, u32[]{:S(2)}, u32[]{:S(2)}) collective-permute-start(f32[32,4096]{1,0:T(8,128)S(1)} %collective-permute-done.11.refs_0_), channel_id=1, source_target_pairs={{0,63},{1,34},{2,33},{3,36},{4,35},{5,38},{6,37},{7,40},{8,39},{9,... | collective-permute-start | bytes 1572872 | tf_op jit(solution)/shard_map/ppermute | solution.py:267
  79.2 14.5 %collective-permute-start.21 = (f32[32,4096]{1,0:T(8,128)S(1)}, f32[32,4096]{1,0:T(8,128)S(1)}, u32[]{:S(2)}, u32[]{:S(2)}) collective-permute-start(f32[32,4096]{1,0:T(8,128)S(1)} %collective-permute-done.11.refs_0_), channel_id=1, source_target_pairs={{0,64},{1,65},{2,66},{3,67},{4,68},{5,69},{6,70},{7,71},{8,72},{9,... | collective-permute-start | bytes 1572872 | tf_op jit(solution)/shard_map/ppermute | solution.py:267
  82.5 16.7 %collective-permute-start.17 = (f32[32,4096]{1,0:T(8,128)S(1)}, f32[32,4096]{1,0:T(8,128)S(1)}, u32[]{:S(2)}, u32[]{:S(2)}) collective-permute-start(f32[32,4096]{1,0:T(8,128)S(1)} %copy-done.1), channel_id=1, source_target_pairs={{0,32},{1,33},{2,34},{3,35},{4,36},{5,37},{6,38},{7,39},{8,40},{9,... | collective-permute-start | bytes 1572872 | tf_op jit(solution)/shard_map/ppermute | solution.py:267
  87.8 16.3 %collective-permute-start.27 = (f32[32,4096]{1,0:T(8,128)S(1)}, f32[32,4096]{1,0:T(8,128)S(1)}, u32[]{:S(2)}, u32[]{:S(2)}) collective-permute-start(f32[32,4096]{1,0:T(8,128)S(1)} %collective-permute-done.18.refs_0_), channel_id=1, source_target_pairs={{0,63},{1,34},{2,33},{3,36},{4,35},{5,38},{6,37},{7,40},{8,39},{9,... | collective-permute-start | bytes 1572872 | tf_op jit(solution)/shard_map/ppermute | solution.py:267
  91.3 14.5 %collective-permute-start.26 = (f32[32,4096]{1,0:T(8,128)S(1)}, f32[32,4096]{1,0:T(8,128)S(1)}, u32[]{:S(2)}, u32[]{:S(2)}) collective-permute-start(f32[32,4096]{1,0:T(8,128)S(1)} %collective-permute-done.18.refs_0_), channel_id=1, source_target_pairs={{0,64},{1,65},{2,66},{3,67},{4,68},{5,69},{6,70},{7,71},{8,72},{9,... | collective-permute-start | bytes 1572872 | tf_op jit(solution)/shard_map/ppermute | solution.py:267
  93.7 17.7 %collective-permute-start.25 = (f32[32,4096]{1,0:T(8,128)S(1)}, f32[32,4096]{1,0:T(8,128)S(1)}, u32[]{:S(2)}, u32[]{:S(2)}) collective-permute-start(f32[32,4096]{1,0:T(8,128)S(1)} %constant_dynamic-update-slice_fusion), channel_id=1, source_target_pairs={{0,32},{1,33},{2,34},{3,35},{4,36},{5,37},{6,38},{7,39},{8,40},{9,... | collective-permute-start | bytes 1572872 | tf_op jit(solution)/shard_map/ppermute | solution.py:267
  99.2 12.2 %collective-permute-start.23 = (f32[16,4096]{1,0:T(8,128)S(1)}, f32[16,4096]{1,0:T(8,128)S(1)}, u32[]{:S(2)}, u32[]{:S(2)}) collective-permute-start(f32[16,4096]{1,0:T(8,128)S(1)} %slice.3), channel_id=1, source_target_pairs={{0,64},{1,65},{2,66},{3,67},{4,68},{5,69},{6,70},{7,71},{8,72},{9,... | collective-permute-start | bytes 786440 | tf_op jit(solution)/shard_map/ppermute | solution.py:267
  99.3 12.1 %collective-permute-start.24 = (f32[16,4096]{1,0:T(8,128)S(1)}, f32[16,4096]{1,0:T(8,128)S(1)}, u32[]{:S(2)}, u32[]{:S(2)}) collective-permute-start(f32[16,4096]{1,0:T(8,128)S(1)} %slice.3), channel_id=1, source_target_pairs={{0,63},{1,34},{2,33},{3,36},{4,35},{5,38},{6,37},{7,40},{8,39},{9,... | collective-permute-start | bytes 786440 | tf_op jit(solution)/shard_map/ppermute | solution.py:267
  (2 other events, 20.2 us)

commit v7 on v6

--- a/solution.py
+++ b/solution.py
@@ -113,6 +113,7 @@
     rows, width = high_ref.shape
     extent = sum(ref.shape[0] for ref in others)
     triple = both_ref.shape[0] == 3 * extent
+    row_halves = pl.ds(0, rows // 2), pl.ds(rows // 2, rows // 2)
 
     def gather(at, cols, state):
         main, rest = state
@@ -141,7 +142,8 @@
         if final:
             stage_ref, sem = refs
             stage_ref[:, cols] = gamma
-            fetch(stage_ref.at[:, cols], gamma_ref.at[:, cols], sem.at[at])
+            for half, piece in enumerate(row_halves):
+                fetch(stage_ref.at[piece, cols], gamma_ref.at[piece, cols], sem.at[2 * at + half])
         else:
             gamma_ref[:, cols] = gamma
         return state
@@ -150,7 +152,10 @@
     if final:
         stage_ref, sem = refs
         for at, cols in enumerate(panels(width)):
-            pltpu.make_async_copy(stage_ref.at[:, cols], gamma_ref.at[:, cols], sem.at[at]).wait()
+            for half, piece in enumerate(row_halves):
+                pltpu.make_async_copy(
+                    stage_ref.at[piece, cols], gamma_ref.at[piece, cols], sem.at[2 * at + half]
+                ).wait()
 
 
 VMEM = pl.BlockSpec(memory_space=pltpu.VMEM)
@@ -233,7 +238,7 @@
         extent += inner_rows[1]
         scratch += [pltpu.VMEM((inner_rows[1], width), jnp.float32), pltpu.SemaphoreType.DMA]
     if final:
-        scratch += [pltpu.VMEM((rows, width), jnp.float32), pltpu.SemaphoreType.DMA((width // PANEL,))]
+        scratch += [pltpu.VMEM((rows, width), jnp.float32), pltpu.SemaphoreType.DMA((2 * width // PANEL,))]
     pieces = 3 if 3 * extent <= rows else 2
     extra = [in_hbm(inner)] if inner_rows else []
     return pl.pallas_call(

time: 116 us -> 116 us (level)
  no operation moved by 1% of the time
where the time goes in v7:
time: 116 us; the launch traced here: 115 us
  Pallas kernels  42.8 us (37%)
  starting transfers between devices  41.2 us (36%)
  waiting for transfers between devices  29.5 us (25%)
  local copies, waits for them, and re-layouts  1.24 us (1%)
    ppermute x28, starting transfers between devices, moved(): return lax.ppermute(block, AXES, route)  41.2 us
    pallas_call x8, Pallas kernels, step_call(): pl.pallas_call(functools.partial(step_kernel, (len(others), inner_rows, g...  33.2 us
    ppermute x28, waiting for transfers between devices, moved(): return lax.ppermute(block, AXES, route)  29.5 us
    pallas_call x1, Pallas kernels, own_call(): pl.pallas_call(own_kernel, out_shape=(factor, factor, pltpu.VMEM((rows, w...  5.35 us
    pallas_call x1, Pallas kernels, split_call(): pl.pallas_call(functools.partial(split_kernel, [start for start, _ in ran...  3.13 us
  transfers between devices with their start and end apart: 28, of which 13 were waited for; matrix products, arithmetic and copies ran while one was open for 1% of the time, Pallas kernels for 34%

profile of v7, /device:TPU:1, one launch (start us, length us, event | category | flops | bytes accessed | tf_op | source)
XLA Modules:
  0.0 115.3 jit_solution(17074671161513933922)
XLA Ops:
  0.0 3.2 %collective-permute-start.2 = (f32[8,32,4096]{2,1,0:T(8,128)}, f32[8,32,4096]{2,1,0:T(8,128)}, u32[]{:S(2)}, u32[]{:S(2)}) collective-permute-start(f32[8,32,4096]{2,1,0:T(8,128)} %param.3), channel_id=1, source_target_pairs={{0,1},{1,0},{2,3},{3,2},{4,5},{5,4},{6,7},{7,6},{8,9},{9,8},{10,11... | collective-permute-start | bytes 12582920 | tf_op jit(solution)/shard_map/ppermute | solution.py:272
  4.4 3.1 %other_cuts.1 = (f32[32,4096]{1,0:T(8,128)}, f32[32,4096]{1,0:T(8,128)}, f32[32,4096]{1,0:T(8,128)}, f32[32,4096]{1,0:T(8,128)}, f32[32,4096]{1,0:T(8,128)}, /*i...) custom-call(f32[256,4096]{1,0:T(8,128)} %bitcast.4), custom_call_target="tpu_custom_call" | custom-call | flops 3221225472 | bytes 4194304 | tf_op jit(solution)/shard_map/other_cuts/pallas_call | solution.py:199
  7.6 2.3 %collective-permute-start.3 = (f32[16,4096]{1,0:T(8,128)}, f32[16,4096]{1,0:T(8,128)S(1)}, u32[]{:S(2)}, u32[]{:S(2)}) collective-permute-start(f32[16,4096]{1,0:T(8,128)} %get-tuple-element.64), channel_id=1, source_target_pairs={{0,192},{1,193},{2,194},{3,195},{4,196},{5,197},{6,198},{7,199},{8... | collective-permute-start | bytes 786440 | tf_op jit(solution)/shard_map/ppermute | solution.py:272
  10.6 1.8 %collective-permute-start = (f32[32,4096]{1,0:T(8,128)}, f32[32,4096]{1,0:T(8,128)S(1)}, u32[]{:S(2)}, u32[]{:S(2)}) collective-permute-start(f32[32,4096]{1,0:T(8,128)} %get-tuple-element.60), channel_id=1, source_target_pairs={{0,32},{1,33},{2,34},{3,35},{4,36},{5,37},{6,38},{7,39},{8,40},{9,... | collective-permute-start | bytes 1572872 | tf_op jit(solution)/shard_map/ppermute | solution.py:272
  13.6 2.1 %collective-permute-done.3 = f32[16,4096]{1,0:T(8,128)S(1)} collective-permute-done((f32[16,4096]{1,0:T(8,128)}, f32[16,4096]{1,0:T(8,128)S(1)}, u32[]{:S(2)}, u32[]{:S(2)}) %collective-permute-start.3) | collective-permute-done | bytes 262176 | tf_op jit(solution)/shard_map/ppermute | solution.py:272
  15.8 2.1 %collective-permute-done.1.refs_0_ = f32[32,4096]{1,0:T(8,128)S(1)} collective-permute-done((f32[32,4096]{1,0:T(8,128)S(1)}, f32[32,4096]{1,0:T(8,128)S(1)}, u32[]{:S(2)}, u32[]{:S(2)}) %collective-permute-start.1) | collective-permute-done | bytes 524320 | tf_op jit(solution)/shard_map/ppermute | solution.py:272
  18.0 1.9 %collective-permute-done.4 = f32[16,4096]{1,0:T(8,128)S(1)} collective-permute-done((f32[16,4096]{1,0:T(8,128)}, f32[16,4096]{1,0:T(8,128)S(1)}, u32[]{:S(2)}, u32[]{:S(2)}) %collective-permute-start.4) | collective-permute-done | bytes 262176 | tf_op jit(solution)/shard_map/ppermute | solution.py:272
  22.5 5.3 %own_block.1 = (bf16[256,4096]{1,0:T(8,128)(2,1)S(1)}, bf16[256,4096]{1,0:T(8,128)(2,1)S(1)}, f32[256,4096]{1,0:T(8,128)S(1)}) custom-call(f32[256,4096]{1,0:T(8,128)} %bitcast.5, f32[256,1]{1,0:T(8,128)S(1)} %sub.106.gap_row_ref.refs_5_.refs_6_, f32[1,256]{1,0:T(1,128)S(1)} %sub.93.gap_col_ref), custom_call_target="tpu_custom_call" | custom-call | flops 1048576 | bytes 65536 | tf_op jit(solution)/shard_map/own_block/pallas_call | solution.py:218
  28.6 2.4 %collective-permute-start.10 = (f32[32,4096]{1,0:T(8,128)S(1)}, f32[32,4096]{1,0:T(8,128)S(1)}, u32[]{:S(2)}, u32[]{:S(2)}) collective-permute-start(f32[32,4096]{1,0:T(8,128)S(1)} %collective-permute-done.refs_0_), channel_id=1, source_target_pairs={{0,63},{1,34},{2,33},{3,36},{4,35},{5,38},{6,37},{7,40},{8,39},{9,... | collective-permute-start | bytes 1572872 | tf_op jit(solution)/shard_map/ppermute | solution.py:272
  32.4 3.2 %collective-permute-done.8.refs_2_ = f32[32,4096]{1,0:T(8,128)S(1)} collective-permute-done((f32[32,4096]{1,0:T(8,128)S(1)}, f32[32,4096]{1,0:T(8,128)S(1)}, u32[]{:S(2)}, u32[]{:S(2)}) %collective-permute-start.8) | collective-permute-done | bytes 524320 | tf_op jit(solution)/shard_map/ppermute | solution.py:272
  35.6 4.2 %step_0.1.refs_7_ = f32[256,4096]{1,0:T(8,128)S(1)} custom-call(f32[32,4096]{1,0:T(8,128)S(1)} %collective-permute-done.1.refs_0_, f32[32,4096]{1,0:T(8,128)S(1)} %collective-permute-done.7.refs_1_, f32[32,4096]{1,0:T(8,128)S(1)} %collective-permute-done.8.refs_2_, ...), custom_call_target="tpu_custom_call", output_to_operand_aliasing={{}: (7, {})} | custom-call | flops 1048576 | bytes 65536 | tf_op jit(solution)/shard_map/step_0/pallas_call | solution.py:244
  39.8 2.4 %collective-permute-start.14 = (f32[32,4096]{1,0:T(8,128)S(1)}, f32[32,4096]{1,0:T(8,128)S(1)}, u32[]{:S(2)}, u32[]{:S(2)}) collective-permute-start(f32[32,4096]{1,0:T(8,128)S(1)} %collective-permute-done.6.refs_0_), channel_id=1, source_target_pairs={{0,63},{1,34},{2,33},{3,36},{4,35},{5,38},{6,37},{7,40},{8,39},{9,... | collective-permute-start | bytes 1572872 | tf_op jit(solution)/shard_map/ppermute | solution.py:272
  43.5 3.3 %collective-permute-done.10.refs_2_ = f32[32,4096]{1,0:T(8,128)S(1)} collective-permute-done((f32[32,4096]{1,0:T(8,128)S(1)}, f32[32,4096]{1,0:T(8,128)S(1)}, u32[]{:S(2)}, u32[]{:S(2)}) %collective-permute-start.10) | collective-permute-done | bytes 524320 | tf_op jit(solution)/shard_map/ppermute | solution.py:272
  46.8 2.2 %collective-permute-start.12 = (f32[32,4096]{1,0:T(8,128)S(1)}, f32[32,4096]{1,0:T(8,128)S(1)}, u32[]{:S(2)}, u32[]{:S(2)}) collective-permute-start(f32[32,4096]{1,0:T(8,128)S(1)} %copy-done.4), channel_id=1, source_target_pairs={{0,32},{1,33},{2,34},{3,35},{4,36},{5,37},{6,38},{7,39},{8,40},{9,... | collective-permute-start | bytes 1572872 | tf_op jit(solution)/shard_map/ppermute | solution.py:272
  49.0 4.2 %step_1.1.refs_7_ = f32[256,4096]{1,0:T(8,128)S(1)} custom-call(f32[32,4096]{1,0:T(8,128)S(1)} %collective-permute-done.refs_0_, f32[32,4096]{1,0:T(8,128)S(1)} %collective-permute-done.9.refs_1_, f32[32,4096]{1,0:T(8,128)S(1)} %collective-permute-done.10.refs_2_, ...), custom_call_target="tpu_custom_call", output_to_operand_aliasing={{}: (7, {})} | custom-call | flops 1048576 | bytes 65536 | tf_op jit(solution)/shard_map/step_1/pallas_call | solution.py:244
  53.2 3.5 %collective-permute-start.16 = (f32[32,4096]{1,0:T(8,128)S(1)}, f32[32,4096]{1,0:T(8,128)S(1)}, u32[]{:S(2)}, u32[]{:S(2)}) collective-permute-start(f32[32,4096]{1,0:T(8,128)S(1)} %collective-permute-done.5.refs_0_), channel_id=1, source_target_pairs={{0,63},{1,34},{2,33},{3,36},{4,35},{5,38},{6,37},{7,40},{8,39},{9,... | collective-permute-start | bytes 1572872 | tf_op jit(solution)/shard_map/ppermute | solution.py:272
  58.1 2.2 %collective-permute-start.11 = (f32[32,4096]{1,0:T(8,128)S(1)}, f32[32,4096]{1,0:T(8,128)S(1)}, u32[]{:S(2)}, u32[]{:S(2)}) collective-permute-start(f32[32,4096]{1,0:T(8,128)S(1)} %copy-done.3), channel_id=1, source_target_pairs={{0,32},{1,33},{2,34},{3,35},{4,36},{5,37},{6,38},{7,39},{8,40},{9,... | collective-permute-start | bytes 1572872 | tf_op jit(solution)/shard_map/ppermute | solution.py:272
  60.3 4.2 %step_2.1.refs_7_ = f32[256,4096]{1,0:T(8,128)S(1)} custom-call(f32[32,4096]{1,0:T(8,128)S(1)} %collective-permute-done.6.refs_0_, f32[32,4096]{1,0:T(8,128)S(1)} %collective-permute-done.13.refs_1_, f32[32,4096]{1,0:T(8,128)S(1)} %collective-permute-done.14.refs_2_, ...), custom_call_target="tpu_custom_call", output_to_operand_aliasing={{}: (7, {})} | custom-call | flops 1048576 | bytes 65536 | tf_op jit(solution)/shard_map/step_2/pallas_call | solution.py:244
  64.5 3.4 %collective-permute-start.20 = (f32[32,4096]{1,0:T(8,128)S(1)}, f32[32,4096]{1,0:T(8,128)S(1)}, u32[]{:S(2)}, u32[]{:S(2)}) collective-permute-start(f32[32,4096]{1,0:T(8,128)S(1)} %collective-permute-done.12.refs_0_), channel_id=1, source_target_pairs={{0,63},{1,34},{2,33},{3,36},{4,35},{5,38},{6,37},{7,40},{8,39},{9,... | collective-permute-start | bytes 1572872 | tf_op jit(solution)/shard_map/ppermute | solution.py:272
  67.9 3.3 %collective-permute-done.16.refs_2_ = f32[32,4096]{1,0:T(8,128)S(1)} collective-permute-done((f32[32,4096]{1,0:T(8,128)S(1)}, f32[32,4096]{1,0:T(8,128)S(1)}, u32[]{:S(2)}, u32[]{:S(2)}) %collective-permute-start.16) | collective-permute-done | bytes 524320 | tf_op jit(solution)/shard_map/ppermute | solution.py:272
  71.5 4.2 %step_3.1.refs_7_ = f32[256,4096]{1,0:T(8,128)S(1)} custom-call(f32[32,4096]{1,0:T(8,128)S(1)} %collective-permute-done.5.refs_0_, f32[32,4096]{1,0:T(8,128)S(1)} %collective-permute-done.15.refs_1_, f32[32,4096]{1,0:T(8,128)S(1)} %collective-permute-done.16.refs_2_, ...), custom_call_target="tpu_custom_call", output_to_operand_aliasing={{}: (7, {})} | custom-call | flops 1048576 | bytes 65536 | tf_op jit(solution)/shard_map/step_3/pallas_call | solution.py:244
  75.7 3.5 %collective-permute-start.22 = (f32[32,4096]{1,0:T(8,128)S(1)}, f32[32,4096]{1,0:T(8,128)S(1)}, u32[]{:S(2)}, u32[]{:S(2)}) collective-permute-start(f32[32,4096]{1,0:T(8,128)S(1)} %collective-permute-done.11.refs_0_), channel_id=1, source_target_pairs={{0,63},{1,34},{2,33},{3,36},{4,35},{5,38},{6,37},{7,40},{8,39},{9,... | collective-permute-start | bytes 1572872 | tf_op jit(solution)/shard_map/ppermute | solution.py:272
  79.2 3.3 %collective-permute-done.20.refs_2_ = f32[32,4096]{1,0:T(8,128)S(1)} collective-permute-done((f32[32,4096]{1,0:T(8,128)S(1)}, f32[32,4096]{1,0:T(8,128)S(1)}, u32[]{:S(2)}, u32[]{:S(2)}) %collective-permute-start.20) | collective-permute-done | bytes 524320 | tf_op jit(solution)/shard_map/ppermute | solution.py:272
  82.7 5.0 %step_4.1.refs_7_ = f32[256,4096]{1,0:T(8,128)S(1)} custom-call(f32[32,4096]{1,0:T(8,128)S(1)} %collective-permute-done.12.refs_0_, f32[32,4096]{1,0:T(8,128)S(1)} %collective-permute-done.19.refs_1_, f32[32,4096]{1,0:T(8,128)S(1)} %collective-permute-done.20.refs_2_, ...), custom_call_target="tpu_custom_call", output_to_operand_aliasing={{}: (7, {})} | custom-call | flops 1048576 | bytes 65536 | tf_op jit(solution)/shard_map/step_4/pallas_call | solution.py:244
  87.8 3.5 %collective-permute-start.27 = (f32[32,4096]{1,0:T(8,128)S(1)}, f32[32,4096]{1,0:T(8,128)S(1)}, u32[]{:S(2)}, u32[]{:S(2)}) collective-permute-start(f32[32,4096]{1,0:T(8,128)S(1)} %collective-permute-done.18.refs_0_), channel_id=1, source_target_pairs={{0,63},{1,34},{2,33},{3,36},{4,35},{5,38},{6,37},{7,40},{8,39},{9,... | collective-permute-start | bytes 1572872 | tf_op jit(solution)/shard_map/ppermute | solution.py:272
  91.3 2.4 %collective-permute-done.22.refs_2_ = f32[32,4096]{1,0:T(8,128)S(1)} collective-permute-done((f32[32,4096]{1,0:T(8,128)S(1)}, f32[32,4096]{1,0:T(8,128)S(1)}, u32[]{:S(2)}, u32[]{:S(2)}) %collective-permute-start.22) | collective-permute-done | bytes 524320 | tf_op jit(solution)/shard_map/ppermute | solution.py:272
  94.1 5.0 %step_5.1.refs_8_ = f32[256,4096]{1,0:T(8,128)S(1)} custom-call(f32[32,4096]{1,0:T(8,128)S(1)} %collective-permute-done.11.refs_0_, f32[32,4096]{1,0:T(8,128)S(1)} %collective-permute-done.21.refs_1_, f32[32,4096]{1,0:T(8,128)S(1)} %collective-permute-done.22.refs_2_, ...), custom_call_target="tpu_custom_call", output_to_operand_aliasing={{}: (7, {})} | custom-call | flops 1048576 | bytes 65536 | tf_op jit(solution)/shard_map/step_5/pallas_call | solution.py:244
  99.3 3.6 %collective-permute-start.24 = (f32[16,4096]{1,0:T(8,128)S(1)}, f32[16,4096]{1,0:T(8,128)S(1)}, u32[]{:S(2)}, u32[]{:S(2)}) collective-permute-start(f32[16,4096]{1,0:T(8,128)S(1)} %slice.3), channel_id=1, source_target_pairs={{0,63},{1,34},{2,33},{3,36},{4,35},{5,38},{6,37},{7,40},{8,39},{9,... | collective-permute-start | bytes 786440 | tf_op jit(solution)/shard_map/ppermute | solution.py:272
  104.1 1.7 %collective-permute-done.26.refs_1_ = f32[32,4096]{1,0:T(8,128)S(1)} collective-permute-done((f32[32,4096]{1,0:T(8,128)S(1)}, f32[32,4096]{1,0:T(8,128)S(1)}, u32[]{:S(2)}, u32[]{:S(2)}) %collective-permute-start.26) | collective-permute-done | bytes 524320 | tf_op jit(solution)/shard_map/ppermute | solution.py:272
  105.8 2.8 %step_6.1.refs_7_ = f32[256,4096]{1,0:T(8,128)S(1)} custom-call(f32[32,4096]{1,0:T(8,128)S(1)} %collective-permute-done.18.refs_0_, f32[32,4096]{1,0:T(8,128)S(1)} %collective-permute-done.26.refs_1_, f32[32,4096]{1,0:T(8,128)S(1)} %collective-permute-done.27.refs_2_, ...), custom_call_target="tpu_custom_call", output_to_operand_aliasing={{}: (8, {})} | custom-call | flops 1048576 | bytes 65536 | tf_op jit(solution)/shard_map/step_6/pallas_call | solution.py:244
  108.5 2.8 %collective-permute-done.23.refs_0_ = f32[16,4096]{1,0:T(8,128)S(1)} collective-permute-done((f32[16,4096]{1,0:T(8,128)S(1)}, f32[16,4096]{1,0:T(8,128)S(1)}, u32[]{:S(2)}, u32[]{:S(2)}) %collective-permute-start.23) | collective-permute-done | bytes 262176 | tf_op jit(solution)/shard_map/ppermute | solution.py:272
  111.4 3.7 %step_7.1 = f32[256,4096]{1,0:T(8,128)} custom-call(f32[16,4096]{1,0:T(8,128)S(1)} %collective-permute-done.23.refs_0_, f32[16,4096]{1,0:T(8,128)S(1)} %collective-permute-done.24.refs_1_, f32[32,4096]{1,0:T(8,128)S(1)} %collective-permute-done.25.refs_2_, bf16[256,4096]{1,0:T(8,128)(2,1)S(1)} %get-tuple-element.74.refs_3_.refs_4_, ...), custom_call_target="tpu_custom_call" | custom-call | flops 1048576 | bytes 65536 | tf_op jit(solution)/shard_map/step_7/pallas_call | solution.py:244
  (56 shorter events, 12.9 us)
Async XLA Ops:
  0.0 22.5 %collective-permute-start.2 = (f32[8,32,4096]{2,1,0:T(8,128)}, f32[8,32,4096]{2,1,0:T(8,128)}, u32[]{:S(2)}, u32[]{:S(2)}) collective-permute-start(f32[8,32,4096]{2,1,0:T(8,128)} %param.3), channel_id=1, source_target_pairs={{0,1},{1,0},{2,3},{3,2},{4,5},{5,4},{6,7},{7,6},{8,9},{9,8},{10,11... | collective-permute-start | bytes 12582920 | tf_op jit(solution)/shard_map/ppermute | solution.py:272
  4.3 13.6 %collective-permute-start.1 = (f32[32,4096]{1,0:T(8,128)S(1)}, f32[32,4096]{1,0:T(8,128)S(1)}, u32[]{:S(2)}, u32[]{:S(2)}) collective-permute-start(f32[32,4096]{1,0:T(8,128)S(1)} %first_cuts.1), channel_id=1, source_target_pairs={{0,32},{1,33},{2,34},{3,35},{4,36},{5,37},{6,38},{7,39},{8,40},{9,... | collective-permute-start | bytes 1572872 | tf_op jit(solution)/shard_map/ppermute | solution.py:272
  7.5 28.0 %copy-start.5 = (f32[32,4096]{1,0:T(8,128)S(1)}, f32[32,4096]{1,0:T(8,128)}, u32[]{:S(2)}) copy-start(f32[32,4096]{1,0:T(8,128)} %get-tuple-element.66) | copy-start | bytes 1572868
  7.6 8.2 %collective-permute-start.3 = (f32[16,4096]{1,0:T(8,128)}, f32[16,4096]{1,0:T(8,128)S(1)}, u32[]{:S(2)}, u32[]{:S(2)}) collective-permute-start(f32[16,4096]{1,0:T(8,128)} %get-tuple-element.64), channel_id=1, source_target_pairs={{0,192},{1,193},{2,194},{3,195},{4,196},{5,197},{6,198},{7,199},{8... | collective-permute-start | bytes 786440 | tf_op jit(solution)/shard_map/ppermute | solution.py:272
  9.8 10.0 %collective-permute-start.4 = (f32[16,4096]{1,0:T(8,128)}, f32[16,4096]{1,0:T(8,128)S(1)}, u32[]{:S(2)}, u32[]{:S(2)}) collective-permute-start(f32[16,4096]{1,0:T(8,128)} %get-tuple-element.64), channel_id=1, source_target_pairs={{0,63},{1,34},{2,33},{3,36},{4,35},{5,38},{6,37},{7,40},{8,39},{9,... | collective-permute-start | bytes 786440 | tf_op jit(solution)/shard_map/ppermute | solution.py:272
  10.6 17.9 %collective-permute-start = (f32[32,4096]{1,0:T(8,128)}, f32[32,4096]{1,0:T(8,128)S(1)}, u32[]{:S(2)}, u32[]{:S(2)}) collective-permute-start(f32[32,4096]{1,0:T(8,128)} %get-tuple-element.60), channel_id=1, source_target_pairs={{0,32},{1,33},{2,34},{3,35},{4,36},{5,37},{6,38},{7,39},{8,40},{9,... | collective-permute-start | bytes 1572872 | tf_op jit(solution)/shard_map/ppermute | solution.py:272
  19.9 15.7 %collective-permute-start.8 = (f32[32,4096]{1,0:T(8,128)S(1)}, f32[32,4096]{1,0:T(8,128)S(1)}, u32[]{:S(2)}, u32[]{:S(2)}) collective-permute-start(f32[32,4096]{1,0:T(8,128)S(1)} %collective-permute-done.1.refs_0_), channel_id=1, source_target_pairs={{0,63},{1,34},{2,33},{3,36},{4,35},{5,38},{6,37},{7,40},{8,39},{9,... | collective-permute-start | bytes 1572872 | tf_op jit(solution)/shard_map/ppermute | solution.py:272
  20.7 14.9 %collective-permute-start.7 = (f32[32,4096]{1,0:T(8,128)S(1)}, f32[32,4096]{1,0:T(8,128)S(1)}, u32[]{:S(2)}, u32[]{:S(2)}) collective-permute-start(f32[32,4096]{1,0:T(8,128)S(1)} %collective-permute-done.1.refs_0_), channel_id=1, source_target_pairs={{0,64},{1,65},{2,66},{3,67},{4,68},{5,69},{6,70},{7,71},{8,72},{9,... | collective-permute-start | bytes 1572872 | tf_op jit(solution)/shard_map/ppermute | solution.py:272
  22.0 17.9 %collective-permute-start.6 = (f32[32,4096]{1,0:T(8,128)}, f32[32,4096]{1,0:T(8,128)S(1)}, u32[]{:S(2)}, u32[]{:S(2)}) collective-permute-start(f32[32,4096]{1,0:T(8,128)} %get-tuple-element.70), channel_id=1, source_target_pairs={{0,32},{1,33},{2,34},{3,35},{4,36},{5,37},{6,38},{7,39},{8,40},{9,... | collective-permute-start | bytes 1572872 | tf_op jit(solution)/shard_map/ppermute | solution.py:272
  28.6 18.2 %collective-permute-start.10 = (f32[32,4096]{1,0:T(8,128)S(1)}, f32[32,4096]{1,0:T(8,128)S(1)}, u32[]{:S(2)}, u32[]{:S(2)}) collective-permute-start(f32[32,4096]{1,0:T(8,128)S(1)} %collective-permute-done.refs_0_), channel_id=1, source_target_pairs={{0,63},{1,34},{2,33},{3,36},{4,35},{5,38},{6,37},{7,40},{8,39},{9,... | collective-permute-start | bytes 1572872 | tf_op jit(solution)/shard_map/ppermute | solution.py:272
  31.1 18.0 %collective-permute-start.9 = (f32[32,4096]{1,0:T(8,128)S(1)}, f32[32,4096]{1,0:T(8,128)S(1)}, u32[]{:S(2)}, u32[]{:S(2)}) collective-permute-start(f32[32,4096]{1,0:T(8,128)S(1)} %collective-permute-done.refs_0_), channel_id=1, source_target_pairs={{0,64},{1,65},{2,66},{3,67},{4,68},{5,69},{6,70},{7,71},{8,72},{9,... | collective-permute-start | bytes 1572872 | tf_op jit(solution)/shard_map/ppermute | solution.py:272
  35.6 17.6 %collective-permute-start.5 = (f32[32,4096]{1,0:T(8,128)S(1)}, f32[32,4096]{1,0:T(8,128)S(1)}, u32[]{:S(2)}, u32[]{:S(2)}) collective-permute-start(f32[32,4096]{1,0:T(8,128)S(1)} %copy-done.5), channel_id=1, source_target_pairs={{0,32},{1,33},{2,34},{3,35},{4,36},{5,37},{6,38},{7,39},{8,40},{9,... | collective-permute-start | bytes 1572872 | tf_op jit(solution)/shard_map/ppermute | solution.py:272
  39.8 18.2 %collective-permute-start.14 = (f32[32,4096]{1,0:T(8,128)S(1)}, f32[32,4096]{1,0:T(8,128)S(1)}, u32[]{:S(2)}, u32[]{:S(2)}) collective-permute-start(f32[32,4096]{1,0:T(8,128)S(1)} %collective-permute-done.6.refs_0_), channel_id=1, source_target_pairs={{0,63},{1,34},{2,33},{3,36},{4,35},{5,38},{6,37},{7,40},{8,39},{9,... | collective-permute-start | bytes 1572872 | tf_op jit(solution)/shard_map/ppermute | solution.py:272
  42.2 18.1 %collective-permute-start.13 = (f32[32,4096]{1,0:T(8,128)S(1)}, f32[32,4096]{1,0:T(8,128)S(1)}, u32[]{:S(2)}, u32[]{:S(2)}) collective-permute-start(f32[32,4096]{1,0:T(8,128)S(1)} %collective-permute-done.6.refs_0_), channel_id=1, source_target_pairs={{0,64},{1,65},{2,66},{3,67},{4,68},{5,69},{6,70},{7,71},{8,72},{9,... | collective-permute-start | bytes 1572872 | tf_op jit(solution)/shard_map/ppermute | solution.py:272
  43.5 14.5 %copy-start.3 = (f32[32,4096]{1,0:T(8,128)S(1)}, f32[32,4096]{1,0:T(8,128)}, u32[]{:S(2)}) copy-start(f32[32,4096]{1,0:T(8,128)} %get-tuple-element.81) | copy-start | bytes 1572868
  46.8 17.6 %collective-permute-start.12 = (f32[32,4096]{1,0:T(8,128)S(1)}, f32[32,4096]{1,0:T(8,128)S(1)}, u32[]{:S(2)}, u32[]{:S(2)}) collective-permute-start(f32[32,4096]{1,0:T(8,128)S(1)} %copy-done.4), channel_id=1, source_target_pairs={{0,32},{1,33},{2,34},{3,35},{4,36},{5,37},{6,38},{7,39},{8,40},{9,... | collective-permute-start | bytes 1572872 | tf_op jit(solution)/shard_map/ppermute | solution.py:272
  53.2 18.0 %collective-permute-start.16 = (f32[32,4096]{1,0:T(8,128)S(1)}, f32[32,4096]{1,0:T(8,128)S(1)}, u32[]{:S(2)}, u32[]{:S(2)}) collective-permute-start(f32[32,4096]{1,0:T(8,128)S(1)} %collective-permute-done.5.refs_0_), channel_id=1, source_target_pairs={{0,63},{1,34},{2,33},{3,36},{4,35},{5,38},{6,37},{7,40},{8,39},{9,... | collective-permute-start | bytes 1572872 | tf_op jit(solution)/shard_map/ppermute | solution.py:272
  56.7 14.8 %collective-permute-start.15 = (f32[32,4096]{1,0:T(8,128)S(1)}, f32[32,4096]{1,0:T(8,128)S(1)}, u32[]{:S(2)}, u32[]{:S(2)}) collective-permute-start(f32[32,4096]{1,0:T(8,128)S(1)} %collective-permute-done.5.refs_0_), channel_id=1, source_target_pairs={{0,64},{1,65},{2,66},{3,67},{4,68},{5,69},{6,70},{7,71},{8,72},{9,... | collective-permute-start | bytes 1572872 | tf_op jit(solution)/shard_map/ppermute | solution.py:272
  56.7 14.6 %copy-start.2 = (f32[32,4096]{1,0:T(8,128)S(1)}, f32[32,4096]{1,0:T(8,128)}, u32[]{:S(2)}) copy-start(f32[32,4096]{1,0:T(8,128)} %get-tuple-element.94) | copy-start | bytes 1572868
  58.1 17.6 %collective-permute-start.11 = (f32[32,4096]{1,0:T(8,128)S(1)}, f32[32,4096]{1,0:T(8,128)S(1)}, u32[]{:S(2)}, u32[]{:S(2)}) collective-permute-start(f32[32,4096]{1,0:T(8,128)S(1)} %copy-done.3), channel_id=1, source_target_pairs={{0,32},{1,33},{2,34},{3,35},{4,36},{5,37},{6,38},{7,39},{8,40},{9,... | collective-permute-start | bytes 1572872 | tf_op jit(solution)/shard_map/ppermute | solution.py:272
  64.5 18.0 %collective-permute-start.20 = (f32[32,4096]{1,0:T(8,128)S(1)}, f32[32,4096]{1,0:T(8,128)S(1)}, u32[]{:S(2)}, u32[]{:S(2)}) collective-permute-start(f32[32,4096]{1,0:T(8,128)S(1)} %collective-permute-done.12.refs_0_), channel_id=1, source_target_pairs={{0,63},{1,34},{2,33},{3,36},{4,35},{5,38},{6,37},{7,40},{8,39},{9,... | collective-permute-start | bytes 1572872 | tf_op jit(solution)/shard_map/ppermute | solution.py:272
  67.9 14.8 %collective-permute-start.19 = (f32[32,4096]{1,0:T(8,128)S(1)}, f32[32,4096]{1,0:T(8,128)S(1)}, u32[]{:S(2)}, u32[]{:S(2)}) collective-permute-start(f32[32,4096]{1,0:T(8,128)S(1)} %collective-permute-done.12.refs_0_), channel_id=1, source_target_pairs={{0,64},{1,65},{2,66},{3,67},{4,68},{5,69},{6,70},{7,71},{8,72},{9,... | collective-permute-start | bytes 1572872 | tf_op jit(solution)/shard_map/ppermute | solution.py:272
  67.9 14.6 %copy-start.1 = (f32[32,4096]{1,0:T(8,128)S(1)}, f32[32,4096]{1,0:T(8,128)}, u32[]{:S(2)}) copy-start(f32[32,4096]{1,0:T(8,128)} %get-tuple-element.92) | copy-start | bytes 1572868
  71.2 16.5 %collective-permute-start.18 = (f32[32,4096]{1,0:T(8,128)S(1)}, f32[32,4096]{1,0:T(8,128)S(1)}, u32[]{:S(2)}, u32[]{:S(2)}) collective-permute-start(f32[32,4096]{1,0:T(8,128)S(1)} %copy-done.2), channel_id=1, source_target_pairs={{0,32},{1,33},{2,34},{3,35},{4,36},{5,37},{6,38},{7,39},{8,40},{9,... | collective-permute-start | bytes 1572872 | tf_op jit(solution)/shard_map/ppermute | solution.py:272
  75.7 18.0 %collective-permute-start.22 = (f32[32,4096]{1,0:T(8,128)S(1)}, f32[32,4096]{1,0:T(8,128)S(1)}, u32[]{:S(2)}, u32[]{:S(2)}) collective-permute-start(f32[32,4096]{1,0:T(8,128)S(1)} %collective-permute-done.11.refs_0_), channel_id=1, source_target_pairs={{0,63},{1,34},{2,33},{3,36},{4,35},{5,38},{6,37},{7,40},{8,39},{9,... | collective-permute-start | bytes 1572872 | tf_op jit(solution)/shard_map/ppermute | solution.py:272
  79.2 14.5 %collective-permute-start.21 = (f32[32,4096]{1,0:T(8,128)S(1)}, f32[32,4096]{1,0:T(8,128)S(1)}, u32[]{:S(2)}, u32[]{:S(2)}) collective-permute-start(f32[32,4096]{1,0:T(8,128)S(1)} %collective-permute-done.11.refs_0_), channel_id=1, source_target_pairs={{0,64},{1,65},{2,66},{3,67},{4,68},{5,69},{6,70},{7,71},{8,72},{9,... | collective-permute-start | bytes 1572872 | tf_op jit(solution)/shard_map/ppermute | solution.py:272
  82.5 16.7 %collective-permute-start.17 = (f32[32,4096]{1,0:T(8,128)S(1)}, f32[32,4096]{1,0:T(8,128)S(1)}, u32[]{:S(2)}, u32[]{:S(2)}) collective-permute-start(f32[32,4096]{1,0:T(8,128)S(1)} %copy-done.1), channel_id=1, source_target_pairs={{0,32},{1,33},{2,34},{3,35},{4,36},{5,37},{6,38},{7,39},{8,40},{9,... | collective-permute-start | bytes 1572872 | tf_op jit(solution)/shard_map/ppermute | solution.py:272
  87.8 16.3 %collective-permute-start.27 = (f32[32,4096]{1,0:T(8,128)S(1)}, f32[32,4096]{1,0:T(8,128)S(1)}, u32[]{:S(2)}, u32[]{:S(2)}) collective-permute-start(f32[32,4096]{1,0:T(8,128)S(1)} %collective-permute-done.18.refs_0_), channel_id=1, source_target_pairs={{0,63},{1,34},{2,33},{3,36},{4,35},{5,38},{6,37},{7,40},{8,39},{9,... | collective-permute-start | bytes 1572872 | tf_op jit(solution)/shard_map/ppermute | solution.py:272
  91.3 14.5 %collective-permute-start.26 = (f32[32,4096]{1,0:T(8,128)S(1)}, f32[32,4096]{1,0:T(8,128)S(1)}, u32[]{:S(2)}, u32[]{:S(2)}) collective-permute-start(f32[32,4096]{1,0:T(8,128)S(1)} %collective-permute-done.18.refs_0_), channel_id=1, source_target_pairs={{0,64},{1,65},{2,66},{3,67},{4,68},{5,69},{6,70},{7,71},{8,72},{9,... | collective-permute-start | bytes 1572872 | tf_op jit(solution)/shard_map/ppermute | solution.py:272
  93.7 17.7 %collective-permute-start.25 = (f32[32,4096]{1,0:T(8,128)S(1)}, f32[32,4096]{1,0:T(8,128)S(1)}, u32[]{:S(2)}, u32[]{:S(2)}) collective-permute-start(f32[32,4096]{1,0:T(8,128)S(1)} %constant_dynamic-update-slice_fusion), channel_id=1, source_target_pairs={{0,32},{1,33},{2,34},{3,35},{4,36},{5,37},{6,38},{7,39},{8,40},{9,... | collective-permute-start | bytes 1572872 | tf_op jit(solution)/shard_map/ppermute | solution.py:272
  99.2 12.2 %collective-permute-start.23 = (f32[16,4096]{1,0:T(8,128)S(1)}, f32[16,4096]{1,0:T(8,128)S(1)}, u32[]{:S(2)}, u32[]{:S(2)}) collective-permute-start(f32[16,4096]{1,0:T(8,128)S(1)} %slice.3), channel_id=1, source_target_pairs={{0,64},{1,65},{2,66},{3,67},{4,68},{5,69},{6,70},{7,71},{8,72},{9,... | collective-permute-start | bytes 786440 | tf_op jit(solution)/shard_map/ppermute | solution.py:272
  99.3 12.1 %collective-permute-start.24 = (f32[16,4096]{1,0:T(8,128)S(1)}, f32[16,4096]{1,0:T(8,128)S(1)}, u32[]{:S(2)}, u32[]{:S(2)}) collective-permute-start(f32[16,4096]{1,0:T(8,128)S(1)} %slice.3), channel_id=1, source_target_pairs={{0,63},{1,34},{2,33},{3,36},{4,35},{5,38},{6,37},{7,40},{8,39},{9,... | collective-permute-start | bytes 786440 | tf_op jit(solution)/shard_map/ppermute | solution.py:272
  (2 other events, 20.2 us)
